TPU v7x, 32 devices: a whole 2x2x4 slice. The times are simulated.
32 devices in a mesh: row: 8 (over z, core), col: 4 (over y, x).
Axes of the slice: x: 2, y: 2, z: 4, core: 2. Of those that a mesh axis runs over, the one named last changes fastest.
Arguments:
- pair_input: float32 [96, 96, 128], P('row', 'col'), may hold values from -6 to 6
- block_valid: int32 [12], replicated, may hold values from 4 to 8, as said below
- proj_weight: bfloat16 [128, 640], replicated, may hold values from -0.5 to 0.5
- out_weight: bfloat16 [128, 128], replicated, may hold values from -0.5 to 0.5
- cotangent: float32 [96, 96, 128], P('row', 'col'), may hold values from -6 to 6
Outputs:
- pair_out: float32 [96, 96, 128], P('row', 'col')
- pair_grad: float32 [96, 96, 128], P('row', 'col')
- proj_grad: float32 [128, 640], replicated
- out_grad: float32 [128, 128], replicated
Inputs may be any that keep to these rules, and one draw needn't show every extreme that they name: `block_valid`: entry q counts the valid tokens at the start of mask block q of 8 tokens.
All inputs are finite; a program needn't handle non-finite values.
Results may differ from a plain program's by a relative error of at most 0.0082.
Values may be sent and summed in bfloat16 or wider, within the bound.
No kernel may reach another device: no remote copies, remote signals or barrier semaphores. Data moves between devices by JAX's collectives and lax.ppermute only.
A program may use at most 128 MiB of HBM per device.

v0:
```python
import jax
import jax.numpy as jnp
from jax import lax
from jax.sharding import PartitionSpec as P

SEG = 8


def layer_norm(values):
    middle = jnp.mean(values, axis=-1, keepdims=True)
    center = values - middle
    spread = jnp.mean(center * center, axis=-1, keepdims=True)
    scaled = lax.rsqrt(spread + 1e-05)
    return (center * scaled, scaled)


def norm_back(grad_norm, normed, scaled):
    first_mean = jnp.mean(grad_norm, axis=-1, keepdims=True)
    second = jnp.mean(grad_norm * normed, axis=-1, keepdims=True)
    return scaled * (grad_norm - first_mean - normed * second)


def gate_back(grad_in, pair_mask, gate_part, value_part):
    sigma_val = jax.nn.sigmoid(gate_part)
    masked = grad_in * pair_mask
    return (masked * value_part * sigma_val * (1.0 - sigma_val), masked * sigma_val)


def body(pair_input, block_valid, proj_weight, out_weight, cotangent):
    row_len = pair_input.shape[0]
    col_len = pair_input.shape[1]
    hidden = out_weight.shape[0]
    total_len = col_len * lax.axis_size("col")
    positions = jnp.arange(total_len)
    token_mask = (positions % SEG < jnp.repeat(block_valid, SEG)).astype(jnp.float32)
    row_mask = lax.dynamic_slice_in_dim(token_mask, lax.axis_index("row") * row_len, row_len)
    col_mask = lax.dynamic_slice_in_dim(token_mask, lax.axis_index("col") * col_len, col_len)
    pair_mask = row_mask[:, None, None] * col_mask[None, :, None]
    normed, scaled = layer_norm(pair_input)
    normed_low = normed.astype(jnp.bfloat16)
    projected = jnp.einsum(
        "ijc,cd->ijd", normed_low, proj_weight, preferred_element_type=jnp.float32
    )
    left_gate = projected[..., :hidden]
    left_value = projected[..., hidden : 2 * hidden]
    right_gate = projected[..., 2 * hidden : 3 * hidden]
    right_value = projected[..., 3 * hidden : 4 * hidden]
    out_logit = projected[..., 4 * hidden :]
    left_proj = (pair_mask * jax.nn.sigmoid(left_gate) * left_value).astype(jnp.bfloat16)
    right_proj = (pair_mask * jax.nn.sigmoid(right_gate) * right_value).astype(jnp.bfloat16)
    left_full = lax.all_gather(left_proj, "col", axis=1, tiled=True)
    right_full = lax.all_gather(right_proj, "row", axis=0, tiled=True)
    right_mine = lax.all_to_all(right_full, "col", split_axis=0, concat_axis=1, tiled=True)
    mixed_sum = jnp.einsum(
        "ikc,jkc->ijc", left_full, right_mine, preferred_element_type=jnp.float32
    )
    mixed_norm, mixed_scale = layer_norm(mixed_sum)
    mixed_low = mixed_norm.astype(jnp.bfloat16)
    update = jnp.einsum("ijh,hc->ijc", mixed_low, out_weight, preferred_element_type=jnp.float32)
    out_gate = jax.nn.sigmoid(out_logit)
    pair_out = out_gate * update
    grad_logit = cotangent * update * out_gate * (1.0 - out_gate)
    grad_update = (cotangent * out_gate).astype(jnp.bfloat16)
    out_local = jnp.einsum(
        "ijh,ijc->hc", mixed_low, grad_update, preferred_element_type=jnp.float32
    )
    grad_mixed_norm = jnp.einsum(
        "ijc,hc->ijh", grad_update, out_weight, preferred_element_type=jnp.float32
    )
    grad_mixed = norm_back(grad_mixed_norm, mixed_norm, mixed_scale).astype(jnp.bfloat16)
    grad_full = lax.all_gather(grad_mixed, "col", axis=1, tiled=True)
    grad_left = jnp.einsum(
        "ijc,jkc->ikc", grad_full, right_full, preferred_element_type=jnp.float32
    )
    grad_columns = lax.all_to_all(grad_full, "row", split_axis=1, concat_axis=0, tiled=True)
    left_all = lax.all_gather(left_proj, "row", axis=0, tiled=True)
    grad_right = jnp.einsum(
        "ijc,ikc->jkc", grad_columns, left_all, preferred_element_type=jnp.float32
    )
    left_dg, left_dv = gate_back(grad_left, pair_mask, left_gate, left_value)
    right_dg, right_dv = gate_back(grad_right, pair_mask, right_gate, right_value)
    grad_proj = jnp.concatenate([left_dg, left_dv, right_dg, right_dv, grad_logit], axis=-1).astype(
        jnp.bfloat16
    )
    proj_local = jnp.einsum(
        "ijc,ijd->cd", normed_low, grad_proj, preferred_element_type=jnp.float32
    )
    grad_normed = jnp.einsum(
        "ijd,cd->ijc", grad_proj, proj_weight, preferred_element_type=jnp.float32
    )
    pair_grad = norm_back(grad_normed, normed, scaled)
    proj_grad, out_grad = lax.psum((proj_local, out_local), ("row", "col"))
    return (pair_out, pair_grad, proj_grad, out_grad)


def solution(mesh):
    return jax.shard_map(
        body,
        mesh=mesh,
        in_specs=(P("row", "col", None), P(), P(), P(), P("row", "col", None)),
        out_specs=(P("row", "col", None), P("row", "col", None), P(), P()),
        check_vma=False,
    )
```

profile of v0, /device:TPU:0, one launch (start us, length us, event | category | flops | bytes accessed | tf_op | source)
XLA Modules:
  0.0 278.3 jit_solution(5058634541539990777)
XLA Ops:
  13.6 17.8 %all_gather.12 = bf16[96,24,128]{2,1,0:T(8,128)(2,1)} all-gather(bf16[12,24,128]{2,1,0:T(8,128)(2,1)S(1)} %get-tuple-element.11), channel_id=1, replica_groups=mesh['row'=8,'col'=4] {'row'}, dimensions={0}, use_global_device_ids=true | all-gather | bytes 663552 | tf_op jit(solution)/shard_map/all_gather | solution.py:52
  31.3 4.1 %all-to-all-start = ((bf16[96,24,128]{2,1,0:T(8,128)(2,1)}), bf16[96,24,128]{2,1,0:T(8,128)(2,1)}, u32[]{:S(2)}, u32[]{:S(2)}) async-start(bf16[96,24,128]{2,1,0:T(8,128)(2,1)} %all_gather.12), calls=%async_computation | async-start | bytes 1179648 | tf_op jit(solution)/shard_map/all_to_all | solution.py:53
  35.5 6.0 %copy.71 = bf16[96,24,128]{1,0,2:T(8,128)(2,1)} copy(bf16[96,24,128]{2,1,0:T(8,128)(2,1)} %all_gather.12) | data formatting | bytes 1179648 | tf_op jit(solution)/shard_map/all_gather | solution.py:52
  41.5 10.0 %all_gather.13 = bf16[12,96,128]{2,1,0:T(8,128)(2,1)S(1)} all-gather(bf16[12,24,128]{2,1,0:T(8,128)(2,1)S(1)} %get-tuple-element.10), channel_id=1, replica_groups=mesh['row'=8,'col'=4] {'col'}, dimensions={1}, use_global_device_ids=true | all-gather | bytes 368640 | tf_op jit(solution)/shard_map/all_gather | solution.py:51
  52.7 15.9 %all_gather.15 = bf16[96,24,128]{2,1,0:T(8,128)(2,1)} all-gather(bf16[12,24,128]{2,1,0:T(8,128)(2,1)S(1)} %get-tuple-element.10), channel_id=1, replica_groups=mesh['row'=8,'col'=4] {'row'}, dimensions={0}, use_global_device_ids=true | all-gather | bytes 663552 | tf_op jit(solution)/shard_map/all_gather | solution.py:76
  68.5 5.2 %copy.77 = bf16[96,24,128]{1,0,2:T(8,128)(2,1)S(1)} copy(bf16[96,24,128]{2,1,0:T(8,128)(2,1)} %all_gather.15) | data formatting | bytes 1179648 | tf_op jit(solution)/shard_map/all_gather | solution.py:76
  73.8 2.0 copy.67
  75.8 2.3 copy.68
  78.1 2.8 %fusion.32 = f32[128,24,12]{1,2,0:T(8,128)} fusion(bf16[24,96,128]{1,0,2:T(8,128)(2,1)} %copy.68, bf16[12,96,128]{1,0,2:T(8,128)(2,1)} %copy.69), kind=kOutput, calls=%fused_computation.63 | convolution fusion | flops 7077888 | bytes 1032192 | tf_op jit(solution)/shard_map/ikc,jkc->ijc/dot_general | solution.py:54
  84.1 10.1 %all_gather.14 = bf16[12,96,128]{2,1,0:T(8,128)(2,1)} all-gather(bf16[12,24,128]{2,1,0:T(8,128)(2,1)S(1)} %multiply_convert_fusion.5), channel_id=1, replica_groups=mesh['row'=8,'col'=4] {'col'}, dimensions={1}, use_global_device_ids=true | all-gather | bytes 368640 | tf_op jit(solution)/shard_map/all_gather | solution.py:71
  94.2 2.2 copy.72
  96.4 1.8 copy.74
  98.2 3.9 %fusion.33 = f32[128,24,12]{1,2,0:T(8,128)} fusion(bf16[96,24,128]{1,0,2:T(8,128)(2,1)} %copy.71, bf16[12,96,128]{1,0,2:T(8,128)(2,1)} %copy.72), kind=kOutput, calls=%fused_computation.64 | convolution fusion | flops 7077888 | bytes 1032192 | tf_op jit(solution)/shard_map/ijc,jkc->ikc/dot_general | solution.py:72
  102.2 2.2 copy.73
  104.3 1.8 fusion.16
  106.1 4.6 %all-to-all-start.1 = ((bf16[12,96,128]{2,0,1:T(8,128)(2,1)}), bf16[12,96,128]{2,0,1:T(8,128)(2,1)}, u32[]{:S(2)}, u32[]{:S(2)}) async-start(bf16[12,96,128]{2,0,1:T(8,128)(2,1)} %copy.74), calls=%async_computation.1 | async-start | bytes 786432 | tf_op jit(solution)/shard_map/all_to_all | solution.py:75
  114.2 1.9 fusion.29
  116.1 7.2 %all-to-all-done.1 = bf16[12,96,128]{2,0,1:T(8,128)(2,1)} async-done(((bf16[12,96,128]{2,0,1:T(8,128)(2,1)}), bf16[12,96,128]{2,0,1:T(8,128)(2,1)}, u32[]{:S(2)}, u32[]{:S(2)}) %all-to-all-start.1) | async-done | bytes 294944 | tf_op jit(solution)/shard_map/all_to_all | solution.py:75
  123.4 1.8 copy.76
  125.1 1.8 all_to_all.33
  126.9 2.2 copy.78
  129.1 3.0 %fusion.34 = f32[128,24,12]{1,2,0:T(8,128)} fusion(bf16[96,24,128]{1,0,2:T(8,128)(2,1)S(1)} %copy.77, bf16[96,12,128]{0,1,2:T(8,128)(2,1)} %copy.78), kind=kOutput, calls=%fused_computation.65 | convolution fusion | flops 7077888 | bytes 1032192 | tf_op jit(solution)/shard_map/ijc,ikc->jkc/dot_general | solution.py:77
  140.1 2.1 convolution_bitcast_fusion
  143.2 125.0 %all-reduce.3.cloned.1.call-done = (f32[128,640]{1,0:T(8,128)}, f32[128,128]{1,0:T(8,128)}) async-done(((f32[128,640]{1,0:T(8,128)}, f32[128,128]{1,0:T(8,128)}), (f32[128,640]{1,0:T(8,128)}, f32[128,128]{1,0:T(8,128)})) %all-reduce.3.cloned.1.call-update) | async-done | bytes 393232 | tf_op jit(solution)/shard_map/psum | solution.py:92
  (46 shorter events, 26.2 us)
Async XLA Ops:
  7.2 3.2 %copy-start = (bf16[128,640]{1,0:T(8,128)(2,1)S(1)}, bf16[128,640]{1,0:T(8,128)(2,1)}, u32[]{:S(2)}) copy-start(bf16[128,640]{1,0:T(8,128)(2,1)} %param.7) | copy-start | bytes 491524
  11.6 0.9 copy-start.1
  31.3 42.5 %all-to-all-start = ((bf16[96,24,128]{2,1,0:T(8,128)(2,1)}), bf16[96,24,128]{2,1,0:T(8,128)(2,1)}, u32[]{:S(2)}, u32[]{:S(2)}) async-start(bf16[96,24,128]{2,1,0:T(8,128)(2,1)} %all_gather.12), calls=%async_computation | async-start | bytes 1179648 | tf_op jit(solution)/shard_map/all_to_all | solution.py:53
  82.5 1.5 copy-start.3
  82.8 1.3 copy-start.4
  106.1 17.2 %all-to-all-start.1 = ((bf16[12,96,128]{2,0,1:T(8,128)(2,1)}), bf16[12,96,128]{2,0,1:T(8,128)(2,1)}, u32[]{:S(2)}, u32[]{:S(2)}) async-start(bf16[12,96,128]{2,0,1:T(8,128)(2,1)} %copy.74), calls=%async_computation.1 | async-start | bytes 786432 | tf_op jit(solution)/shard_map/all_to_all | solution.py:75
  110.7 157.5 %all-reduce.3.cloned.1.call-start = ((), (), s32[]{:S(2)}) async-start(), calls=%async_computation.2 | async-start | bytes 786432 | tf_op jit(solution)/shard_map/psum | solution.py:92
  129.1 9.7 %copy-start.2 = (f32[12,24,128]{2,1,0:T(8,128)S(1)}, f32[12,24,128]{2,1,0:T(8,128)}, u32[]{:S(2)}) copy-start(f32[12,24,128]{2,1,0:T(8,128)} %param.5) | copy-start | bytes 442372
Sparse Core Ops, SparseCore 0:
  142.4 125.7 all-reduce.2
where the time goes:
time: 280 us; the launch traced here: 278 us
  waiting for transfers between devices  132 us (47%)
  blocking collectives  53.7 us (19%)
  local copies, waits for them, and re-layouts  36.6 us (13%)
  matrix products  19.2 us (7%)
  between operations  14.2 us (5%)
  other arithmetic  13.4 us (5%)
  starting transfers between devices  8.75 us (3%)
    psum x1, waiting for transfers between devices, body(): proj_grad, out_grad = lax.psum((proj_local, out_local), ('row', 'col'))  125 us
    all_gather x1, blocking collectives, body(): right_full = lax.all_gather(right_proj, 'row', axis=0, tiled=True)  17.8 us
    all_gather x1, blocking collectives, body(): left_all = lax.all_gather(left_proj, 'row', axis=0, tiled=True)  15.9 us
    all_gather x1, blocking collectives, body(): grad_full = lax.all_gather(grad_mixed, 'col', axis=1, tiled=True)  10.1 us
    all_gather x1, blocking collectives, body(): left_full = lax.all_gather(left_proj, 'col', axis=1, tiled=True)  9.96 us
    all_to_all x1, waiting for transfers between devices, body(): lax.all_to_all(grad_full, 'row', split_axis=1, concat_axis=0, tiled=True)  7.25 us
    unnamed x4, other arithmetic  6.96 us
    all_gather x1, local copies, waits for them, and re-layouts, body(): right_full = lax.all_gather(right_proj, 'row', axis=0, tiled=True)  6.01 us
  transfers between devices with their start and end apart: 3, of which 2 were waited for; matrix products, arithmetic and copies ran while one was open for 7% of the time, Pallas kernels for 0%

commit v1 on v0

v1 whole, which is shorter than its diff:
```python
import functools

import jax
import jax.numpy as jnp
from jax import lax
from jax.experimental import pallas as pl
from jax.experimental.pallas import tpu as pltpu
from jax.sharding import PartitionSpec as P

SEG = 8
F32 = jnp.float32
BF16 = jnp.bfloat16


def sigmoid(values):
    return 0.5 * jnp.tanh(0.5 * values) + 0.5


def layer_norm(values):
    center = values - jnp.mean(values, axis=-1, keepdims=True)
    scaled = lax.rsqrt(jnp.mean(center * center, axis=-1, keepdims=True) + 1e-05)
    return center * scaled, scaled


def norm_back(grad_norm, normed, scaled):
    first_mean = jnp.mean(grad_norm, axis=-1, keepdims=True)
    second = jnp.mean(grad_norm * normed, axis=-1, keepdims=True)
    return scaled * (grad_norm - first_mean - normed * second)


def dot(a, b):
    return jnp.dot(a, b, preferred_element_type=F32)


def dot_nt(a, b):
    return lax.dot_general(a, b, (((1,), (1,)), ((), ())), preferred_element_type=F32)


def dot_tn(a, b):
    return lax.dot_general(a, b, (((0,), (0,)), ((), ())), preferred_element_type=F32)


def flip(z, count):
    out, bit = z & 0, 1
    top = count >> 1
    while bit < count:
        if isinstance(z, int):
            out |= top if z & bit else 0
        else:
            out = out + jnp.where((z & bit) != 0, top, 0)
        bit, top = bit << 1, top >> 1
    return out


def place(cols):
    row, col = lax.axis_index("row"), lax.axis_index("col")
    z, core = row >> 1, row & 1
    step = flip(z, cols)
    return row, core, col, step, col ^ step


def norm_kernel(pair_ref, low_ref):
    low_ref[...] = layer_norm(pair_ref[...])[0].astype(BF16)


def project_block(projected, valid_ref, row, block, sizes, index, v_ref, a_ref, b_ref):
    row_len, col_len, width = sizes
    spot = lax.broadcasted_iota(jnp.int32, (SEG, width), 0)
    groups = col_len // SEG
    keep_col = jnp.concatenate(
        [jnp.where(spot < valid_ref[block * groups + g], 1.0, 0.0) for g in range(groups)], axis=0
    )
    for i in range(row_len):
        token = row * row_len + i
        valid = (token & (SEG - 1)) < valid_ref[token >> 3]
        keep = keep_col * jnp.where(valid, 1.0, 0.0)
        part = projected[i * col_len : (i + 1) * col_len]
        gate = sigmoid(part[:, :width])
        kept = keep * gate
        gated = kept * part[:, width:]
        v_ref[index + (i,)] = gated.astype(BF16).astype(F32)
        a_ref[index + (i,)] = gated * (1.0 - gate)
        b_ref[index + (i,)] = kept


def project_kernel(side, cols, sizes, valid_ref, x_ref, w_ref, v_ref, a_ref, b_ref):
    row_len, col_len, width = sizes
    area = row_len * col_len
    row, core, col, step, pair = place(cols)
    if side == 1:
        row = 2 * pair + core

    def one(d, carry):
        rows = pl.ds(pl.multiple_of(d * area, area), area)
        projected = dot(x_ref[rows, :], w_ref[:, side * 2 * width : (side + 1) * 2 * width])
        project_block(projected, valid_ref, row, col ^ d, sizes, (d,), v_ref, a_ref, b_ref)
        return carry

    lax.fori_loop(0, cols, one, 0)


def main_kernel(
    cols,
    sizes,
    valid_ref,
    lv_ref,
    la_ref,
    lb_ref,
    ov_ref,
    oa_ref,
    ob_ref,
    x_ref,
    own_x_ref,
    other_x_ref,
    cot_ref,
    w_ref,
    wout_ref,
    out_ref,
    send_ref,
    keep_y_ref,
    gx_ref,
    keep_w_ref,
    rv_ref,
    ra_ref,
    rb_ref,
    mixed_ref,
    grad_ref,
    wide_ref,
    dl_ref,
    dr_ref,
    wg_ref,
):
    row_len, col_len, width = sizes
    area = row_len * col_len
    row, core, col, step, pair = place(cols)
    groups = col_len // SEG
    other = 1 - core
    zero = jnp.zeros((SEG, width), F32)

    def block_rows(d):
        return pl.ds(pl.multiple_of(d * area, area), area)

    def tile(g):
        return slice(g * SEG, (g + 1) * SEG)

    def right_side(d, carry):
        projected = dot(other_x_ref[block_rows(d), :], w_ref[:, 2 * width : 4 * width])
        project_block(
            projected, valid_ref, 2 * pair + other, col ^ d, sizes, (other, d), rv_ref, ra_ref, rb_ref
        )
        rv_ref[core, d] = ov_ref[d]
        ra_ref[core, d] = oa_ref[d]
        rb_ref[core, d] = ob_ref[d]
        return carry

    lax.fori_loop(0, cols, right_side, 0)

    def mix_rows(pair_at, carry):
        for jt in range(col_len // SEG):

            def over(d, acc):
                for g in range(groups):
                    left = [lv_ref[d, 2 * pair_at + a, tile(g), :] for a in range(2)]
                    right = [
                        rv_ref[j // row_len, d, j % row_len, tile(g), :]
                        for j in range(jt * SEG, (jt + 1) * SEG)
                    ]
                    acc = tuple(acc[n] + left[n // SEG] * right[n % SEG] for n in range(2 * SEG))
                return acc

            acc = lax.fori_loop(0, cols, over, (zero,) * (2 * SEG))
            for a in range(2):
                mixed_ref[2 * pair_at + a, tile(jt), :] = jnp.concatenate(
                    [jnp.sum(acc[a * SEG + n], axis=0, keepdims=True) for n in range(SEG)], axis=0
                )
        return carry

    lax.fori_loop(0, row_len // 2, mix_rows, 0)

    mixed_norm, mixed_scale = layer_norm(mixed_ref[...].reshape(area, width))
    mixed_low = mixed_norm.astype(BF16)
    update = dot(mixed_low, wout_ref[...])
    home = x_ref[block_rows(step), :]
    out_gate = sigmoid(dot(home, w_ref[:, 4 * width :]))
    out_ref[...] = out_gate * update
    cot = cot_ref[...]
    gated_cot = cot * out_gate
    grad_logit = (gated_cot * update * (1.0 - out_gate)).astype(BF16)
    grad_update = gated_cot.astype(BF16)
    wg_ref[1, 2 * width :, :] = dot_tn(mixed_low, grad_update)
    wg_ref[1, width : 2 * width, :] = dot_tn(home, grad_logit)
    grad_mixed = norm_back(dot_nt(grad_update, wout_ref[...]), mixed_norm, mixed_scale)
    grad_ref[...] = grad_mixed.astype(BF16).astype(F32).reshape(row_len, col_len, width)

    def widen(i, carry):
        for j in range(col_len):
            wide_ref[i, j] = jnp.broadcast_to(grad_ref[i, j : j + 1, :], (SEG, width))
        return carry

    lax.fori_loop(0, row_len, widen, 0)

    def gradient(load, count, first, a_ref, b_ref, index, d_ref, d_index):
        acc = [[zero] * groups for _ in range(4)]
        for n in range(count):
            value, weights = load(n)
            for a in range(4):
                for g in range(groups):
                    acc[a][g] = acc[a][g] + value[g] * weights[a]
        full = [jnp.concatenate(acc[a], axis=0) for a in range(4)]
        gates = [full[a] * a_ref[index + (first + a,)] for a in range(4)]
        values = [full[a] * b_ref[index + (first + a,)] for a in range(4)]
        d_ref[d_index + (slice(0, width),)] = jnp.concatenate(gates, axis=0).astype(BF16)
        d_ref[d_index + (slice(width, 2 * width),)] = jnp.concatenate(values, axis=0).astype(BF16)

    quarter = 4 * col_len

    def spot(d, b):
        return pl.ds(pl.multiple_of(d * area + b * quarter, quarter), quarter)

    for half in range(2):

        def right_back(n, carry):
            b, d = n // cols, n % cols

            def load(i):
                return (
                    [lv_ref[d, i, tile(g), :] for g in range(groups)],
                    [wide_ref[i, half * row_len + 4 * b + a] for a in range(4)],
                )

            gradient(load, row_len, 4 * b, ra_ref, rb_ref, (half, d), dr_ref, (half, spot(d, b)))
            return carry

        lax.fori_loop(0, (row_len // 4) * cols, right_back, 0)

    def left_back(n, carry):
        b, d = n // cols, n % cols

        def load(j):
            return (
                [rv_ref[j // row_len, d, j % row_len, tile(g), :] for g in range(groups)],
                [wide_ref[4 * b + a, j] for a in range(4)],
            )

        gradient(load, col_len, 4 * b, la_ref, lb_ref, (d,), dl_ref, (spot(d, b),))
        return carry

    lax.fori_loop(0, (row_len // 4) * cols, left_back, 0)

    def back(d, carry):
        rows = block_rows(d)
        w_left = w_ref[:, : 2 * width]
        w_right = w_ref[:, 2 * width : 4 * width]
        send_ref[rows, :] = dot_nt(dr_ref[other, rows, :], w_right).astype(BF16)
        keep_y_ref[rows, :] = dot_nt(dr_ref[core, rows, :], w_right)
        gx_ref[rows, :] = dot_nt(dl_ref[rows, :], w_left)
        return carry

    lax.fori_loop(0, cols, back, 0)
    gx_ref[block_rows(step), :] += dot_nt(grad_logit, w_ref[:, 4 * width :])

    left_w = dot_tn(x_ref[...], dl_ref[...])
    right_w = dot_tn(own_x_ref[...], dr_ref[core]) + dot_tn(other_x_ref[...], dr_ref[other])
    wg_ref[0, :width, :] = left_w[:, :width]
    wg_ref[0, width : 2 * width, :] = left_w[:, width:]
    wg_ref[0, 2 * width :, :] = right_w[:, :width]
    wg_ref[1, :width, :] = right_w[:, width:]
    send_ref[cols * area :, :] = wg_ref[other].astype(BF16)
    keep_w_ref[...] = wg_ref[core]


def core_sum_kernel(cols, rows, keep_y_ref, keep_w_ref, got_ref, y_ref, own_ref, *rest):
    chunk_refs, sum_ref = rest[:-1], rest[-1]
    col = lax.axis_index("col")
    y_ref[...] = (keep_y_ref[...] + got_ref[:rows, :].astype(F32)).astype(BF16)
    total = keep_w_ref[...] + got_ref[rows:, :].astype(F32)
    sum_ref[...] = total.reshape(sum_ref.shape)
    own_ref[...] = sum_ref[col]
    for d in range(1, cols):
        chunk_refs[d - 1][...] = sum_ref[col ^ d].astype(BF16)


def row_sum_kernel(cols, area, gx_ref, got_ref, chunk_ref, own_ref, *send_refs):
    own_ref[...] = gx_ref[:area, :] + got_ref[:area, :].astype(F32)
    for d in range(1, cols):
        rows = slice(d * area, (d + 1) * area)
        send_refs[d - 1][:area, :] = (gx_ref[rows, :] + got_ref[rows, :].astype(F32)).astype(BF16)
        send_refs[d - 1][area:, :] = chunk_ref[...]


def pair_grad_kernel(cols, area, own_ref, pair_ref, chunk_ref, *rest):
    got_refs, (grad_ref, half_ref, order_ref) = rest[: cols - 1], rest[cols - 1 :]
    col = lax.axis_index("col")
    total = own_ref[...]
    order_ref[col] = chunk_ref[...].astype(F32)
    for d in range(1, cols):
        total = total + got_refs[d - 1][:area, :].astype(F32)
        order_ref[col ^ d] = got_refs[d - 1][area:, :].astype(F32)
    normed, scaled = layer_norm(pair_ref[...])
    grad_ref[...] = norm_back(total, normed, scaled)
    half_ref[...] = order_ref[...].reshape(half_ref.shape).astype(BF16)


def weights_kernel(width, mine_ref, other_ref, proj_ref, out_ref):
    first = (lax.axis_index("row") & 1) == 0
    mine, other = mine_ref[...].astype(F32), other_ref[...].astype(F32)
    low, high = jnp.where(first, mine, other), jnp.where(first, other, mine)
    for n in range(3):
        proj_ref[:, n * width : (n + 1) * width] = low[n * width : (n + 1) * width]
    for n in range(2):
        proj_ref[:, (3 + n) * width : (4 + n) * width] = high[n * width : (n + 1) * width]
    out_ref[...] = high[2 * width :]


def call(kernel, name, out_shape, args, scratch=(), smem=0):
    specs = [pl.BlockSpec(memory_space=pltpu.SMEM if n < smem else pltpu.VMEM) for n in range(len(args))]
    total = sum(a.size * a.dtype.itemsize for a in list(args) + list(out_shape))
    total += sum(_bytes(s) for s in scratch)
    return pl.pallas_call(
        kernel,
        out_shape=tuple(out_shape),
        in_specs=specs,
        out_specs=tuple(pl.BlockSpec(memory_space=pltpu.VMEM) for _ in out_shape),
        scratch_shapes=list(scratch),
        compiler_params=pltpu.CompilerParams(vmem_limit_bytes=min(60 << 20, total + (8 << 20))),
        name=name,
    )(*args)


def _bytes(ref):
    size = jnp.dtype(ref.dtype).itemsize
    for n in ref.shape:
        size *= n
    return size


def body(rows, cols, pair_input, block_valid, proj_weight, out_weight, cotangent):
    row_len, col_len, width = pair_input.shape
    area = row_len * col_len
    sizes = (row_len, col_len, width)
    planes = rows // 2
    assert planes == cols and col_len == 2 * row_len and cols & (cols - 1) == 0
    assert col_len % SEG == 0 and out_weight.shape == (width, width)

    def permute(value, target):
        pairs = []
        for z in range(planes):
            for core in range(2):
                for col in range(cols):
                    to = target(z, core, col)
                    pairs.append(((2 * z + core) * cols + col, (2 * to[0] + to[1]) * cols + to[2]))
        return lax.ppermute(value, ("row", "col"), pairs)

    def in_plane(value, d):
        return permute(value, lambda z, core, col: (z, core, col ^ d))

    def across(value, d):
        return permute(value, lambda z, core, col: (z ^ d, core, col))

    def to_pair(value):
        return permute(value, lambda z, core, col: (z, core, col ^ flip(z, cols)))

    def swap(value):
        return permute(value, lambda z, core, col: (z, 1 - core, col))

    def like(*shape, dtype=F32):
        return jax.ShapeDtypeStruct(shape, dtype)

    pair = pair_input.reshape(area, width)
    cot = cotangent.reshape(area, width)
    (low,) = call(norm_kernel, "norm", [like(area, width, dtype=BF16)], [pair])
    blocks = [low] + [in_plane(low, d) for d in range(1, cols)]
    x = jnp.concatenate(blocks, axis=0)
    own_x = permute(x, lambda z, core, col: (flip(col ^ z, cols), core, col))
    cot = to_pair(cot)
    gated = [like(cols, row_len, col_len, width)] * 3
    left = call(
        functools.partial(project_kernel, 0, cols, sizes),
        "left",
        gated,
        [block_valid, x, proj_weight],
        smem=1,
    )
    other_x = swap(own_x)
    right = call(
        functools.partial(project_kernel, 1, cols, sizes),
        "right",
        gated,
        [block_valid, own_x, proj_weight],
        smem=1,
    )
    tall = cols * area
    half = 3 * width
    both = pltpu.VMEM((2, cols, row_len, col_len, width), F32)
    flat = pltpu.VMEM((row_len, col_len, width), F32)
    pair_out, send, keep_y, gx, keep_w = call(
        functools.partial(main_kernel, cols, sizes),
        "triangle",
        [
            like(area, width),
            like(tall + half, width, dtype=BF16),
            like(tall, width),
            like(tall, width),
            like(half, width),
        ],
        [block_valid, *left, *right, x, own_x, other_x, cot, proj_weight, out_weight],
        [
            both,
            both,
            both,
            flat,
            flat,
            pltpu.VMEM((row_len, col_len, SEG, width), F32),
            pltpu.VMEM((tall, 2 * width), BF16),
            pltpu.VMEM((2, tall, 2 * width), BF16),
            pltpu.VMEM((2, half, width), F32),
        ],
        smem=1,
    )
    got = swap(send)
    chunk = half // cols
    y, mine, *chunks = call(
        functools.partial(core_sum_kernel, cols, tall),
        "core_sum",
        [like(tall, width, dtype=BF16), like(chunk, width)]
        + [like(chunk, width, dtype=BF16)] * (cols - 1),
        [keep_y, keep_w, got],
        [pltpu.VMEM((cols, chunk, width), F32)],
    )
    pair_out = to_pair(pair_out)
    back_y = permute(y, lambda z, core, col: (col ^ flip(z, cols), core, col))
    for d in range(1, cols):
        mine = mine + in_plane(chunks[d - 1], d).astype(F32)
    low_mine = mine.astype(BF16)
    for d in range(1, cols):
        mine = mine + across(low_mine, d).astype(F32)
    low_mine = mine.astype(BF16)
    own, *sends = call(
        functools.partial(row_sum_kernel, cols, area),
        "row_sum",
        [like(area, width)] + [like(area + chunk, width, dtype=BF16)] * (cols - 1),
        [gx, back_y, low_mine],
    )
    gets = [in_plane(sends[d - 1], d) for d in range(1, cols)]
    pair_grad, mine_w = call(
        functools.partial(pair_grad_kernel, cols, area),
        "pair_grad",
        [like(area, width), like(half, width, dtype=BF16)],
        [own, pair, low_mine, *gets],
        [pltpu.VMEM((cols, chunk, width), F32)],
    )
    proj_grad, out_grad = call(
        functools.partial(weights_kernel, width),
        "weights",
        [like(*proj_weight.shape), like(width, width)],
        [mine_w, swap(mine_w)],
    )
    shape = pair_input.shape
    return pair_out.reshape(shape), pair_grad.reshape(shape), proj_grad, out_grad


def solution(mesh):
    return jax.shard_map(
        functools.partial(body, mesh.shape["row"], mesh.shape["col"]),
        mesh=mesh,
        in_specs=(P("row", "col", None), P(), P(), P(), P("row", "col", None)),
        out_specs=(P("row", "col", None), P("row", "col", None), P(), P()),
        check_vma=False,
    )
```

time: 280 us -> 71.9 us (0.26)
  the two profiles are of different devices: /device:TPU:0 before, /device:TPU:29 now
where the time goes in v1:
time: 71.9 us; the launch traced here: 71.7 us
  starting transfers between devices  32.1 us (45%)
  waiting for transfers between devices  23.7 us (33%)
  Pallas kernels  13.3 us (18%)
  local copies, waits for them, and re-layouts  1.6 us (2%)
  between operations  0.82 us (1%)
    ppermute x19, starting transfers between devices, permute(): return lax.ppermute(value, ('row', 'col'), pairs)  32.1 us
    ppermute x19, waiting for transfers between devices, permute(): return lax.ppermute(value, ('row', 'col'), pairs)  23.7 us
    pallas_call x8, Pallas kernels, call(): pl.pallas_call(kernel, out_shape=tuple(out_shape), in_specs=specs, out_sp...  13.3 us
    unnamed x13, local copies, waits for them, and re-layouts  1.6 us
  transfers between devices with their start and end apart: 19, of which 10 were waited for; matrix products, arithmetic and copies ran while one was open for 0% of the time, Pallas kernels for 5%

profile of v1, /device:TPU:29, one launch (start us, length us, event | category | flops | bytes accessed | tf_op | source)
XLA Modules:
  0.0 71.7 jit_solution(16676585031568466919)
XLA Ops:
  1.8 1.2 %collective-permute-start.2 = (bf16[288,128]{1,0:T(8,128)(2,1)S(1)}, bf16[288,128]{1,0:T(8,128)(2,1)S(1)}, u32[]{:S(2)}, u32[]{:S(2)}) collective-permute-start(bf16[288,128]{1,0:T(8,128)(2,1)S(1)} %norm.1), channel_id=1, source_target_pairs={{0,3},{1,2},{2,1},{3,0},{4,7},{5,6},{6,5},{7,4},{8,11},{9,10},{10,... | collective-permute-start | bytes 221192 | tf_op jit(solution)/shard_map/ppermute | solution.py:352
  3.0 1.2 %collective-permute-start.1 = (bf16[288,128]{1,0:T(8,128)(2,1)S(1)}, bf16[288,128]{1,0:T(8,128)(2,1)S(1)}, u32[]{:S(2)}, u32[]{:S(2)}) collective-permute-start(bf16[288,128]{1,0:T(8,128)(2,1)S(1)} %norm.1), channel_id=1, source_target_pairs={{0,2},{1,3},{2,0},{3,1},{4,6},{5,7},{6,4},{7,5},{8,10},{9,11},{10,... | collective-permute-start | bytes 221192 | tf_op jit(solution)/shard_map/ppermute | solution.py:352
  4.5 1.5 %collective-permute-done.2 = bf16[288,128]{1,0:T(8,128)(2,1)S(1)} collective-permute-done((bf16[288,128]{1,0:T(8,128)(2,1)S(1)}, bf16[288,128]{1,0:T(8,128)(2,1)S(1)}, u32[]{:S(2)}, u32[]{:S(2)}) %collective-permute-start.2) | collective-permute-done | bytes 73760 | tf_op jit(solution)/shard_map/ppermute | solution.py:352
  6.0 2.1 %collective-permute-done.1 = bf16[288,128]{1,0:T(8,128)(2,1)S(1)} collective-permute-done((bf16[288,128]{1,0:T(8,128)(2,1)S(1)}, bf16[288,128]{1,0:T(8,128)(2,1)S(1)}, u32[]{:S(2)}, u32[]{:S(2)}) %collective-permute-start.1) | collective-permute-done | bytes 73760 | tf_op jit(solution)/shard_map/ppermute | solution.py:352
  8.1 2.1 %collective-permute-start.3 = (bf16[1152,128]{1,0:T(8,128)(2,1)S(1)}, bf16[1152,128]{1,0:T(8,128)(2,1)S(1)}, u32[]{:S(2)}, u32[]{:S(2)}) collective-permute-start(bf16[1152,128]{1,0:T(8,128)(2,1)S(1)} %pad_maximum_fusion.x_ref), channel_id=1, source_target_pairs={{0,0},{1,17},{2,10},{3,27},{4,4},{5,21},{6,14},{7,31},{8,16},{9,1}... | collective-permute-start | bytes 884744 | tf_op jit(solution)/shard_map/ppermute | solution.py:352
  10.2 7.5 %collective-permute-done.3.x_ref.own_x_ref = bf16[1152,128]{1,0:T(8,128)(2,1)S(1)} collective-permute-done((bf16[1152,128]{1,0:T(8,128)(2,1)S(1)}, bf16[1152,128]{1,0:T(8,128)(2,1)S(1)}, u32[]{:S(2)}, u32[]{:S(2)}) %collective-permute-start.3) | collective-permute-done | bytes 294944 | tf_op jit(solution)/shard_map/ppermute | solution.py:352
  17.7 2.6 %collective-permute-start.4 = (bf16[1152,128]{1,0:T(8,128)(2,1)S(1)}, bf16[1152,128]{1,0:T(8,128)(2,1)S(1)}, u32[]{:S(2)}, u32[]{:S(2)}) collective-permute-start(bf16[1152,128]{1,0:T(8,128)(2,1)S(1)} %collective-permute-done.3.x_ref.own_x_ref), channel_id=1, source_target_pairs={{0,4},{1,5},{2,6},{3,7},{4,0},{5,1},{6,2},{7,3},{8,12},{9,13},{10,... | collective-permute-start | bytes 884744 | tf_op jit(solution)/shard_map/ppermute | solution.py:352
  20.3 2.1 %collective-permute-start.5 = (f32[288,128]{1,0:T(8,128)S(1)}, f32[288,128]{1,0:T(8,128)S(1)}, u32[]{:S(2)}, u32[]{:S(2)}) collective-permute-start(f32[288,128]{1,0:T(8,128)S(1)} %bitcast.7), channel_id=1, source_target_pairs={{0,0},{1,1},{2,2},{3,3},{4,4},{5,5},{6,6},{7,7},{8,10},{9,11},{10,... | collective-permute-start | bytes 442376 | tf_op jit(solution)/shard_map/ppermute | solution.py:352
  22.5 1.3 %left.1 = (f32[4,12,24,128]{3,2,1,0:T(8,128)S(1)}, f32[4,12,24,128]{3,2,1,0:T(8,128)S(1)}, f32[4,12,24,128]{3,2,1,0:T(8,128)S(1)}) custom-call(s32[12]{0:T(128)S(1)} %copy-done.4, bf16[1152,128]{1,0:T(8,128)(2,1)S(1)} %pad_maximum_fusion.x_ref, bf16[128,640]{1,0:T(8,128)(2,1)S(1)} %copy-done), custom_call_target="tpu_custom_call" | custom-call | tf_op jit(solution)/shard_map/left/pallas_call | solution.py:319
  23.8 1.3 %right.1 = (f32[4,12,24,128]{3,2,1,0:T(8,128)S(1)}, f32[4,12,24,128]{3,2,1,0:T(8,128)S(1)}, f32[4,12,24,128]{3,2,1,0:T(8,128)S(1)}) custom-call(s32[12]{0:T(128)S(1)} %copy-done.4, bf16[1152,128]{1,0:T(8,128)(2,1)S(1)} %collective-permute-done.3.x_ref.own_x_ref, bf16[128,640]{1,0:T(8,128)(2,1)S(1)} %copy-done), custom_call_target="tpu_custom_call" | custom-call | tf_op jit(solution)/shard_map/right/pallas_call | solution.py:319
  25.2 3.4 %collective-permute-done.5.cot_ref = f32[288,128]{1,0:T(8,128)S(1)} collective-permute-done((f32[288,128]{1,0:T(8,128)S(1)}, f32[288,128]{1,0:T(8,128)S(1)}, u32[]{:S(2)}, u32[]{:S(2)}) %collective-permute-start.5) | collective-permute-done | bytes 147488 | tf_op jit(solution)/shard_map/ppermute | solution.py:352
  28.6 8.5 %triangle.1 = (f32[288,128]{1,0:T(8,128)S(1)}, bf16[1536,128]{1,0:T(8,128)(2,1)S(1)}, f32[1152,128]{1,0:T(8,128)S(1)}, f32[1152,128]{1,0:T(8,128)S(1)}, f32[384,128]{1,0:T(8,128)S(1)}) custom-call(s32[12]{0:T(128)S(1)} %copy-done.4, f32[4,12,24,128]{3,2,1,0:T(8,128)S(1)} %get-tuple-element.28.lv_ref, f32[4,12,24,128]{3,2,1,0:T(8,128)S(1)} %get-tuple-element.29.la_ref, ...), custom_call_target="tpu_custom_call" | custom-call | tf_op jit(solution)/shard_map/triangle/pallas_call | solution.py:319
  38.0 1.3 %collective-permute-done.7.got_ref = bf16[1536,128]{1,0:T(8,128)(2,1)S(1)} collective-permute-done((bf16[1536,128]{1,0:T(8,128)(2,1)S(1)}, bf16[1536,128]{1,0:T(8,128)(2,1)S(1)}, u32[]{:S(2)}, u32[]{:S(2)}) %collective-permute-start.7) | collective-permute-done | bytes 393248 | tf_op jit(solution)/shard_map/ppermute | solution.py:352
  39.5 1.3 %collective-permute-start.9 = (bf16[96,128]{1,0:T(8,128)(2,1)S(1)}, bf16[96,128]{1,0:T(8,128)(2,1)S(1)}, u32[]{:S(2)}, u32[]{:S(2)}) collective-permute-start(bf16[96,128]{1,0:T(8,128)(2,1)S(1)} %get-tuple-element.41), channel_id=1, source_target_pairs={{0,1},{1,0},{2,3},{3,2},{4,5},{5,4},{6,7},{7,6},{8,9},{9,8},{10,11... | collective-permute-start | bytes 73736 | tf_op jit(solution)/shard_map/ppermute | solution.py:352
  40.8 1.4 %collective-permute-start.11 = (bf16[96,128]{1,0:T(8,128)(2,1)S(1)}, bf16[96,128]{1,0:T(8,128)(2,1)S(1)}, u32[]{:S(2)}, u32[]{:S(2)}) collective-permute-start(bf16[96,128]{1,0:T(8,128)(2,1)S(1)} %get-tuple-element.43), channel_id=1, source_target_pairs={{0,3},{1,2},{2,1},{3,0},{4,7},{5,6},{6,5},{7,4},{8,11},{9,10},{10,... | collective-permute-start | bytes 73736 | tf_op jit(solution)/shard_map/ppermute | solution.py:352
  42.2 1.9 %collective-permute-start.8 = (bf16[1152,128]{1,0:T(8,128)(2,1)S(1)}, bf16[1152,128]{1,0:T(8,128)(2,1)S(1)}, u32[]{:S(2)}, u32[]{:S(2)}) collective-permute-start(bf16[1152,128]{1,0:T(8,128)(2,1)S(1)} %get-tuple-element.39), channel_id=1, source_target_pairs={{0,0},{1,9},{2,18},{3,27},{4,4},{5,13},{6,22},{7,31},{8,16},{9,25}... | collective-permute-start | bytes 884744 | tf_op jit(solution)/shard_map/ppermute | solution.py:352
  44.7 2.2 %collective-permute-start.13 = (bf16[96,128]{1,0:T(8,128)(2,1)S(1)}, bf16[96,128]{1,0:T(8,128)(2,1)S(1)}, u32[]{:S(2)}, u32[]{:S(2)}) collective-permute-start(bf16[96,128]{1,0:T(8,128)(2,1)S(1)} %fusion), channel_id=1, source_target_pairs={{0,16},{1,17},{2,18},{3,19},{4,20},{5,21},{6,22},{7,23},{8,24},{9,... | collective-permute-start | bytes 73736 | tf_op jit(solution)/shard_map/ppermute | solution.py:352
  46.9 1.1 %collective-permute-start.12 = (bf16[96,128]{1,0:T(8,128)(2,1)S(1)}, bf16[96,128]{1,0:T(8,128)(2,1)S(1)}, u32[]{:S(2)}, u32[]{:S(2)}) collective-permute-start(bf16[96,128]{1,0:T(8,128)(2,1)S(1)} %fusion), channel_id=1, source_target_pairs={{0,8},{1,9},{2,10},{3,11},{4,12},{5,13},{6,14},{7,15},{8,0},{9,1},... | collective-permute-start | bytes 73736 | tf_op jit(solution)/shard_map/ppermute | solution.py:352
  48.0 2.7 %collective-permute-done.14 = bf16[96,128]{1,0:T(8,128)(2,1)S(1)} collective-permute-done((bf16[96,128]{1,0:T(8,128)(2,1)S(1)}, bf16[96,128]{1,0:T(8,128)(2,1)S(1)}, u32[]{:S(2)}, u32[]{:S(2)}) %collective-permute-start.14) | collective-permute-done | bytes 24608 | tf_op jit(solution)/shard_map/ppermute | solution.py:352
  50.7 3.4 %collective-permute-done.13 = bf16[96,128]{1,0:T(8,128)(2,1)S(1)} collective-permute-done((bf16[96,128]{1,0:T(8,128)(2,1)S(1)}, bf16[96,128]{1,0:T(8,128)(2,1)S(1)}, u32[]{:S(2)}, u32[]{:S(2)}) %collective-permute-start.13) | collective-permute-done | bytes 24608 | tf_op jit(solution)/shard_map/ppermute | solution.py:352
  54.2 3.6 %collective-permute-start.15 = (bf16[384,128]{1,0:T(8,128)(2,1)S(1)}, bf16[384,128]{1,0:T(8,128)(2,1)S(1)}, u32[]{:S(2)}, u32[]{:S(2)}) collective-permute-start(bf16[384,128]{1,0:T(8,128)(2,1)S(1)} %get-tuple-element.45), channel_id=1, source_target_pairs={{0,1},{1,0},{2,3},{3,2},{4,5},{5,4},{6,7},{7,6},{8,9},{9,8},{10,11... | collective-permute-start | bytes 294920 | tf_op jit(solution)/shard_map/ppermute | solution.py:352
  57.8 1.3 %collective-permute-start.17 = (bf16[384,128]{1,0:T(8,128)(2,1)S(1)}, bf16[384,128]{1,0:T(8,128)(2,1)S(1)}, u32[]{:S(2)}, u32[]{:S(2)}) collective-permute-start(bf16[384,128]{1,0:T(8,128)(2,1)S(1)} %get-tuple-element.47), channel_id=1, source_target_pairs={{0,3},{1,2},{2,1},{3,0},{4,7},{5,6},{6,5},{7,4},{8,11},{9,10},{10,... | collective-permute-start | bytes 294920 | tf_op jit(solution)/shard_map/ppermute | solution.py:352
  59.1 3.0 %collective-permute-start.6 = (f32[288,128]{1,0:T(8,128)S(1)}, f32[288,128]{1,0:T(8,128)S(1)}, u32[]{:S(2)}, u32[]{:S(2)}) collective-permute-start(f32[288,128]{1,0:T(8,128)S(1)} %get-tuple-element.34), channel_id=1, source_target_pairs={{0,0},{1,1},{2,2},{3,3},{4,4},{5,5},{6,6},{7,7},{8,10},{9,11},{10,... | collective-permute-start | bytes 442376 | tf_op jit(solution)/shard_map/ppermute | solution.py:352
  63.6 5.6 %collective-permute-start.18 = (bf16[384,128]{1,0:T(8,128)(2,1)S(1)}, bf16[384,128]{1,0:T(8,128)(2,1)S(1)}, u32[]{:S(2)}, u32[]{:S(2)}) collective-permute-start(bf16[384,128]{1,0:T(8,128)(2,1)S(1)} %get-tuple-element.49.mine_ref), channel_id=1, source_target_pairs={{0,4},{1,5},{2,6},{3,7},{4,0},{5,1},{6,2},{7,3},{8,12},{9,13},{10,... | collective-permute-start | bytes 294920 | tf_op jit(solution)/shard_map/ppermute | solution.py:352
  (38 shorter events, 6.9 us)
Async XLA Ops:
  1.7 18.6 %copy-start.5 = (f32[12,24,128]{2,1,0:T(8,128)S(1)}, f32[12,24,128]{2,1,0:T(8,128)}, u32[]{:S(2)}) copy-start(f32[12,24,128]{2,1,0:T(8,128)} %param.9) | copy-start | bytes 442372
  1.8 20.7 %copy-start = (bf16[128,640]{1,0:T(8,128)(2,1)S(1)}, bf16[128,640]{1,0:T(8,128)(2,1)}, u32[]{:S(2)}) copy-start(bf16[128,640]{1,0:T(8,128)(2,1)} %w_ref.5) | copy-start | bytes 491524
  1.8 4.2 %collective-permute-start.2 = (bf16[288,128]{1,0:T(8,128)(2,1)S(1)}, bf16[288,128]{1,0:T(8,128)(2,1)S(1)}, u32[]{:S(2)}, u32[]{:S(2)}) collective-permute-start(bf16[288,128]{1,0:T(8,128)(2,1)S(1)} %norm.1), channel_id=1, source_target_pairs={{0,3},{1,2},{2,1},{3,0},{4,7},{5,6},{6,5},{7,4},{8,11},{9,10},{10,... | collective-permute-start | bytes 221192 | tf_op jit(solution)/shard_map/ppermute | solution.py:352
  3.0 5.1 %collective-permute-start.1 = (bf16[288,128]{1,0:T(8,128)(2,1)S(1)}, bf16[288,128]{1,0:T(8,128)(2,1)S(1)}, u32[]{:S(2)}, u32[]{:S(2)}) collective-permute-start(bf16[288,128]{1,0:T(8,128)(2,1)S(1)} %norm.1), channel_id=1, source_target_pairs={{0,2},{1,3},{2,0},{3,1},{4,6},{5,7},{6,4},{7,5},{8,10},{9,11},{10,... | collective-permute-start | bytes 221192 | tf_op jit(solution)/shard_map/ppermute | solution.py:352
  4.2 3.9 %collective-permute-start = (bf16[288,128]{1,0:T(8,128)(2,1)S(1)}, bf16[288,128]{1,0:T(8,128)(2,1)S(1)}, u32[]{:S(2)}, u32[]{:S(2)}) collective-permute-start(bf16[288,128]{1,0:T(8,128)(2,1)S(1)} %norm.1), channel_id=1, source_target_pairs={{0,1},{1,0},{2,3},{3,2},{4,5},{5,4},{6,7},{7,6},{8,9},{9,8},{10,11... | collective-permute-start | bytes 221192 | tf_op jit(solution)/shard_map/ppermute | solution.py:352
  8.1 14.4 %copy-start.4 = (s32[12]{0:T(128)S(1)}, s32[12]{0:T(128)}, u32[]{:S(2)}) copy-start(s32[12]{0:T(128)} %valid_ref.5) | copy-start | bytes 148
  8.1 9.6 %collective-permute-start.3 = (bf16[1152,128]{1,0:T(8,128)(2,1)S(1)}, bf16[1152,128]{1,0:T(8,128)(2,1)S(1)}, u32[]{:S(2)}, u32[]{:S(2)}) collective-permute-start(bf16[1152,128]{1,0:T(8,128)(2,1)S(1)} %pad_maximum_fusion.x_ref), channel_id=1, source_target_pairs={{0,0},{1,17},{2,10},{3,27},{4,4},{5,21},{6,14},{7,31},{8,16},{9,1}... | collective-permute-start | bytes 884744 | tf_op jit(solution)/shard_map/ppermute | solution.py:352
  17.7 10.9 %collective-permute-start.4 = (bf16[1152,128]{1,0:T(8,128)(2,1)S(1)}, bf16[1152,128]{1,0:T(8,128)(2,1)S(1)}, u32[]{:S(2)}, u32[]{:S(2)}) collective-permute-start(bf16[1152,128]{1,0:T(8,128)(2,1)S(1)} %collective-permute-done.3.x_ref.own_x_ref), channel_id=1, source_target_pairs={{0,4},{1,5},{2,6},{3,7},{4,0},{5,1},{6,2},{7,3},{8,12},{9,13},{10,... | collective-permute-start | bytes 884744 | tf_op jit(solution)/shard_map/ppermute | solution.py:352
  20.3 8.3 %collective-permute-start.5 = (f32[288,128]{1,0:T(8,128)S(1)}, f32[288,128]{1,0:T(8,128)S(1)}, u32[]{:S(2)}, u32[]{:S(2)}) collective-permute-start(f32[288,128]{1,0:T(8,128)S(1)} %bitcast.7), channel_id=1, source_target_pairs={{0,0},{1,1},{2,2},{3,3},{4,4},{5,5},{6,6},{7,7},{8,10},{9,11},{10,... | collective-permute-start | bytes 442376 | tf_op jit(solution)/shard_map/ppermute | solution.py:352
  23.8 4.8 %copy-start.3 = (bf16[128,128]{1,0:T(8,128)(2,1)S(1)}, bf16[128,128]{1,0:T(8,128)(2,1)}, u32[]{:S(2)}) copy-start(bf16[128,128]{1,0:T(8,128)(2,1)} %wout_ref.1) | copy-start | bytes 98308
  37.1 2.2 %collective-permute-start.7 = (bf16[1536,128]{1,0:T(8,128)(2,1)S(1)}, bf16[1536,128]{1,0:T(8,128)(2,1)S(1)}, u32[]{:S(2)}, u32[]{:S(2)}) collective-permute-start(bf16[1536,128]{1,0:T(8,128)(2,1)S(1)} %get-tuple-element.38), channel_id=1, source_target_pairs={{0,4},{1,5},{2,6},{3,7},{4,0},{5,1},{6,2},{7,3},{8,12},{9,13},{10,... | collective-permute-start | bytes 1179656 | tf_op jit(solution)/shard_map/ppermute | solution.py:352
  39.5 4.6 %collective-permute-start.9 = (bf16[96,128]{1,0:T(8,128)(2,1)S(1)}, bf16[96,128]{1,0:T(8,128)(2,1)S(1)}, u32[]{:S(2)}, u32[]{:S(2)}) collective-permute-start(bf16[96,128]{1,0:T(8,128)(2,1)S(1)} %get-tuple-element.41), channel_id=1, source_target_pairs={{0,1},{1,0},{2,3},{3,2},{4,5},{5,4},{6,7},{7,6},{8,9},{9,8},{10,11... | collective-permute-start | bytes 73736 | tf_op jit(solution)/shard_map/ppermute | solution.py:352
  40.8 3.4 %collective-permute-start.10 = (bf16[96,128]{1,0:T(8,128)(2,1)S(1)}, bf16[96,128]{1,0:T(8,128)(2,1)S(1)}, u32[]{:S(2)}, u32[]{:S(2)}) collective-permute-start(bf16[96,128]{1,0:T(8,128)(2,1)S(1)} %get-tuple-element.42), channel_id=1, source_target_pairs={{0,2},{1,3},{2,0},{3,1},{4,6},{5,7},{6,4},{7,5},{8,10},{9,11},{10,... | collective-permute-start | bytes 73736 | tf_op jit(solution)/shard_map/ppermute | solution.py:352
  40.8 3.6 %collective-permute-start.11 = (bf16[96,128]{1,0:T(8,128)(2,1)S(1)}, bf16[96,128]{1,0:T(8,128)(2,1)S(1)}, u32[]{:S(2)}, u32[]{:S(2)}) collective-permute-start(bf16[96,128]{1,0:T(8,128)(2,1)S(1)} %get-tuple-element.43), channel_id=1, source_target_pairs={{0,3},{1,2},{2,1},{3,0},{4,7},{5,6},{6,5},{7,4},{8,11},{9,10},{10,... | collective-permute-start | bytes 73736 | tf_op jit(solution)/shard_map/ppermute | solution.py:352
  42.2 11.9 %collective-permute-start.8 = (bf16[1152,128]{1,0:T(8,128)(2,1)S(1)}, bf16[1152,128]{1,0:T(8,128)(2,1)S(1)}, u32[]{:S(2)}, u32[]{:S(2)}) collective-permute-start(bf16[1152,128]{1,0:T(8,128)(2,1)S(1)} %get-tuple-element.39), channel_id=1, source_target_pairs={{0,0},{1,9},{2,18},{3,27},{4,4},{5,13},{6,22},{7,31},{8,16},{9,25}... | collective-permute-start | bytes 884744 | tf_op jit(solution)/shard_map/ppermute | solution.py:352
  44.4 6.3 %collective-permute-start.14 = (bf16[96,128]{1,0:T(8,128)(2,1)S(1)}, bf16[96,128]{1,0:T(8,128)(2,1)S(1)}, u32[]{:S(2)}, u32[]{:S(2)}) collective-permute-start(bf16[96,128]{1,0:T(8,128)(2,1)S(1)} %fusion), channel_id=1, source_target_pairs={{0,24},{1,25},{2,26},{3,27},{4,28},{5,29},{6,30},{7,31},{8,16},{9,... | collective-permute-start | bytes 73736 | tf_op jit(solution)/shard_map/ppermute | solution.py:352
  44.7 9.4 %collective-permute-start.13 = (bf16[96,128]{1,0:T(8,128)(2,1)S(1)}, bf16[96,128]{1,0:T(8,128)(2,1)S(1)}, u32[]{:S(2)}, u32[]{:S(2)}) collective-permute-start(bf16[96,128]{1,0:T(8,128)(2,1)S(1)} %fusion), channel_id=1, source_target_pairs={{0,16},{1,17},{2,18},{3,19},{4,20},{5,21},{6,22},{7,23},{8,24},{9,... | collective-permute-start | bytes 73736 | tf_op jit(solution)/shard_map/ppermute | solution.py:352
  46.9 7.2 %collective-permute-start.12 = (bf16[96,128]{1,0:T(8,128)(2,1)S(1)}, bf16[96,128]{1,0:T(8,128)(2,1)S(1)}, u32[]{:S(2)}, u32[]{:S(2)}) collective-permute-start(bf16[96,128]{1,0:T(8,128)(2,1)S(1)} %fusion), channel_id=1, source_target_pairs={{0,8},{1,9},{2,10},{3,11},{4,12},{5,13},{6,14},{7,15},{8,0},{9,1},... | collective-permute-start | bytes 73736 | tf_op jit(solution)/shard_map/ppermute | solution.py:352
  54.1 8.5 %copy-start.2 = (f32[12,24,128]{2,1,0:T(8,128)S(1)}, f32[12,24,128]{2,1,0:T(8,128)}, u32[]{:S(2)}) copy-start(f32[12,24,128]{2,1,0:T(8,128)} %param.5) | copy-start | bytes 442372
  54.2 7.9 %collective-permute-start.15 = (bf16[384,128]{1,0:T(8,128)(2,1)S(1)}, bf16[384,128]{1,0:T(8,128)(2,1)S(1)}, u32[]{:S(2)}, u32[]{:S(2)}) collective-permute-start(bf16[384,128]{1,0:T(8,128)(2,1)S(1)} %get-tuple-element.45), channel_id=1, source_target_pairs={{0,1},{1,0},{2,3},{3,2},{4,5},{5,4},{6,7},{7,6},{8,9},{9,8},{10,11... | collective-permute-start | bytes 294920 | tf_op jit(solution)/shard_map/ppermute | solution.py:352
  57.8 4.8 %collective-permute-start.16 = (bf16[384,128]{1,0:T(8,128)(2,1)S(1)}, bf16[384,128]{1,0:T(8,128)(2,1)S(1)}, u32[]{:S(2)}, u32[]{:S(2)}) collective-permute-start(bf16[384,128]{1,0:T(8,128)(2,1)S(1)} %get-tuple-element.46), channel_id=1, source_target_pairs={{0,2},{1,3},{2,0},{3,1},{4,6},{5,7},{6,4},{7,5},{8,10},{9,11},{10,... | collective-permute-start | bytes 294920 | tf_op jit(solution)/shard_map/ppermute | solution.py:352
  57.8 4.8 %collective-permute-start.17 = (bf16[384,128]{1,0:T(8,128)(2,1)S(1)}, bf16[384,128]{1,0:T(8,128)(2,1)S(1)}, u32[]{:S(2)}, u32[]{:S(2)}) collective-permute-start(bf16[384,128]{1,0:T(8,128)(2,1)S(1)} %get-tuple-element.47), channel_id=1, source_target_pairs={{0,3},{1,2},{2,1},{3,0},{4,7},{5,6},{6,5},{7,4},{8,11},{9,10},{10,... | collective-permute-start | bytes 294920 | tf_op jit(solution)/shard_map/ppermute | solution.py:352
  59.1 10.2 %collective-permute-start.6 = (f32[288,128]{1,0:T(8,128)S(1)}, f32[288,128]{1,0:T(8,128)S(1)}, u32[]{:S(2)}, u32[]{:S(2)}) collective-permute-start(f32[288,128]{1,0:T(8,128)S(1)} %get-tuple-element.34), channel_id=1, source_target_pairs={{0,0},{1,1},{2,2},{3,3},{4,4},{5,5},{6,6},{7,7},{8,10},{9,11},{10,... | collective-permute-start | bytes 442376 | tf_op jit(solution)/shard_map/ppermute | solution.py:352
  63.6 6.6 %collective-permute-start.18 = (bf16[384,128]{1,0:T(8,128)(2,1)S(1)}, bf16[384,128]{1,0:T(8,128)(2,1)S(1)}, u32[]{:S(2)}, u32[]{:S(2)}) collective-permute-start(bf16[384,128]{1,0:T(8,128)(2,1)S(1)} %get-tuple-element.49.mine_ref), channel_id=1, source_target_pairs={{0,4},{1,5},{2,6},{3,7},{4,0},{5,1},{6,2},{7,3},{8,12},{9,13},{10,... | collective-permute-start | bytes 294920 | tf_op jit(solution)/shard_map/ppermute | solution.py:352
  (1 other events, 0.9 us)

commit v2 on v1

v2 whole, which is shorter than its diff:
```python
import functools

import jax
import jax.numpy as jnp
from jax import lax
from jax.experimental import pallas as pl
from jax.experimental.pallas import tpu as pltpu
from jax.sharding import PartitionSpec as P

SEG = 8
F32 = jnp.float32
BF16 = jnp.bfloat16


def sigmoid(values):
    return 0.5 * jnp.tanh(0.5 * values) + 0.5


def layer_norm(values):
    center = values - jnp.mean(values, axis=-1, keepdims=True)
    scaled = lax.rsqrt(jnp.mean(center * center, axis=-1, keepdims=True) + 1e-05)
    return center * scaled, scaled


def norm_back(grad_norm, normed, scaled):
    first_mean = jnp.mean(grad_norm, axis=-1, keepdims=True)
    second = jnp.mean(grad_norm * normed, axis=-1, keepdims=True)
    return scaled * (grad_norm - first_mean - normed * second)


def dot(a, b):
    return jnp.dot(a, b, preferred_element_type=F32)


def dot_nt(a, b):
    return lax.dot_general(a, b, (((1,), (1,)), ((), ())), preferred_element_type=F32)


def dot_tn(a, b):
    return lax.dot_general(a, b, (((0,), (0,)), ((), ())), preferred_element_type=F32)


def flip(z, count):
    out, bit = z & 0, 1
    top = count >> 1
    while bit < count:
        if isinstance(z, int):
            out |= top if z & bit else 0
        else:
            out = out + jnp.where((z & bit) != 0, top, 0)
        bit, top = bit << 1, top >> 1
    return out


def place(cols):
    row, col = lax.axis_index("row"), lax.axis_index("col")
    z, core = row >> 1, row & 1
    step = flip(z, cols)
    return row, core, col, step, col ^ step


def norm_kernel(pair_ref, low_ref):
    low_ref[...] = layer_norm(pair_ref[...])[0].astype(BF16)


def project_block(projected, valid_ref, row, block, sizes, index, v_ref, a_ref, b_ref):
    row_len, col_len, width = sizes
    spot = lax.broadcasted_iota(jnp.int32, (SEG, width), 0)
    groups = col_len // SEG
    keep_col = jnp.concatenate(
        [jnp.where(spot < valid_ref[block * groups + g], 1.0, 0.0) for g in range(groups)], axis=0
    )
    for i in range(row_len):
        token = row * row_len + i
        valid = (token & (SEG - 1)) < valid_ref[token >> 3]
        keep = keep_col * jnp.where(valid, 1.0, 0.0)
        part = projected[i * col_len : (i + 1) * col_len]
        gate = sigmoid(part[:, :width])
        kept = keep * gate
        gated = kept * part[:, width:]
        v_ref[index + (i,)] = gated.astype(BF16).astype(F32)
        a_ref[index + (i,)] = gated * (1.0 - gate)
        b_ref[index + (i,)] = kept


def project_kernel(side, cols, sizes, valid_ref, x_ref, w_ref, *refs):
    row_len, col_len, width = sizes
    area = row_len * col_len
    row, core, col, step, pair = place(cols)
    half = core if side < 2 else 1 - core
    if side:
        row = 2 * pair + half
    base = 2 * width if side else 0
    outs = refs[-3:]

    def one(d, carry):
        rows = pl.ds(pl.multiple_of(d * area, area), area)
        projected = dot(x_ref[rows, :], w_ref[:, base : base + 2 * width])
        index = (half, d) if side else (d,)
        project_block(projected, valid_ref, row, col ^ d, sizes, index, *outs)
        return carry

    lax.fori_loop(0, cols, one, 0)


def tile(g):
    return slice(g * SEG, (g + 1) * SEG)


def rows_of(d, area):
    return pl.ds(pl.multiple_of(d * area, area), area)


def mix_kernel(
    cols,
    sizes,
    lv_ref,
    rv_ref,
    x_ref,
    cot_ref,
    w_ref,
    wout_ref,
    out_ref,
    logit_ref,
    wide_ref,
    wg_ref,
    mixed_ref,
    grad_ref,
):
    row_len, col_len, width = sizes
    area = row_len * col_len
    row, core, col, step, pair = place(cols)
    groups = col_len // SEG
    zero = jnp.zeros((SEG, width), F32)

    def mix_rows(pair_at, carry):
        for jt in range(groups):

            def over(d, acc):
                for g in range(groups):
                    left = [lv_ref[d, 2 * pair_at + a, tile(g), :] for a in range(2)]
                    right = [
                        rv_ref[j // row_len, d, j % row_len, tile(g), :]
                        for j in range(jt * SEG, (jt + 1) * SEG)
                    ]
                    acc = tuple(acc[n] + left[n // SEG] * right[n % SEG] for n in range(2 * SEG))
                return acc

            acc = lax.fori_loop(0, cols, over, (zero,) * (2 * SEG))
            for a in range(2):
                mixed_ref[2 * pair_at + a, tile(jt), :] = jnp.concatenate(
                    [jnp.sum(acc[a * SEG + n], axis=0, keepdims=True) for n in range(SEG)], axis=0
                )
        return carry

    lax.fori_loop(0, row_len // 2, mix_rows, 0)

    mixed_norm, mixed_scale = layer_norm(mixed_ref[...].reshape(area, width))
    mixed_low = mixed_norm.astype(BF16)
    update = dot(mixed_low, wout_ref[...])
    home = x_ref[rows_of(step, area), :]
    out_gate = sigmoid(dot(home, w_ref[:, 4 * width :]))
    out_ref[...] = out_gate * update
    gated_cot = cot_ref[...] * out_gate
    grad_logit = (gated_cot * update * (1.0 - out_gate)).astype(BF16)
    grad_update = gated_cot.astype(BF16)
    logit_ref[...] = grad_logit
    wg_ref[:width, :] = dot_tn(home, grad_logit)
    wg_ref[width:, :] = dot_tn(mixed_low, grad_update)
    grad_mixed = norm_back(dot_nt(grad_update, wout_ref[...]), mixed_norm, mixed_scale)
    grad_ref[...] = grad_mixed.astype(BF16).astype(F32).reshape(row_len, col_len, width)

    def widen(i, carry):
        for j in range(col_len):
            wide_ref[i, j] = jnp.broadcast_to(grad_ref[i, j : j + 1, :], (SEG, width))
        return carry

    lax.fori_loop(0, row_len, widen, 0)


def gradient(load, count, first, sizes, a_ref, b_ref, index, d_ref, d_index):
    row_len, col_len, width = sizes
    groups = col_len // SEG
    acc = [[jnp.zeros((SEG, width), F32)] * groups for _ in range(4)]
    for n in range(count):
        value, weights = load(n)
        for a in range(4):
            for g in range(groups):
                acc[a][g] = acc[a][g] + value[g] * weights[a]
    full = [jnp.concatenate(acc[a], axis=0) for a in range(4)]
    gates = [full[a] * a_ref[index + (first + a,)] for a in range(4)]
    values = [full[a] * b_ref[index + (first + a,)] for a in range(4)]
    d_ref[d_index + (slice(0, width),)] = jnp.concatenate(gates, axis=0).astype(BF16)
    d_ref[d_index + (slice(width, 2 * width),)] = jnp.concatenate(values, axis=0).astype(BF16)


def grads_kernel(
    cols, sizes, lv_ref, la_ref, lb_ref, rv_ref, ra_ref, rb_ref, wide_ref, dl_ref, dr_ref
):
    row_len, col_len, width = sizes
    area = row_len * col_len
    groups = col_len // SEG
    quarter = 4 * col_len

    def spot(d, b):
        return pl.ds(pl.multiple_of(d * area + b * quarter, quarter), quarter)

    for half in range(2):

        def right_back(n, carry):
            b, d = n // cols, n % cols

            def load(i):
                return (
                    [lv_ref[d, i, tile(g), :] for g in range(groups)],
                    [wide_ref[i, half * row_len + 4 * b + a] for a in range(4)],
                )

            where = (half, spot(d, b))
            gradient(load, row_len, 4 * b, sizes, ra_ref, rb_ref, (half, d), dr_ref, where)
            return carry

        lax.fori_loop(0, (row_len // 4) * cols, right_back, 0)

    def left_back(n, carry):
        b, d = n // cols, n % cols

        def load(j):
            return (
                [rv_ref[j // row_len, d, j % row_len, tile(g), :] for g in range(groups)],
                [wide_ref[4 * b + a, j] for a in range(4)],
            )

        gradient(load, col_len, 4 * b, sizes, la_ref, lb_ref, (d,), dl_ref, (spot(d, b),))
        return carry

    lax.fori_loop(0, (row_len // 4) * cols, left_back, 0)


def weight_sums_kernel(
    width, x_ref, own_x_ref, other_x_ref, dl_ref, dr_ref, wg_ref, send_ref, keep_ref, sum_ref
):
    core = lax.axis_index("row") & 1
    left_w = dot_tn(x_ref[...], dl_ref[...])
    right_w = dot_tn(own_x_ref[...], dr_ref[core]) + dot_tn(other_x_ref[...], dr_ref[1 - core])
    sum_ref[0, :width, :] = left_w[:, :width]
    sum_ref[0, width : 2 * width, :] = left_w[:, width:]
    sum_ref[0, 2 * width :, :] = right_w[:, :width]
    sum_ref[1, :width, :] = right_w[:, width:]
    sum_ref[1, width:, :] = wg_ref[...]
    send_ref[...] = sum_ref[1 - core].astype(BF16)
    keep_ref[...] = sum_ref[core]


def back_other_kernel(cols, area, width, dr_ref, w_ref, send_ref):
    core = lax.axis_index("row") & 1

    def back(d, carry):
        rows = rows_of(d, area)
        part = dot_nt(dr_ref[1 - core, rows, :], w_ref[:, 2 * width : 4 * width])
        send_ref[rows, :] = part.astype(BF16)
        return carry

    lax.fori_loop(0, cols, back, 0)


def back_own_kernel(cols, area, width, dl_ref, dr_ref, logit_ref, w_ref, keep_ref, gx_ref):
    row, core, col, step, pair = place(cols)

    def back(d, carry):
        rows = rows_of(d, area)
        keep_ref[rows, :] = dot_nt(dr_ref[core, rows, :], w_ref[:, 2 * width : 4 * width])
        gx_ref[rows, :] = dot_nt(dl_ref[rows, :], w_ref[:, : 2 * width])
        return carry

    lax.fori_loop(0, cols, back, 0)
    gx_ref[rows_of(step, area), :] += dot_nt(logit_ref[...], w_ref[:, 4 * width :])


def core_sum_kernel(keep_ref, got_ref, y_ref):
    y_ref[...] = (keep_ref[...] + got_ref[...].astype(F32)).astype(BF16)


def chunks_kernel(cols, keep_ref, got_ref, own_ref, *rest):
    chunk_refs, sum_ref = rest[:-1], rest[-1]
    col = lax.axis_index("col")
    total = keep_ref[...] + got_ref[...].astype(F32)
    sum_ref[...] = total.reshape(sum_ref.shape)
    own_ref[...] = sum_ref[col]
    for d in range(1, cols):
        chunk_refs[d - 1][...] = sum_ref[col ^ d].astype(BF16)


def row_sum_kernel(cols, area, gx_ref, got_ref, chunk_ref, swapped_ref, own_ref, *send_refs):
    chunk = chunk_ref.shape[0]
    own_ref[...] = gx_ref[:area, :] + got_ref[:area, :].astype(F32)
    for d in range(1, cols):
        rows = slice(d * area, (d + 1) * area)
        send_refs[d - 1][:area, :] = (gx_ref[rows, :] + got_ref[rows, :].astype(F32)).astype(BF16)
        send_refs[d - 1][area : area + chunk, :] = chunk_ref[...]
        send_refs[d - 1][area + chunk :, :] = swapped_ref[...]


def final_kernel(cols, area, own_ref, pair_ref, chunk_ref, swapped_ref, home_ref, *rest):
    got_refs = rest[: cols - 1]
    grad_ref, proj_ref, out_ref, home_out_ref, order_ref = rest[cols - 1 :]
    chunk, width = chunk_ref.shape
    col, core = lax.axis_index("col"), lax.axis_index("row") & 1
    home_out_ref[...] = home_ref[...]
    total = own_ref[...]
    order_ref[core, col] = chunk_ref[...].astype(F32)
    order_ref[1 - core, col] = swapped_ref[...].astype(F32)
    for d in range(1, cols):
        got = got_refs[d - 1]
        total = total + got[:area, :].astype(F32)
        order_ref[core, col ^ d] = got[area : area + chunk, :].astype(F32)
        order_ref[1 - core, col ^ d] = got[area + chunk :, :].astype(F32)
    normed, scaled = layer_norm(pair_ref[...])
    grad_ref[...] = norm_back(total, normed, scaled)
    whole = order_ref[...].reshape(6 * width, width)
    for n in range(5):
        proj_ref[:, n * width : (n + 1) * width] = whole[n * width : (n + 1) * width]
    out_ref[...] = whole[5 * width :]


def call(kernel, name, micros, out_shape, args, scratch=(), smem=0, aliases=None):
    specs = [pl.BlockSpec(memory_space=pltpu.SMEM if n < smem else pltpu.VMEM) for n in range(len(args))]
    total = sum(_bytes(ref) for ref in [*args, *out_shape, *scratch])
    return pl.pallas_call(
        kernel,
        out_shape=tuple(out_shape),
        in_specs=specs,
        out_specs=tuple(pl.BlockSpec(memory_space=pltpu.VMEM) for _ in out_shape),
        scratch_shapes=list(scratch),
        input_output_aliases=aliases or {},
        cost_estimate=pl.CostEstimate(
            flops=0, transcendentals=0, bytes_accessed=int(micros * 3_690_000)
        ),
        compiler_params=pltpu.CompilerParams(vmem_limit_bytes=min(60 << 20, total + (8 << 20))),
        name=name,
    )(*args)


def _bytes(ref):
    size = jnp.dtype(ref.dtype).itemsize
    for n in ref.shape:
        size *= n
    return size


def body(rows, cols, pair_input, block_valid, proj_weight, out_weight, cotangent):
    row_len, col_len, width = pair_input.shape
    area = row_len * col_len
    sizes = (row_len, col_len, width)
    planes = rows // 2
    assert planes == cols and col_len == 2 * row_len and cols & (cols - 1) == 0
    assert col_len % SEG == 0 and out_weight.shape == (width, width)

    def permute(value, target):
        pairs = []
        for z in range(planes):
            for core in range(2):
                for col in range(cols):
                    to = target(z, core, col)
                    pairs.append(((2 * z + core) * cols + col, (2 * to[0] + to[1]) * cols + to[2]))
        return lax.ppermute(value, ("row", "col"), pairs)

    def in_plane(value, d):
        return permute(value, lambda z, core, col: (z, core, col ^ d))

    def across(value, d):
        return permute(value, lambda z, core, col: (z ^ d, core, col))

    def to_pair(value):
        return permute(value, lambda z, core, col: (z, core, col ^ flip(z, cols)))

    def swap(value):
        return permute(value, lambda z, core, col: (z, 1 - core, col))

    def like(*shape, dtype=F32):
        return jax.ShapeDtypeStruct(shape, dtype)

    pair = pair_input.reshape(area, width)
    cot = cotangent.reshape(area, width)
    tall, half = cols * area, 3 * width
    chunk = half // cols
    (low,) = call(norm_kernel, "norm", 0.3, [like(area, width, dtype=BF16)], [pair])
    blocks = [low] + [in_plane(low, d) for d in range(1, cols)]
    x = jnp.concatenate(blocks, axis=0)
    own_x = permute(x, lambda z, core, col: (flip(col ^ z, cols), core, col))
    cot, x = lax.optimization_barrier((cot, x))
    cot = to_pair(cot)
    left = call(
        functools.partial(project_kernel, 0, cols, sizes),
        "left",
        1.4,
        [like(cols, row_len, col_len, width)] * 3,
        [block_valid, x, proj_weight],
        smem=1,
    )
    left, cot, own_x = lax.optimization_barrier((left, cot, own_x))
    other_x = swap(own_x)
    right_shape = [like(2, cols, row_len, col_len, width)] * 3
    right = call(
        functools.partial(project_kernel, 1, cols, sizes),
        "right_own",
        1.4,
        right_shape,
        [block_valid, own_x, proj_weight],
        smem=1,
    )
    right = call(
        functools.partial(project_kernel, 2, cols, sizes),
        "right_other",
        1.4,
        right_shape,
        [block_valid, other_x, proj_weight, *right],
        smem=1,
        aliases={3: 0, 4: 1, 5: 2},
    )
    flat = pltpu.VMEM((row_len, col_len, width), F32)
    pair_out, grad_logit, wide, wg = call(
        functools.partial(mix_kernel, cols, sizes),
        "mix",
        3.0,
        [
            like(area, width),
            like(area, width, dtype=BF16),
            like(row_len, col_len, SEG, width),
            like(2 * width, width),
        ],
        [left[0], right[0], x, cot, proj_weight, out_weight],
        [flat, flat],
    )
    dl, dr = call(
        functools.partial(grads_kernel, cols, sizes),
        "grads",
        3.0,
        [like(tall, 2 * width, dtype=BF16), like(2, tall, 2 * width, dtype=BF16)],
        [*left, *right, wide],
    )
    send_w, keep_w = call(
        functools.partial(weight_sums_kernel, width),
        "weight_sums",
        1.0,
        [like(half, width, dtype=BF16), like(half, width)],
        [x, own_x, other_x, dl, dr, wg],
        [pltpu.VMEM((2, half, width), F32)],
    )
    got_w = swap(send_w)
    (send_y,) = call(
        functools.partial(back_other_kernel, cols, area, width),
        "back_other",
        0.4,
        [like(tall, width, dtype=BF16)],
        [dr, proj_weight],
    )
    got_y = swap(send_y)
    keep_y, gx = call(
        functools.partial(back_own_kernel, cols, area, width),
        "back_own",
        0.6,
        [like(tall, width)] * 2,
        [dl, dr, grad_logit, proj_weight],
    )
    mine, *chunks = call(
        functools.partial(chunks_kernel, cols),
        "chunks",
        0.1,
        [like(chunk, width)] + [like(chunk, width, dtype=BF16)] * (cols - 1),
        [keep_w, got_w],
        [pltpu.VMEM((cols, chunk, width), F32)],
    )
    (y,) = call(core_sum_kernel, "core_sum", 0.1, [like(tall, width, dtype=BF16)], [keep_y, got_y])
    back_y = permute(y, lambda z, core, col: (col ^ flip(z, cols), core, col))
    for d in range(1, cols):
        mine = mine + in_plane(chunks[d - 1], d).astype(F32)
    low_mine = mine.astype(BF16)
    low_mine, pair_out = lax.optimization_barrier((low_mine, pair_out))
    home = to_pair(pair_out)
    for d in range(1, cols):
        mine = mine + across(low_mine, d).astype(F32)
    low_mine = mine.astype(BF16)
    swapped = swap(low_mine)
    swapped, home = lax.optimization_barrier((swapped, home))
    own, *sends = call(
        functools.partial(row_sum_kernel, cols, area),
        "row_sum",
        0.1,
        [like(area, width)] + [like(area + 2 * chunk, width, dtype=BF16)] * (cols - 1),
        [gx, back_y, low_mine, swapped],
    )
    gets = [in_plane(sends[d - 1], d) for d in range(1, cols)]
    pair_grad, proj_grad, out_grad, pair_out = call(
        functools.partial(final_kernel, cols, area),
        "final",
        1.0,
        [like(area, width), like(*proj_weight.shape), like(width, width), like(area, width)],
        [own, pair, low_mine, swapped, home, *gets],
        [pltpu.VMEM((2, cols, chunk, width), F32)],
    )
    shape = pair_input.shape
    return pair_out.reshape(shape), pair_grad.reshape(shape), proj_grad, out_grad


def solution(mesh):
    return jax.shard_map(
        functools.partial(body, mesh.shape["row"], mesh.shape["col"]),
        mesh=mesh,
        in_specs=(P("row", "col", None), P(), P(), P(), P("row", "col", None)),
        out_specs=(P("row", "col", None), P("row", "col", None), P(), P()),
        check_vma=False,
    )
```

time: 71.9 us -> 64.1 us (0.89)
  the two profiles are of different devices: /device:TPU:29 before, /device:TPU:0 now
where the time goes in v2:
time: 64.1 us; the launch traced here: 63.8 us
  starting transfers between devices  25.7 us (40%)
  waiting for transfers between devices  21.6 us (34%)
  Pallas kernels  13.1 us (20%)
  local copies, waits for them, and re-layouts  2.53 us (4%)
  between operations  0.86 us (1%)
    ppermute x20, starting transfers between devices, permute(): return lax.ppermute(value, ('row', 'col'), pairs)  25.7 us
    ppermute x20, waiting for transfers between devices, permute(): return lax.ppermute(value, ('row', 'col'), pairs)  21.6 us
    pallas_call x13, Pallas kernels, call(): pl.pallas_call(kernel, out_shape=tuple(out_shape), in_specs=specs, out_sp...  13.1 us
    unnamed x14, local copies, waits for them, and re-layouts  2.53 us
  transfers between devices with their start and end apart: 20, of which 12 were waited for; matrix products, arithmetic and copies ran while one was open for 0% of the time, Pallas kernels for 7%

profile of v2, /device:TPU:0, one launch (start us, length us, event | category | flops | bytes accessed | tf_op | source)
XLA Modules:
  0.0 63.8 jit_solution(4751921900049258180)
XLA Ops:
  0.7 0.9 %copy-done.2 = f32[12,24,128]{2,1,0:T(8,128)S(1)} copy-done((f32[12,24,128]{2,1,0:T(8,128)S(1)}, f32[12,24,128]{2,1,0:T(8,128)}, u32[]{:S(2)}) %copy-start.2) | copy-done | bytes 147480
  1.8 4.0 %collective-permute-start.2 = (bf16[288,128]{1,0:T(8,128)(2,1)S(1)}, bf16[288,128]{1,0:T(8,128)(2,1)S(1)}, u32[]{:S(2)}, u32[]{:S(2)}) collective-permute-start(bf16[288,128]{1,0:T(8,128)(2,1)S(1)} %norm.1), channel_id=1, source_target_pairs={{0,3},{1,2},{2,1},{3,0},{4,7},{5,6},{6,5},{7,4},{8,11},{9,10},{10,... | collective-permute-start | bytes 221192 | tf_op jit(solution)/shard_map/ppermute | solution.py:366
  6.4 1.7 %collective-permute-done.2 = bf16[288,128]{1,0:T(8,128)(2,1)S(1)} collective-permute-done((bf16[288,128]{1,0:T(8,128)(2,1)S(1)}, bf16[288,128]{1,0:T(8,128)(2,1)S(1)}, u32[]{:S(2)}, u32[]{:S(2)}) %collective-permute-start.2) | collective-permute-done | bytes 73760 | tf_op jit(solution)/shard_map/ppermute | solution.py:366
  8.1 2.0 %collective-permute-done.1 = bf16[288,128]{1,0:T(8,128)(2,1)S(1)} collective-permute-done((bf16[288,128]{1,0:T(8,128)(2,1)S(1)}, bf16[288,128]{1,0:T(8,128)(2,1)S(1)}, u32[]{:S(2)}, u32[]{:S(2)}) %collective-permute-start.1) | collective-permute-done | bytes 73760 | tf_op jit(solution)/shard_map/ppermute | solution.py:366
  11.3 1.6 %collective-permute-start.3 = (f32[288,128]{1,0:T(8,128)}, f32[288,128]{1,0:T(8,128)S(1)}, u32[]{:S(2)}, u32[]{:S(2)}) collective-permute-start(f32[288,128]{1,0:T(8,128)} %bitcast.6), channel_id=1, source_target_pairs={{0,0},{1,1},{2,2},{3,3},{4,4},{5,5},{6,6},{7,7},{8,10},{9,11},{10,... | collective-permute-start | bytes 442376 | tf_op jit(solution)/shard_map/ppermute | solution.py:366
  14.5 1.3 %left.1 = (f32[4,12,24,128]{3,2,1,0:T(8,128)S(1)}, f32[4,12,24,128]{3,2,1,0:T(8,128)S(1)}, f32[4,12,24,128]{3,2,1,0:T(8,128)S(1)}) custom-call(s32[12]{0:T(128)S(1)} %copy-done.5, bf16[1152,128]{1,0:T(8,128)(2,1)S(1)} %pad_maximum_fusion.x_ref, bf16[128,640]{1,0:T(8,128)(2,1)S(1)} %copy-done), custom_call_target="tpu_custom_call" | custom-call | bytes 5166000 | tf_op jit(solution)/shard_map/left/pallas_call | solution.py:329
  15.9 1.4 %right_own.1 = (f32[2,4,12,24,128]{4,3,2,1,0:T(8,128)S(1)}, f32[2,4,12,24,128]{4,3,2,1,0:T(8,128)S(1)}, f32[2,4,12,24,128]{4,3,2,1,0:T(8,128)S(1)}) custom-call(s32[12]{0:T(128)S(1)} %copy-done.6, bf16[1152,128]{1,0:T(8,128)(2,1)S(1)} %collective-permute-done.4.x_ref.own_x_ref, bf16[128,640]{1,0:T(8,128)(2,1)S(1)} %copy-done.1), custom_call_target="tpu_custom_call" | custom-call | bytes 5166000 | tf_op jit(solution)/shard_map/right_own/pallas_call | solution.py:329
  17.5 1.3 %right_other.1 = (f32[2,4,12,24,128]{4,3,2,1,0:T(8,128)S(1)}, f32[2,4,12,24,128]{4,3,2,1,0:T(8,128)S(1)}, f32[2,4,12,24,128]{4,3,2,1,0:T(8,128)S(1)}) custom-call(s32[12]{0:T(128)S(1)} %copy-done.6, bf16[1152,128]{1,0:T(8,128)(2,1)S(1)} %collective-permute-done.5.x_ref.other_x_ref, ...), custom_call_target="tpu_custom_call", output_to_operand_aliasing={{0}: (3, {}), {1}: (4, {}), {2}: (5, {})} | custom-call | bytes 5166000 | tf_op jit(solution)/shard_map/right_other/pallas_call | solution.py:329
  18.9 2.5 %mix.1 = (f32[288,128]{1,0:T(8,128)S(1)}, bf16[288,128]{1,0:T(8,128)(2,1)S(1)}, f32[12,24,8,128]{3,2,1,0:T(8,128)S(1)}, f32[256,128]{1,0:T(8,128)S(1)}) custom-call(f32[4,12,24,128]{3,2,1,0:T(8,128)S(1)} %get-tuple-element.51.lv_ref, f32[2,4,12,24,128]{4,3,2,1,0:T(8,128)S(1)} %get-tuple-element.58.rv_ref, bf16[1152,128]{1,0:T(8,128)(2,1)S(1)} %pad_maximum_fusion.x_ref, ...), custom_call_target="tpu_custom_call" | custom-call | bytes 11070000 | tf_op jit(solution)/shard_map/mix/pallas_call | solution.py:329
  21.4 2.7 %grads.1 = (bf16[1152,256]{1,0:T(8,128)(2,1)S(1)}, bf16[2,1152,256]{2,1,0:T(8,128)(2,1)S(1)}) custom-call(f32[4,12,24,128]{3,2,1,0:T(8,128)S(1)} %get-tuple-element.51.lv_ref, f32[4,12,24,128]{3,2,1,0:T(8,128)S(1)} %get-tuple-element.52.la_ref, f32[4,12,24,128]{3,2,1,0:T(8,128)S(1)} %get-tuple-element.53.lb_ref, ...), custom_call_target="tpu_custom_call" | custom-call | bytes 11070000 | tf_op jit(solution)/shard_map/grads/pallas_call | solution.py:329
  26.1 1.1 %collective-permute-done.8.got_ref = bf16[384,128]{1,0:T(8,128)(2,1)S(1)} collective-permute-done((bf16[384,128]{1,0:T(8,128)(2,1)S(1)}, bf16[384,128]{1,0:T(8,128)(2,1)S(1)}, u32[]{:S(2)}, u32[]{:S(2)}) %collective-permute-start.8) | collective-permute-done | bytes 98336 | tf_op jit(solution)/shard_map/ppermute | solution.py:366
  27.2 5.9 %collective-permute-start.9 = (bf16[96,128]{1,0:T(8,128)(2,1)S(1)}, bf16[96,128]{1,0:T(8,128)(2,1)S(1)}, u32[]{:S(2)}, u32[]{:S(2)}) collective-permute-start(bf16[96,128]{1,0:T(8,128)(2,1)S(1)} %get-tuple-element.72), channel_id=1, source_target_pairs={{0,1},{1,0},{2,3},{3,2},{4,5},{5,4},{6,7},{7,6},{8,9},{9,8},{10,11... | collective-permute-start | bytes 73736 | tf_op jit(solution)/shard_map/ppermute | solution.py:366
  33.2 2.4 %collective-permute-start.10 = (bf16[96,128]{1,0:T(8,128)(2,1)S(1)}, bf16[96,128]{1,0:T(8,128)(2,1)S(1)}, u32[]{:S(2)}, u32[]{:S(2)}) collective-permute-start(bf16[96,128]{1,0:T(8,128)(2,1)S(1)} %get-tuple-element.73), channel_id=1, source_target_pairs={{0,2},{1,3},{2,0},{3,1},{4,6},{5,7},{6,4},{7,5},{8,10},{9,11},{10,... | collective-permute-start | bytes 73736 | tf_op jit(solution)/shard_map/ppermute | solution.py:366
  35.6 1.1 %back_own.1 = (f32[1152,128]{1,0:T(8,128)S(1)}, f32[1152,128]{1,0:T(8,128)S(1)}) custom-call(bf16[1152,256]{1,0:T(8,128)(2,1)S(1)} %get-tuple-element.63.dl_ref, bf16[2,1152,256]{2,1,0:T(8,128)(2,1)S(1)} %get-tuple-element.64.dr_ref, bf16[288,128]{1,0:T(8,128)(2,1)S(1)} %get-tuple-element.65.logit_ref, bf16[128,640]{1,0:T(8,128)(2,1)S(1)} %copy-done.1), custom_call_target="tpu_custom_call" | custom-call | bytes 2214000 | tf_op jit(solution)/shard_map/back_own/pallas_call | solution.py:329
  37.5 2.9 %collective-permute-done.11 = bf16[96,128]{1,0:T(8,128)(2,1)S(1)} collective-permute-done((bf16[96,128]{1,0:T(8,128)(2,1)S(1)}, bf16[96,128]{1,0:T(8,128)(2,1)S(1)}, u32[]{:S(2)}, u32[]{:S(2)}) %collective-permute-start.11) | collective-permute-done | bytes 24608 | tf_op jit(solution)/shard_map/ppermute | solution.py:366
  40.3 3.6 %collective-permute-start.14 = (bf16[96,128]{1,0:T(8,128)(2,1)S(1)}, bf16[96,128]{1,0:T(8,128)(2,1)S(1)}, u32[]{:S(2)}, u32[]{:S(2)}) collective-permute-start(bf16[96,128]{1,0:T(8,128)(2,1)S(1)} %fusion), channel_id=1, source_target_pairs={{0,24},{1,25},{2,26},{3,27},{4,28},{5,29},{6,30},{7,31},{8,16},{9,... | collective-permute-start | bytes 73736 | tf_op jit(solution)/shard_map/ppermute | solution.py:366
  46.2 5.3 %collective-permute-done.13 = bf16[96,128]{1,0:T(8,128)(2,1)S(1)} collective-permute-done((bf16[96,128]{1,0:T(8,128)(2,1)S(1)}, bf16[96,128]{1,0:T(8,128)(2,1)S(1)}, u32[]{:S(2)}, u32[]{:S(2)}) %collective-permute-start.13) | collective-permute-done | bytes 24608 | tf_op jit(solution)/shard_map/ppermute | solution.py:366
  51.6 1.2 %collective-permute-done.15.swapped_ref = bf16[96,128]{1,0:T(8,128)(2,1)S(1)} collective-permute-done((bf16[96,128]{1,0:T(8,128)(2,1)S(1)}, bf16[96,128]{1,0:T(8,128)(2,1)S(1)}, u32[]{:S(2)}, u32[]{:S(2)}) %collective-permute-start.15) | collective-permute-done | bytes 24608 | tf_op jit(solution)/shard_map/ppermute | solution.py:366
  53.3 2.2 %collective-permute-start.18 = (bf16[480,128]{1,0:T(8,128)(2,1)S(1)}, bf16[480,128]{1,0:T(8,128)(2,1)S(1)}, u32[]{:S(2)}, u32[]{:S(2)}) collective-permute-start(bf16[480,128]{1,0:T(8,128)(2,1)S(1)} %get-tuple-element.82), channel_id=1, source_target_pairs={{0,2},{1,3},{2,0},{3,1},{4,6},{5,7},{6,4},{7,5},{8,10},{9,11},{10,... | collective-permute-start | bytes 368648 | tf_op jit(solution)/shard_map/ppermute | solution.py:366
  55.5 1.3 %collective-permute-start.19 = (bf16[480,128]{1,0:T(8,128)(2,1)S(1)}, bf16[480,128]{1,0:T(8,128)(2,1)S(1)}, u32[]{:S(2)}, u32[]{:S(2)}) collective-permute-start(bf16[480,128]{1,0:T(8,128)(2,1)S(1)} %get-tuple-element.83), channel_id=1, source_target_pairs={{0,3},{1,2},{2,1},{3,0},{4,7},{5,6},{6,5},{7,4},{8,11},{9,10},{10,... | collective-permute-start | bytes 368648 | tf_op jit(solution)/shard_map/ppermute | solution.py:366
  56.8 2.0 %collective-permute-done.17.rest_0_ = bf16[480,128]{1,0:T(8,128)(2,1)S(1)} collective-permute-done((bf16[480,128]{1,0:T(8,128)(2,1)S(1)}, bf16[480,128]{1,0:T(8,128)(2,1)S(1)}, u32[]{:S(2)}, u32[]{:S(2)}) %collective-permute-start.17) | collective-permute-done | bytes 122912 | tf_op jit(solution)/shard_map/ppermute | solution.py:366
  58.8 2.1 %collective-permute-done.18.rest_1_ = bf16[480,128]{1,0:T(8,128)(2,1)S(1)} collective-permute-done((bf16[480,128]{1,0:T(8,128)(2,1)S(1)}, bf16[480,128]{1,0:T(8,128)(2,1)S(1)}, u32[]{:S(2)}, u32[]{:S(2)}) %collective-permute-start.18) | collective-permute-done | bytes 122912 | tf_op jit(solution)/shard_map/ppermute | solution.py:366
  60.9 1.8 %collective-permute-done.19.rest_2_ = bf16[480,128]{1,0:T(8,128)(2,1)S(1)} collective-permute-done((bf16[480,128]{1,0:T(8,128)(2,1)S(1)}, bf16[480,128]{1,0:T(8,128)(2,1)S(1)}, u32[]{:S(2)}, u32[]{:S(2)}) %collective-permute-start.19) | collective-permute-done | bytes 122912 | tf_op jit(solution)/shard_map/ppermute | solution.py:366
  62.8 1.1 %final.1 = (f32[288,128]{1,0:T(8,128)}, f32[128,640]{1,0:T(8,128)}, f32[128,128]{1,0:T(8,128)}, f32[288,128]{1,0:T(8,128)}) custom-call(f32[288,128]{1,0:T(8,128)S(1)} %get-tuple-element.79.own_ref, f32[288,128]{1,0:T(8,128)S(1)} %bitcast.5, bf16[96,128]{1,0:T(8,128)(2,1)S(1)} %add_convert_fusion.chunk_ref, ...), custom_call_target="tpu_custom_call" | custom-call | bytes 3690000 | tf_op jit(solution)/shard_map/final/pallas_call | solution.py:329
  (46 shorter events, 9.5 us)
Async XLA Ops:
  0.6 15.3 %copy-start.1 = (bf16[128,640]{1,0:T(8,128)(2,1)S(1)}, bf16[128,640]{1,0:T(8,128)(2,1)}, u32[]{:S(2)}) copy-start(bf16[128,640]{1,0:T(8,128)(2,1)} %w_ref.11) | copy-start | bytes 491524
  1.6 14.3 %copy-start.6 = (s32[12]{0:T(128)S(1)}, s32[12]{0:T(128)}, u32[]{:S(2)}) copy-start(s32[12]{0:T(128)} %valid_ref.5) | copy-start | bytes 148
  1.8 6.3 %collective-permute-start.2 = (bf16[288,128]{1,0:T(8,128)(2,1)S(1)}, bf16[288,128]{1,0:T(8,128)(2,1)S(1)}, u32[]{:S(2)}, u32[]{:S(2)}) collective-permute-start(bf16[288,128]{1,0:T(8,128)(2,1)S(1)} %norm.1), channel_id=1, source_target_pairs={{0,3},{1,2},{2,1},{3,0},{4,7},{5,6},{6,5},{7,4},{8,11},{9,10},{10,... | collective-permute-start | bytes 221192 | tf_op jit(solution)/shard_map/ppermute | solution.py:366
  5.8 4.4 %collective-permute-start.1 = (bf16[288,128]{1,0:T(8,128)(2,1)S(1)}, bf16[288,128]{1,0:T(8,128)(2,1)S(1)}, u32[]{:S(2)}, u32[]{:S(2)}) collective-permute-start(bf16[288,128]{1,0:T(8,128)(2,1)S(1)} %norm.1), channel_id=1, source_target_pairs={{0,2},{1,3},{2,0},{3,1},{4,6},{5,7},{6,4},{7,5},{8,10},{9,11},{10,... | collective-permute-start | bytes 221192 | tf_op jit(solution)/shard_map/ppermute | solution.py:366
  6.3 4.4 %collective-permute-start = (bf16[288,128]{1,0:T(8,128)(2,1)S(1)}, bf16[288,128]{1,0:T(8,128)(2,1)S(1)}, u32[]{:S(2)}, u32[]{:S(2)}) collective-permute-start(bf16[288,128]{1,0:T(8,128)(2,1)S(1)} %norm.1), channel_id=1, source_target_pairs={{0,1},{1,0},{2,3},{3,2},{4,5},{5,4},{6,7},{7,6},{8,9},{9,8},{10,11... | collective-permute-start | bytes 221192 | tf_op jit(solution)/shard_map/ppermute | solution.py:366
  10.6 5.2 %collective-permute-start.4 = (bf16[1152,128]{1,0:T(8,128)(2,1)S(1)}, bf16[1152,128]{1,0:T(8,128)(2,1)S(1)}, u32[]{:S(2)}, u32[]{:S(2)}) collective-permute-start(bf16[1152,128]{1,0:T(8,128)(2,1)S(1)} %pad_maximum_fusion.x_ref), channel_id=1, source_target_pairs={{0,0},{1,17},{2,10},{3,27},{4,4},{5,21},{6,14},{7,31},{8,16},{9,1}... | collective-permute-start | bytes 884744 | tf_op jit(solution)/shard_map/ppermute | solution.py:366
  11.3 4.5 %collective-permute-start.3 = (f32[288,128]{1,0:T(8,128)}, f32[288,128]{1,0:T(8,128)S(1)}, u32[]{:S(2)}, u32[]{:S(2)}) collective-permute-start(f32[288,128]{1,0:T(8,128)} %bitcast.6), channel_id=1, source_target_pairs={{0,0},{1,1},{2,2},{3,3},{4,4},{5,5},{6,6},{7,7},{8,10},{9,11},{10,... | collective-permute-start | bytes 442376 | tf_op jit(solution)/shard_map/ppermute | solution.py:366
  15.8 1.6 %collective-permute-start.5 = (bf16[1152,128]{1,0:T(8,128)(2,1)S(1)}, bf16[1152,128]{1,0:T(8,128)(2,1)S(1)}, u32[]{:S(2)}, u32[]{:S(2)}) collective-permute-start(bf16[1152,128]{1,0:T(8,128)(2,1)S(1)} %collective-permute-done.4.x_ref.own_x_ref), channel_id=1, source_target_pairs={{0,4},{1,5},{2,6},{3,7},{4,0},{5,1},{6,2},{7,3},{8,12},{9,13},{10,... | collective-permute-start | bytes 884744 | tf_op jit(solution)/shard_map/ppermute | solution.py:366
  17.5 1.4 %copy-start.4 = (bf16[128,128]{1,0:T(8,128)(2,1)S(1)}, bf16[128,128]{1,0:T(8,128)(2,1)}, u32[]{:S(2)}) copy-start(bf16[128,128]{1,0:T(8,128)(2,1)} %wout_ref.1) | copy-start | bytes 98308
  24.9 11.8 %collective-permute-start.6 = (bf16[1152,128]{1,0:T(8,128)(2,1)S(1)}, bf16[1152,128]{1,0:T(8,128)(2,1)S(1)}, u32[]{:S(2)}, u32[]{:S(2)}) collective-permute-start(bf16[1152,128]{1,0:T(8,128)(2,1)S(1)} %back_other.1), channel_id=1, source_target_pairs={{0,4},{1,5},{2,6},{3,7},{4,0},{5,1},{6,2},{7,3},{8,12},{9,13},{10,... | collective-permute-start | bytes 884744 | tf_op jit(solution)/shard_map/ppermute | solution.py:366
  25.8 1.4 %collective-permute-start.8 = (bf16[384,128]{1,0:T(8,128)(2,1)S(1)}, bf16[384,128]{1,0:T(8,128)(2,1)S(1)}, u32[]{:S(2)}, u32[]{:S(2)}) collective-permute-start(bf16[384,128]{1,0:T(8,128)(2,1)S(1)} %get-tuple-element.70), channel_id=1, source_target_pairs={{0,4},{1,5},{2,6},{3,7},{4,0},{5,1},{6,2},{7,3},{8,12},{9,13},{10,... | collective-permute-start | bytes 294920 | tf_op jit(solution)/shard_map/ppermute | solution.py:366
  27.2 10.2 %collective-permute-start.9 = (bf16[96,128]{1,0:T(8,128)(2,1)S(1)}, bf16[96,128]{1,0:T(8,128)(2,1)S(1)}, u32[]{:S(2)}, u32[]{:S(2)}) collective-permute-start(bf16[96,128]{1,0:T(8,128)(2,1)S(1)} %get-tuple-element.72), channel_id=1, source_target_pairs={{0,1},{1,0},{2,3},{3,2},{4,5},{5,4},{6,7},{7,6},{8,9},{9,8},{10,11... | collective-permute-start | bytes 73736 | tf_op jit(solution)/shard_map/ppermute | solution.py:366
  33.2 4.3 %collective-permute-start.10 = (bf16[96,128]{1,0:T(8,128)(2,1)S(1)}, bf16[96,128]{1,0:T(8,128)(2,1)S(1)}, u32[]{:S(2)}, u32[]{:S(2)}) collective-permute-start(bf16[96,128]{1,0:T(8,128)(2,1)S(1)} %get-tuple-element.73), channel_id=1, source_target_pairs={{0,2},{1,3},{2,0},{3,1},{4,6},{5,7},{6,4},{7,5},{8,10},{9,11},{10,... | collective-permute-start | bytes 73736 | tf_op jit(solution)/shard_map/ppermute | solution.py:366
  35.6 4.7 %collective-permute-start.11 = (bf16[96,128]{1,0:T(8,128)(2,1)S(1)}, bf16[96,128]{1,0:T(8,128)(2,1)S(1)}, u32[]{:S(2)}, u32[]{:S(2)}) collective-permute-start(bf16[96,128]{1,0:T(8,128)(2,1)S(1)} %get-tuple-element.74), channel_id=1, source_target_pairs={{0,3},{1,2},{2,1},{3,0},{4,7},{5,6},{6,5},{7,4},{8,11},{9,10},{10,... | collective-permute-start | bytes 73736 | tf_op jit(solution)/shard_map/ppermute | solution.py:366
  36.7 26.1 %copy-start.3 = (f32[12,24,128]{2,1,0:T(8,128)S(1)}, f32[12,24,128]{2,1,0:T(8,128)}, u32[]{:S(2)}) copy-start(f32[12,24,128]{2,1,0:T(8,128)} %param.5) | copy-start | bytes 442372
  36.8 16.0 %collective-permute-start.7 = (bf16[1152,128]{1,0:T(8,128)(2,1)S(1)}, bf16[1152,128]{1,0:T(8,128)(2,1)S(1)}, u32[]{:S(2)}, u32[]{:S(2)}) collective-permute-start(bf16[1152,128]{1,0:T(8,128)(2,1)S(1)} %core_sum.1), channel_id=1, source_target_pairs={{0,0},{1,9},{2,18},{3,27},{4,4},{5,13},{6,22},{7,31},{8,16},{9,25}... | collective-permute-start | bytes 884744 | tf_op jit(solution)/shard_map/ppermute | solution.py:366
  40.3 5.8 %collective-permute-start.14 = (bf16[96,128]{1,0:T(8,128)(2,1)S(1)}, bf16[96,128]{1,0:T(8,128)(2,1)S(1)}, u32[]{:S(2)}, u32[]{:S(2)}) collective-permute-start(bf16[96,128]{1,0:T(8,128)(2,1)S(1)} %fusion), channel_id=1, source_target_pairs={{0,24},{1,25},{2,26},{3,27},{4,28},{5,29},{6,30},{7,31},{8,16},{9,... | collective-permute-start | bytes 73736 | tf_op jit(solution)/shard_map/ppermute | solution.py:366
  43.9 7.5 %collective-permute-start.13 = (bf16[96,128]{1,0:T(8,128)(2,1)S(1)}, bf16[96,128]{1,0:T(8,128)(2,1)S(1)}, u32[]{:S(2)}, u32[]{:S(2)}) collective-permute-start(bf16[96,128]{1,0:T(8,128)(2,1)S(1)} %fusion), channel_id=1, source_target_pairs={{0,16},{1,17},{2,18},{3,19},{4,20},{5,21},{6,22},{7,23},{8,24},{9,... | collective-permute-start | bytes 73736 | tf_op jit(solution)/shard_map/ppermute | solution.py:366
  43.9 7.5 %collective-permute-start.12 = (bf16[96,128]{1,0:T(8,128)(2,1)S(1)}, bf16[96,128]{1,0:T(8,128)(2,1)S(1)}, u32[]{:S(2)}, u32[]{:S(2)}) collective-permute-start(bf16[96,128]{1,0:T(8,128)(2,1)S(1)} %fusion), channel_id=1, source_target_pairs={{0,8},{1,9},{2,10},{3,11},{4,12},{5,13},{6,14},{7,15},{8,0},{9,1},... | collective-permute-start | bytes 73736 | tf_op jit(solution)/shard_map/ppermute | solution.py:366
  44.8 8.0 %collective-permute-start.16 = (f32[288,128]{1,0:T(8,128)S(1)}, f32[288,128]{1,0:T(8,128)S(1)}, u32[]{:S(2)}, u32[]{:S(2)}) collective-permute-start(f32[288,128]{1,0:T(8,128)S(1)} %get-tuple-element.77), channel_id=1, source_target_pairs={{0,0},{1,1},{2,2},{3,3},{4,4},{5,5},{6,6},{7,7},{8,10},{9,11},{10,... | collective-permute-start | bytes 442376 | tf_op jit(solution)/shard_map/ppermute | solution.py:366
  51.5 1.3 %collective-permute-start.15 = (bf16[96,128]{1,0:T(8,128)(2,1)S(1)}, bf16[96,128]{1,0:T(8,128)(2,1)S(1)}, u32[]{:S(2)}, u32[]{:S(2)}) collective-permute-start(bf16[96,128]{1,0:T(8,128)(2,1)S(1)} %add_convert_fusion.chunk_ref), channel_id=1, source_target_pairs={{0,4},{1,5},{2,6},{3,7},{4,0},{5,1},{6,2},{7,3},{8,12},{9,13},{10,... | collective-permute-start | bytes 73736 | tf_op jit(solution)/shard_map/ppermute | solution.py:366
  52.8 5.9 %collective-permute-start.17 = (bf16[480,128]{1,0:T(8,128)(2,1)S(1)}, bf16[480,128]{1,0:T(8,128)(2,1)S(1)}, u32[]{:S(2)}, u32[]{:S(2)}) collective-permute-start(bf16[480,128]{1,0:T(8,128)(2,1)S(1)} %get-tuple-element.81), channel_id=1, source_target_pairs={{0,1},{1,0},{2,3},{3,2},{4,5},{5,4},{6,7},{7,6},{8,9},{9,8},{10,11... | collective-permute-start | bytes 368648 | tf_op jit(solution)/shard_map/ppermute | solution.py:366
  53.3 7.6 %collective-permute-start.18 = (bf16[480,128]{1,0:T(8,128)(2,1)S(1)}, bf16[480,128]{1,0:T(8,128)(2,1)S(1)}, u32[]{:S(2)}, u32[]{:S(2)}) collective-permute-start(bf16[480,128]{1,0:T(8,128)(2,1)S(1)} %get-tuple-element.82), channel_id=1, source_target_pairs={{0,2},{1,3},{2,0},{3,1},{4,6},{5,7},{6,4},{7,5},{8,10},{9,11},{10,... | collective-permute-start | bytes 368648 | tf_op jit(solution)/shard_map/ppermute | solution.py:366
  55.5 7.3 %collective-permute-start.19 = (bf16[480,128]{1,0:T(8,128)(2,1)S(1)}, bf16[480,128]{1,0:T(8,128)(2,1)S(1)}, u32[]{:S(2)}, u32[]{:S(2)}) collective-permute-start(bf16[480,128]{1,0:T(8,128)(2,1)S(1)} %get-tuple-element.83), channel_id=1, source_target_pairs={{0,3},{1,2},{2,1},{3,0},{4,7},{5,6},{6,5},{7,4},{8,11},{9,10},{10,... | collective-permute-start | bytes 368648 | tf_op jit(solution)/shard_map/ppermute | solution.py:366
  (3 other events, 2.5 us)

commit v3 on v2

--- a/solution.py
+++ b/solution.py
@@ -83,24 +83,28 @@
         b_ref[index + (i,)] = kept
 
 
-def project_kernel(side, cols, sizes, valid_ref, x_ref, w_ref, *refs):
+def project_kernel(side, cols, sizes, valid_ref, x_ref, home_ref, w_ref, *refs):
     row_len, col_len, width = sizes
     area = row_len * col_len
     row, core, col, step, pair = place(cols)
     half = core if side < 2 else 1 - core
+    row_here = row
     if side:
         row = 2 * pair + half
     base = 2 * width if side else 0
     outs = refs[-3:]
 
-    def one(d, carry):
-        rows = pl.ds(pl.multiple_of(d * area, area), area)
-        projected = dot(x_ref[rows, :], w_ref[:, base : base + 2 * width])
+    def one(d):
+        rows = rows_of(d, area)
+        used = x_ref[rows, :]
+        if side:
+            used = jnp.where(pair == row_here >> 1, home_ref[rows, :], used)
+            refs[-4][rows, :] = used
+        projected = dot(used, w_ref[:, base : base + 2 * width])
         index = (half, d) if side else (d,)
         project_block(projected, valid_ref, row, col ^ d, sizes, index, *outs)
-        return carry
-
-    lax.fori_loop(0, cols, one, 0)
+
+    by_fours(cols, one)
 
 
 def tile(g):
@@ -108,28 +112,37 @@
 
 
 def rows_of(d, area):
+    if isinstance(d, int):
+        return pl.ds(d * area, area)
     return pl.ds(pl.multiple_of(d * area, area), area)
 
 
-def mix_kernel(
-    cols,
-    sizes,
-    lv_ref,
-    rv_ref,
-    x_ref,
-    cot_ref,
-    w_ref,
-    wout_ref,
-    out_ref,
-    logit_ref,
-    wide_ref,
-    wg_ref,
-    mixed_ref,
-    grad_ref,
-):
+def by_fours(count, one):
+    def four(q, carry):
+        for n in range(4):
+            one(4 * q + n)
+        return carry
+
+    if count == 4:
+        four(0, 0)
+    else:
+        lax.fori_loop(0, count // 4, four, 0)
+
+
+def gate_kernel(cols, area, width, x_ref, cot_ref, own_cot_ref, w_ref, wout_ref, gate_ref, cot_out_ref, grad_ref, low_ref):
+    row, core, col, step, pair = place(cols)
+    out_gate = sigmoid(dot(x_ref[rows_of(step, area), :], w_ref[:, 4 * width :]))
+    gated = jnp.where(step == 0, own_cot_ref[...], cot_ref[...]) * out_gate
+    low = gated.astype(BF16)
+    gate_ref[...] = out_gate
+    cot_out_ref[...] = gated * (1.0 - out_gate)
+    low_ref[...] = low
+    grad_ref[...] = dot_nt(low, wout_ref[...])
+
+
+def mix_kernel(cols, sizes, lv_ref, rv_ref, back_ref, low_ref, wide_ref, mixed_ref, grad_ref):
     row_len, col_len, width = sizes
     area = row_len * col_len
-    row, core, col, step, pair = place(cols)
     groups = col_len // SEG
     zero = jnp.zeros((SEG, width), F32)
 
@@ -156,18 +169,8 @@
     lax.fori_loop(0, row_len // 2, mix_rows, 0)
 
     mixed_norm, mixed_scale = layer_norm(mixed_ref[...].reshape(area, width))
-    mixed_low = mixed_norm.astype(BF16)
-    update = dot(mixed_low, wout_ref[...])
-    home = x_ref[rows_of(step, area), :]
-    out_gate = sigmoid(dot(home, w_ref[:, 4 * width :]))
-    out_ref[...] = out_gate * update
-    gated_cot = cot_ref[...] * out_gate
-    grad_logit = (gated_cot * update * (1.0 - out_gate)).astype(BF16)
-    grad_update = gated_cot.astype(BF16)
-    logit_ref[...] = grad_logit
-    wg_ref[:width, :] = dot_tn(home, grad_logit)
-    wg_ref[width:, :] = dot_tn(mixed_low, grad_update)
-    grad_mixed = norm_back(dot_nt(grad_update, wout_ref[...]), mixed_norm, mixed_scale)
+    low_ref[...] = mixed_norm.astype(BF16)
+    grad_mixed = norm_back(back_ref[...], mixed_norm, mixed_scale)
     grad_ref[...] = grad_mixed.astype(BF16).astype(F32).reshape(row_len, col_len, width)
 
     def widen(i, carry):
@@ -238,42 +241,62 @@
 
 
 def weight_sums_kernel(
-    width, x_ref, own_x_ref, other_x_ref, dl_ref, dr_ref, wg_ref, send_ref, keep_ref, sum_ref
+    cols,
+    area,
+    width,
+    x_ref,
+    own_x_ref,
+    other_x_ref,
+    dl_ref,
+    dr_ref,
+    low_ref,
+    gate_ref,
+    cot_ref,
+    update_low_ref,
+    wout_ref,
+    send_ref,
+    keep_ref,
+    out_ref,
+    logit_ref,
+    sum_ref,
 ):
-    core = lax.axis_index("row") & 1
+    row, core, col, step, pair = place(cols)
+    update = dot(low_ref[...], wout_ref[...])
+    out_ref[...] = gate_ref[...] * update
+    grad_logit = (cot_ref[...] * update).astype(BF16)
+    logit_ref[...] = grad_logit
     left_w = dot_tn(x_ref[...], dl_ref[...])
     right_w = dot_tn(own_x_ref[...], dr_ref[core]) + dot_tn(other_x_ref[...], dr_ref[1 - core])
     sum_ref[0, :width, :] = left_w[:, :width]
     sum_ref[0, width : 2 * width, :] = left_w[:, width:]
     sum_ref[0, 2 * width :, :] = right_w[:, :width]
     sum_ref[1, :width, :] = right_w[:, width:]
-    sum_ref[1, width:, :] = wg_ref[...]
+    sum_ref[1, width : 2 * width, :] = dot_tn(x_ref[rows_of(step, area), :], grad_logit)
+    sum_ref[1, 2 * width :, :] = dot_tn(low_ref[...], update_low_ref[...])
     send_ref[...] = sum_ref[1 - core].astype(BF16)
     keep_ref[...] = sum_ref[core]
 
 
-def back_other_kernel(cols, area, width, dr_ref, w_ref, send_ref):
+def back_right_kernel(cols, area, width, other, dr_ref, w_ref, part_ref):
     core = lax.axis_index("row") & 1
-
-    def back(d, carry):
+    half = 1 - core if other else core
+
+    def back(d):
         rows = rows_of(d, area)
-        part = dot_nt(dr_ref[1 - core, rows, :], w_ref[:, 2 * width : 4 * width])
-        send_ref[rows, :] = part.astype(BF16)
-        return carry
-
-    lax.fori_loop(0, cols, back, 0)
-
-
-def back_own_kernel(cols, area, width, dl_ref, dr_ref, logit_ref, w_ref, keep_ref, gx_ref):
+        part = dot_nt(dr_ref[half, rows, :], w_ref[:, 2 * width : 4 * width])
+        part_ref[rows, :] = part.astype(part_ref.dtype)
+
+    by_fours(cols, back)
+
+
+def back_left_kernel(cols, area, width, dl_ref, logit_ref, w_ref, gx_ref):
     row, core, col, step, pair = place(cols)
 
-    def back(d, carry):
+    def back(d):
         rows = rows_of(d, area)
-        keep_ref[rows, :] = dot_nt(dr_ref[core, rows, :], w_ref[:, 2 * width : 4 * width])
         gx_ref[rows, :] = dot_nt(dl_ref[rows, :], w_ref[:, : 2 * width])
-        return carry
-
-    lax.fori_loop(0, cols, back, 0)
+
+    by_fours(cols, back)
     gx_ref[rows_of(step, area), :] += dot_nt(logit_ref[...], w_ref[:, 4 * width :])
 
 
@@ -291,22 +314,30 @@
         chunk_refs[d - 1][...] = sum_ref[col ^ d].astype(BF16)
 
 
-def row_sum_kernel(cols, area, gx_ref, got_ref, chunk_ref, swapped_ref, own_ref, *send_refs):
+def row_sum_kernel(cols, area, gx_ref, got_ref, y_ref, chunk_ref, swapped_ref, own_ref, *send_refs):
     chunk = chunk_ref.shape[0]
-    own_ref[...] = gx_ref[:area, :] + got_ref[:area, :].astype(F32)
+    row, core, col, step, pair = place(cols)
+    stays = pair == row >> 1
+
+    def total(d):
+        rows = slice(d * area, (d + 1) * area)
+        return gx_ref[rows, :] + jnp.where(stays, y_ref[rows, :], got_ref[rows, :]).astype(F32)
+
+    own_ref[...] = total(0)
     for d in range(1, cols):
-        rows = slice(d * area, (d + 1) * area)
-        send_refs[d - 1][:area, :] = (gx_ref[rows, :] + got_ref[rows, :].astype(F32)).astype(BF16)
+        send_refs[d - 1][:area, :] = total(d).astype(BF16)
         send_refs[d - 1][area : area + chunk, :] = chunk_ref[...]
         send_refs[d - 1][area + chunk :, :] = swapped_ref[...]
 
 
-def final_kernel(cols, area, own_ref, pair_ref, chunk_ref, swapped_ref, home_ref, *rest):
+def final_kernel(
+    cols, area, own_ref, pair_ref, chunk_ref, swapped_ref, home_ref, own_out_ref, *rest
+):
     got_refs = rest[: cols - 1]
     grad_ref, proj_ref, out_ref, home_out_ref, order_ref = rest[cols - 1 :]
     chunk, width = chunk_ref.shape
-    col, core = lax.axis_index("col"), lax.axis_index("row") & 1
-    home_out_ref[...] = home_ref[...]
+    row, core, col, step, pair = place(cols)
+    home_out_ref[...] = jnp.where(step == 0, own_out_ref[...], home_ref[...])
     total = own_ref[...]
     order_ref[core, col] = chunk_ref[...].astype(F32)
     order_ref[1 - core, col] = swapped_ref[...].astype(F32)
@@ -362,6 +393,8 @@
             for core in range(2):
                 for col in range(cols):
                     to = target(z, core, col)
+                    if to == (z, core, col):
+                        to = (z, 1 - core, col)
                     pairs.append(((2 * z + core) * cols + col, (2 * to[0] + to[1]) * cols + to[2]))
         return lax.ppermute(value, ("row", "col"), pairs)
 
@@ -387,49 +420,51 @@
     (low,) = call(norm_kernel, "norm", 0.3, [like(area, width, dtype=BF16)], [pair])
     blocks = [low] + [in_plane(low, d) for d in range(1, cols)]
     x = jnp.concatenate(blocks, axis=0)
-    own_x = permute(x, lambda z, core, col: (flip(col ^ z, cols), core, col))
+    got_x = permute(x, lambda z, core, col: (flip(col ^ z, cols), core, col))
     cot, x = lax.optimization_barrier((cot, x))
-    cot = to_pair(cot)
+    got_cot = to_pair(cot)
     left = call(
         functools.partial(project_kernel, 0, cols, sizes),
         "left",
-        1.4,
+        0.9,
         [like(cols, row_len, col_len, width)] * 3,
-        [block_valid, x, proj_weight],
+        [block_valid, x, x, proj_weight],
         smem=1,
     )
-    left, cot, own_x = lax.optimization_barrier((left, cot, own_x))
-    other_x = swap(own_x)
-    right_shape = [like(2, cols, row_len, col_len, width)] * 3
-    right = call(
+    out_gate, cot, back, update_low = call(
+        functools.partial(gate_kernel, cols, area, width),
+        "gate",
+        0.3,
+        [like(area, width)] * 3 + [like(area, width, dtype=BF16)],
+        [x, got_cot, cot, proj_weight, out_weight],
+    )
+    left, back, got_x = lax.optimization_barrier((left, back, got_x))
+    swapped_x = swap(got_x)
+    right_shape = [like(tall, width, dtype=BF16)] + [like(2, cols, row_len, col_len, width)] * 3
+    own_x, *right = call(
         functools.partial(project_kernel, 1, cols, sizes),
         "right_own",
-        1.4,
+        0.9,
         right_shape,
-        [block_valid, own_x, proj_weight],
+        [block_valid, got_x, x, proj_weight],
         smem=1,
     )
-    right = call(
+    other_x, *right = call(
         functools.partial(project_kernel, 2, cols, sizes),
         "right_other",
-        1.4,
+        0.9,
         right_shape,
-        [block_valid, other_x, proj_weight, *right],
+        [block_valid, swapped_x, got_x, proj_weight, *right],
         smem=1,
-        aliases={3: 0, 4: 1, 5: 2},
+        aliases={4: 1, 5: 2, 6: 3},
     )
     flat = pltpu.VMEM((row_len, col_len, width), F32)
-    pair_out, grad_logit, wide, wg = call(
+    mixed_low, wide = call(
         functools.partial(mix_kernel, cols, sizes),
         "mix",
-        3.0,
-        [
-            like(area, width),
-            like(area, width, dtype=BF16),
-            like(row_len, col_len, SEG, width),
-            like(2 * width, width),
-        ],
-        [left[0], right[0], x, cot, proj_weight, out_weight],
+        1.8,
+        [like(area, width, dtype=BF16), like(row_len, col_len, SEG, width)],
+        [left[0], right[0], back],
         [flat, flat],
     )
     dl, dr = call(
@@ -439,30 +474,29 @@
         [like(tall, 2 * width, dtype=BF16), like(2, tall, 2 * width, dtype=BF16)],
         [*left, *right, wide],
     )
-    send_w, keep_w = call(
-        functools.partial(weight_sums_kernel, width),
+    send_w, keep_w, pair_out, grad_logit = call(
+        functools.partial(weight_sums_kernel, cols, area, width),
         "weight_sums",
-        1.0,
-        [like(half, width, dtype=BF16), like(half, width)],
-        [x, own_x, other_x, dl, dr, wg],
+        0.6,
+        [
+            like(half, width, dtype=BF16),
+            like(half, width),
+            like(area, width),
+            like(area, width, dtype=BF16),
+        ],
+        [x, own_x, other_x, dl, dr, mixed_low, out_gate, cot, update_low, out_weight],
         [pltpu.VMEM((2, half, width), F32)],
     )
     got_w = swap(send_w)
+    dr, send_w = lax.optimization_barrier((dr, send_w))
     (send_y,) = call(
-        functools.partial(back_other_kernel, cols, area, width),
+        functools.partial(back_right_kernel, cols, area, width, True),
         "back_other",
-        0.4,
+        0.3,
         [like(tall, width, dtype=BF16)],
         [dr, proj_weight],
     )
     got_y = swap(send_y)
-    keep_y, gx = call(
-        functools.partial(back_own_kernel, cols, area, width),
-        "back_own",
-        0.6,
-        [like(tall, width)] * 2,
-        [dl, dr, grad_logit, proj_weight],
-    )
     mine, *chunks = call(
         functools.partial(chunks_kernel, cols),
         "chunks",
@@ -471,12 +505,27 @@
         [keep_w, got_w],
         [pltpu.VMEM((cols, chunk, width), F32)],
     )
+    dr, dl, mine = lax.optimization_barrier((dr, dl, mine))
+    (keep_y,) = call(
+        functools.partial(back_right_kernel, cols, area, width, False),
+        "back_own",
+        0.3,
+        [like(tall, width)],
+        [dr, proj_weight],
+    )
     (y,) = call(core_sum_kernel, "core_sum", 0.1, [like(tall, width, dtype=BF16)], [keep_y, got_y])
     back_y = permute(y, lambda z, core, col: (col ^ flip(z, cols), core, col))
+    (gx,) = call(
+        functools.partial(back_left_kernel, cols, area, width),
+        "back_left",
+        0.3,
+        [like(tall, width)],
+        [dl, grad_logit, proj_weight],
+    )
     for d in range(1, cols):
         mine = mine + in_plane(chunks[d - 1], d).astype(F32)
     low_mine = mine.astype(BF16)
-    low_mine, pair_out = lax.optimization_barrier((low_mine, pair_out))
+    low_mine, pair_out, gx = lax.optimization_barrier((low_mine, pair_out, gx))
     home = to_pair(pair_out)
     for d in range(1, cols):
         mine = mine + across(low_mine, d).astype(F32)
@@ -488,7 +537,7 @@
         "row_sum",
         0.1,
         [like(area, width)] + [like(area + 2 * chunk, width, dtype=BF16)] * (cols - 1),
-        [gx, back_y, low_mine, swapped],
+        [gx, back_y, y, low_mine, swapped],
     )
     gets = [in_plane(sends[d - 1], d) for d in range(1, cols)]
     pair_grad, proj_grad, out_grad, pair_out = call(
@@ -496,7 +545,7 @@
         "final",
         1.0,
         [like(area, width), like(*proj_weight.shape), like(width, width), like(area, width)],
-        [own, pair, low_mine, swapped, home, *gets],
+        [own, pair, low_mine, swapped, home, pair_out, *gets],
         [pltpu.VMEM((2, cols, chunk, width), F32)],
     )
     shape = pair_input.shape

time: 64.1 us -> 57.7 us (0.900)
  starting transfers between devices: 25.7 us -> 22.3 us
  Pallas kernels: 13.1 us -> 11 us
  waiting for transfers between devices: 21.6 us -> 20.7 us
    ppermute x20, starting transfers between devices: 25.7 us -> 22.3 us  [permute(): return lax.ppermute(value, ('row', 'col'), pairs)]
    pallas_call x13 -> x15, Pallas kernels: 13.1 us -> 11 us  [call(): pl.pallas_call(kernel, out_shape=tuple(out_shape), in_specs=specs, out_sp...]
    ppermute x20, waiting for transfers between devices: 21.6 us -> 20.7 us  [permute(): return lax.ppermute(value, ('row', 'col'), pairs)]
    unnamed x14 -> x16, local copies, waits for them, and re-layouts: 2.53 us -> 2.54 us
  transfers between devices with their start and end apart: 20 -> 20, of which waited for: 12 -> 13; matrix products, arithmetic and copies ran while one was open for 0% -> 0% of each run, Pallas kernels for 7% -> 5%
where the time goes in v3:
time: 57.7 us; the launch traced here: 57.5 us
  starting transfers between devices  22.3 us (39%)
  waiting for transfers between devices  20.7 us (36%)
  Pallas kernels  11 us (19%)
  local copies, waits for them, and re-layouts  2.54 us (4%)
  between operations  0.86 us (1%)
    ppermute x20, starting transfers between devices, permute(): return lax.ppermute(value, ('row', 'col'), pairs)  22.3 us
    ppermute x20, waiting for transfers between devices, permute(): return lax.ppermute(value, ('row', 'col'), pairs)  20.7 us
    pallas_call x15, Pallas kernels, call(): pl.pallas_call(kernel, out_shape=tuple(out_shape), in_specs=specs, out_sp...  11 us
    unnamed x16, local copies, waits for them, and re-layouts  2.54 us
  transfers between devices with their start and end apart: 20, of which 13 were waited for; matrix products, arithmetic and copies ran while one was open for 0% of the time, Pallas kernels for 5%

profile of v3, /device:TPU:0, one launch (start us, length us, event | category | flops | bytes accessed | tf_op | source)
XLA Modules:
  0.0 57.5 jit_solution(10912370564319597634)
XLA Ops:
  0.7 0.9 %copy-done.2 = f32[12,24,128]{2,1,0:T(8,128)S(1)} copy-done((f32[12,24,128]{2,1,0:T(8,128)S(1)}, f32[12,24,128]{2,1,0:T(8,128)}, u32[]{:S(2)}) %copy-start.2) | copy-done | bytes 147480
  1.8 4.0 %collective-permute-start.2 = (bf16[288,128]{1,0:T(8,128)(2,1)S(1)}, bf16[288,128]{1,0:T(8,128)(2,1)S(1)}, u32[]{:S(2)}, u32[]{:S(2)}) collective-permute-start(bf16[288,128]{1,0:T(8,128)(2,1)S(1)} %norm.1), channel_id=1, source_target_pairs={{0,3},{1,2},{2,1},{3,0},{4,7},{5,6},{6,5},{7,4},{8,11},{9,10},{10,... | collective-permute-start | bytes 221192 | tf_op jit(solution)/shard_map/ppermute | solution.py:399
  6.4 1.7 %collective-permute-done.2 = bf16[288,128]{1,0:T(8,128)(2,1)S(1)} collective-permute-done((bf16[288,128]{1,0:T(8,128)(2,1)S(1)}, bf16[288,128]{1,0:T(8,128)(2,1)S(1)}, u32[]{:S(2)}, u32[]{:S(2)}) %collective-permute-start.2) | collective-permute-done | bytes 73760 | tf_op jit(solution)/shard_map/ppermute | solution.py:399
  8.1 2.0 %collective-permute-done.1 = bf16[288,128]{1,0:T(8,128)(2,1)S(1)} collective-permute-done((bf16[288,128]{1,0:T(8,128)(2,1)S(1)}, bf16[288,128]{1,0:T(8,128)(2,1)S(1)}, u32[]{:S(2)}, u32[]{:S(2)}) %collective-permute-start.1) | collective-permute-done | bytes 73760 | tf_op jit(solution)/shard_map/ppermute | solution.py:399
  11.2 0.9 %copy-done = bf16[128,640]{1,0:T(8,128)(2,1)S(1)} copy-done((bf16[128,640]{1,0:T(8,128)(2,1)S(1)}, bf16[128,640]{1,0:T(8,128)(2,1)}, u32[]{:S(2)}) %copy-start) | copy-done | bytes 163864
  12.8 0.9 %left.1 = (f32[4,12,24,128]{3,2,1,0:T(8,128)S(1)}, f32[4,12,24,128]{3,2,1,0:T(8,128)S(1)}, f32[4,12,24,128]{3,2,1,0:T(8,128)S(1)}) custom-call(s32[12]{0:T(128)S(1)} %copy-done.6, bf16[1152,128]{1,0:T(8,128)(2,1)S(1)} %pad_maximum_fusion.x_ref.home_ref, bf16[1152,128]{1,0:T(8,128)(2,1)S(1)} %pad_maximum_fusion.x_ref.home_ref, bf16[128,640]{1,0:T(8,128)(2,1)S(1)} %copy-done), custom_call_target="tpu_custom_call" | custom-call | bytes 3321000 | tf_op jit(solution)/shard_map/left/pallas_call | solution.py:360
  14.2 0.9 %right_own.1 = (bf16[1152,128]{1,0:T(8,128)(2,1)S(1)}, f32[2,4,12,24,128]{4,3,2,1,0:T(8,128)S(1)}, f32[2,4,12,24,128]{4,3,2,1,0:T(8,128)S(1)}, f32[2,4,12,24,128]{4,3,2,1,0:T(8,128)S(1)}) custom-call(s32[12]{0:T(128)S(1)} %copy-done.7, bf16[1152,128]{1,0:T(8,128)(2,1)S(1)} %collective-permute-done.4.x_ref.home_ref, ...), custom_call_target="tpu_custom_call" | custom-call | bytes 3321000 | tf_op jit(solution)/shard_map/right_own/pallas_call | solution.py:360
  15.7 0.9 %right_other.1 = (bf16[1152,128]{1,0:T(8,128)(2,1)S(1)}, f32[2,4,12,24,128]{4,3,2,1,0:T(8,128)S(1)}, f32[2,4,12,24,128]{4,3,2,1,0:T(8,128)S(1)}, f32[2,4,12,24,128]{4,3,2,1,0:T(8,128)S(1)}) custom-call(s32[12]{0:T(128)S(1)} %copy-done.7, ...), custom_call_target="tpu_custom_call", output_to_operand_aliasing={{1}: (4, {}), {2}: (5, {}), {3}: (6, {})} | custom-call | bytes 3321000 | tf_op jit(solution)/shard_map/right_other/pallas_call | solution.py:360
  16.6 2.1 %mix.1 = (bf16[288,128]{1,0:T(8,128)(2,1)S(1)}, f32[12,24,8,128]{3,2,1,0:T(8,128)S(1)}) custom-call(f32[4,12,24,128]{3,2,1,0:T(8,128)S(1)} %get-tuple-element.61.lv_ref, f32[2,4,12,24,128]{4,3,2,1,0:T(8,128)S(1)} %get-tuple-element.68.rv_ref, f32[288,128]{1,0:T(8,128)S(1)} %get-tuple-element.71.back_ref), custom_call_target="tpu_custom_call" | custom-call | bytes 6642000 | tf_op jit(solution)/shard_map/mix/pallas_call | solution.py:360
  18.7 2.7 %grads.1 = (bf16[1152,256]{1,0:T(8,128)(2,1)S(1)}, bf16[2,1152,256]{2,1,0:T(8,128)(2,1)S(1)}) custom-call(f32[4,12,24,128]{3,2,1,0:T(8,128)S(1)} %get-tuple-element.61.lv_ref, f32[4,12,24,128]{3,2,1,0:T(8,128)S(1)} %get-tuple-element.62.la_ref, f32[4,12,24,128]{3,2,1,0:T(8,128)S(1)} %get-tuple-element.63.lb_ref, ...), custom_call_target="tpu_custom_call" | custom-call | bytes 11070000 | tf_op jit(solution)/shard_map/grads/pallas_call | solution.py:360
  23.0 1.2 %collective-permute-done.6.got_ref = bf16[384,128]{1,0:T(8,128)(2,1)S(1)} collective-permute-done((bf16[384,128]{1,0:T(8,128)(2,1)S(1)}, bf16[384,128]{1,0:T(8,128)(2,1)S(1)}, u32[]{:S(2)}, u32[]{:S(2)}) %collective-permute-start.6) | collective-permute-done | bytes 98336 | tf_op jit(solution)/shard_map/ppermute | solution.py:399
  24.3 5.9 %collective-permute-start.7 = (bf16[96,128]{1,0:T(8,128)(2,1)S(1)}, bf16[96,128]{1,0:T(8,128)(2,1)S(1)}, u32[]{:S(2)}, u32[]{:S(2)}) collective-permute-start(bf16[96,128]{1,0:T(8,128)(2,1)S(1)} %get-tuple-element.86), channel_id=1, source_target_pairs={{0,1},{1,0},{2,3},{3,2},{4,5},{5,4},{6,7},{7,6},{8,9},{9,8},{10,11... | collective-permute-start | bytes 73736 | tf_op jit(solution)/shard_map/ppermute | solution.py:399
  30.2 2.4 %collective-permute-start.8 = (bf16[96,128]{1,0:T(8,128)(2,1)S(1)}, bf16[96,128]{1,0:T(8,128)(2,1)S(1)}, u32[]{:S(2)}, u32[]{:S(2)}) collective-permute-start(bf16[96,128]{1,0:T(8,128)(2,1)S(1)} %get-tuple-element.87), channel_id=1, source_target_pairs={{0,2},{1,3},{2,0},{3,1},{4,6},{5,7},{6,4},{7,5},{8,10},{9,11},{10,... | collective-permute-start | bytes 73736 | tf_op jit(solution)/shard_map/ppermute | solution.py:399
  33.4 1.0 %collective-permute-done.8 = bf16[96,128]{1,0:T(8,128)(2,1)S(1)} collective-permute-done((bf16[96,128]{1,0:T(8,128)(2,1)S(1)}, bf16[96,128]{1,0:T(8,128)(2,1)S(1)}, u32[]{:S(2)}, u32[]{:S(2)}) %collective-permute-start.8) | collective-permute-done | bytes 24608 | tf_op jit(solution)/shard_map/ppermute | solution.py:399
  34.4 2.9 %collective-permute-done.9 = bf16[96,128]{1,0:T(8,128)(2,1)S(1)} collective-permute-done((bf16[96,128]{1,0:T(8,128)(2,1)S(1)}, bf16[96,128]{1,0:T(8,128)(2,1)S(1)}, u32[]{:S(2)}, u32[]{:S(2)}) %collective-permute-start.9) | collective-permute-done | bytes 24608 | tf_op jit(solution)/shard_map/ppermute | solution.py:399
  37.3 3.6 %collective-permute-start.14 = (bf16[96,128]{1,0:T(8,128)(2,1)S(1)}, bf16[96,128]{1,0:T(8,128)(2,1)S(1)}, u32[]{:S(2)}, u32[]{:S(2)}) collective-permute-start(bf16[96,128]{1,0:T(8,128)(2,1)S(1)} %fusion), channel_id=1, source_target_pairs={{0,24},{1,25},{2,26},{3,27},{4,28},{5,29},{6,30},{7,31},{8,16},{9,... | collective-permute-start | bytes 73736 | tf_op jit(solution)/shard_map/ppermute | solution.py:399
  41.8 1.3 %collective-permute-done.14 = bf16[96,128]{1,0:T(8,128)(2,1)S(1)} collective-permute-done((bf16[96,128]{1,0:T(8,128)(2,1)S(1)}, bf16[96,128]{1,0:T(8,128)(2,1)S(1)}, u32[]{:S(2)}, u32[]{:S(2)}) %collective-permute-start.14) | collective-permute-done | bytes 24608 | tf_op jit(solution)/shard_map/ppermute | solution.py:399
  43.1 2.5 %collective-permute-done.13 = bf16[96,128]{1,0:T(8,128)(2,1)S(1)} collective-permute-done((bf16[96,128]{1,0:T(8,128)(2,1)S(1)}, bf16[96,128]{1,0:T(8,128)(2,1)S(1)}, u32[]{:S(2)}, u32[]{:S(2)}) %collective-permute-start.13) | collective-permute-done | bytes 24608 | tf_op jit(solution)/shard_map/ppermute | solution.py:399
  45.8 1.2 %collective-permute-done.15.swapped_ref = bf16[96,128]{1,0:T(8,128)(2,1)S(1)} collective-permute-done((bf16[96,128]{1,0:T(8,128)(2,1)S(1)}, bf16[96,128]{1,0:T(8,128)(2,1)S(1)}, u32[]{:S(2)}, u32[]{:S(2)}) %collective-permute-start.15) | collective-permute-done | bytes 24608 | tf_op jit(solution)/shard_map/ppermute | solution.py:399
  48.0 2.2 %collective-permute-start.18 = (bf16[480,128]{1,0:T(8,128)(2,1)S(1)}, bf16[480,128]{1,0:T(8,128)(2,1)S(1)}, u32[]{:S(2)}, u32[]{:S(2)}) collective-permute-start(bf16[480,128]{1,0:T(8,128)(2,1)S(1)} %get-tuple-element.100), channel_id=1, source_target_pairs={{0,2},{1,3},{2,0},{3,1},{4,6},{5,7},{6,4},{7,5},{8,10},{9,11},{10,... | collective-permute-start | bytes 368648 | tf_op jit(solution)/shard_map/ppermute | solution.py:399
  50.6 2.2 %collective-permute-done.17.rest_0_ = bf16[480,128]{1,0:T(8,128)(2,1)S(1)} collective-permute-done((bf16[480,128]{1,0:T(8,128)(2,1)S(1)}, bf16[480,128]{1,0:T(8,128)(2,1)S(1)}, u32[]{:S(2)}, u32[]{:S(2)}) %collective-permute-start.17) | collective-permute-done | bytes 122912 | tf_op jit(solution)/shard_map/ppermute | solution.py:399
  52.9 2.6 %collective-permute-done.18.rest_1_ = bf16[480,128]{1,0:T(8,128)(2,1)S(1)} collective-permute-done((bf16[480,128]{1,0:T(8,128)(2,1)S(1)}, bf16[480,128]{1,0:T(8,128)(2,1)S(1)}, u32[]{:S(2)}, u32[]{:S(2)}) %collective-permute-start.18) | collective-permute-done | bytes 122912 | tf_op jit(solution)/shard_map/ppermute | solution.py:399
  55.5 0.9 %collective-permute-done.19.rest_2_ = bf16[480,128]{1,0:T(8,128)(2,1)S(1)} collective-permute-done((bf16[480,128]{1,0:T(8,128)(2,1)S(1)}, bf16[480,128]{1,0:T(8,128)(2,1)S(1)}, u32[]{:S(2)}, u32[]{:S(2)}) %collective-permute-start.19) | collective-permute-done | bytes 122912 | tf_op jit(solution)/shard_map/ppermute | solution.py:399
  56.4 1.1 %final.1 = (f32[288,128]{1,0:T(8,128)}, f32[128,640]{1,0:T(8,128)}, f32[128,128]{1,0:T(8,128)}, f32[288,128]{1,0:T(8,128)}) custom-call(f32[288,128]{1,0:T(8,128)S(1)} %get-tuple-element.97.own_ref, f32[288,128]{1,0:T(8,128)S(1)} %bitcast.5, bf16[96,128]{1,0:T(8,128)(2,1)S(1)} %add_convert_fusion.chunk_ref, ...), custom_call_target="tpu_custom_call" | custom-call | bytes 3690000 | tf_op jit(solution)/shard_map/final/pallas_call | solution.py:360
  (50 shorter events, 8.3 us)
Async XLA Ops:
  0.6 13.1 %copy-start.1 = (bf16[128,640]{1,0:T(8,128)(2,1)S(1)}, bf16[128,640]{1,0:T(8,128)(2,1)}, u32[]{:S(2)}) copy-start(bf16[128,640]{1,0:T(8,128)(2,1)} %w_ref.13) | copy-start | bytes 491524
  1.6 12.1 %copy-start.5 = (bf16[128,128]{1,0:T(8,128)(2,1)S(1)}, bf16[128,128]{1,0:T(8,128)(2,1)}, u32[]{:S(2)}) copy-start(bf16[128,128]{1,0:T(8,128)(2,1)} %wout_ref.3) | copy-start | bytes 98308
  1.6 12.6 %copy-start.7 = (s32[12]{0:T(128)S(1)}, s32[12]{0:T(128)}, u32[]{:S(2)}) copy-start(s32[12]{0:T(128)} %valid_ref.5) | copy-start | bytes 148
  1.8 6.3 %collective-permute-start.2 = (bf16[288,128]{1,0:T(8,128)(2,1)S(1)}, bf16[288,128]{1,0:T(8,128)(2,1)S(1)}, u32[]{:S(2)}, u32[]{:S(2)}) collective-permute-start(bf16[288,128]{1,0:T(8,128)(2,1)S(1)} %norm.1), channel_id=1, source_target_pairs={{0,3},{1,2},{2,1},{3,0},{4,7},{5,6},{6,5},{7,4},{8,11},{9,10},{10,... | collective-permute-start | bytes 221192 | tf_op jit(solution)/shard_map/ppermute | solution.py:399
  5.8 4.4 %collective-permute-start.1 = (bf16[288,128]{1,0:T(8,128)(2,1)S(1)}, bf16[288,128]{1,0:T(8,128)(2,1)S(1)}, u32[]{:S(2)}, u32[]{:S(2)}) collective-permute-start(bf16[288,128]{1,0:T(8,128)(2,1)S(1)} %norm.1), channel_id=1, source_target_pairs={{0,2},{1,3},{2,0},{3,1},{4,6},{5,7},{6,4},{7,5},{8,10},{9,11},{10,... | collective-permute-start | bytes 221192 | tf_op jit(solution)/shard_map/ppermute | solution.py:399
  6.3 4.4 %collective-permute-start = (bf16[288,128]{1,0:T(8,128)(2,1)S(1)}, bf16[288,128]{1,0:T(8,128)(2,1)S(1)}, u32[]{:S(2)}, u32[]{:S(2)}) collective-permute-start(bf16[288,128]{1,0:T(8,128)(2,1)S(1)} %norm.1), channel_id=1, source_target_pairs={{0,1},{1,0},{2,3},{3,2},{4,5},{5,4},{6,7},{7,6},{8,9},{9,8},{10,11... | collective-permute-start | bytes 221192 | tf_op jit(solution)/shard_map/ppermute | solution.py:399
  10.6 3.4 %collective-permute-start.4 = (bf16[1152,128]{1,0:T(8,128)(2,1)S(1)}, bf16[1152,128]{1,0:T(8,128)(2,1)S(1)}, u32[]{:S(2)}, u32[]{:S(2)}) collective-permute-start(bf16[1152,128]{1,0:T(8,128)(2,1)S(1)} %pad_maximum_fusion.x_ref.home_ref), channel_id=1, source_target_pairs={{0,4},{1,17},{2,10},{3,27},{4,0},{5,21},{6,14},{7,31},{8,16},{9,1}... | collective-permute-start | bytes 884744 | tf_op jit(solution)/shard_map/ppermute | solution.py:399
  10.7 3.0 %collective-permute-start.3 = (f32[288,128]{1,0:T(8,128)}, f32[288,128]{1,0:T(8,128)S(1)}, u32[]{:S(2)}, u32[]{:S(2)}) collective-permute-start(f32[288,128]{1,0:T(8,128)} %bitcast.6), channel_id=1, source_target_pairs={{0,4},{1,5},{2,6},{3,7},{4,0},{5,1},{6,2},{7,3},{8,10},{9,11},{10,... | collective-permute-start | bytes 442376 | tf_op jit(solution)/shard_map/ppermute | solution.py:399
  14.0 1.6 %collective-permute-start.5 = (bf16[1152,128]{1,0:T(8,128)(2,1)S(1)}, bf16[1152,128]{1,0:T(8,128)(2,1)S(1)}, u32[]{:S(2)}, u32[]{:S(2)}) collective-permute-start(bf16[1152,128]{1,0:T(8,128)(2,1)S(1)} %collective-permute-done.4.x_ref.home_ref), channel_id=1, source_target_pairs={{0,4},{1,5},{2,6},{3,7},{4,0},{5,1},{6,2},{7,3},{8,12},{9,13},{10,... | collective-permute-start | bytes 884744 | tf_op jit(solution)/shard_map/ppermute | solution.py:399
  22.4 10.8 %collective-permute-start.10 = (bf16[1152,128]{1,0:T(8,128)(2,1)S(1)}, bf16[1152,128]{1,0:T(8,128)(2,1)S(1)}, u32[]{:S(2)}, u32[]{:S(2)}) collective-permute-start(bf16[1152,128]{1,0:T(8,128)(2,1)S(1)} %back_other.1), channel_id=1, source_target_pairs={{0,4},{1,5},{2,6},{3,7},{4,0},{5,1},{6,2},{7,3},{8,12},{9,13},{10,... | collective-permute-start | bytes 884744 | tf_op jit(solution)/shard_map/ppermute | solution.py:399
  22.6 1.6 %collective-permute-start.6 = (bf16[384,128]{1,0:T(8,128)(2,1)S(1)}, bf16[384,128]{1,0:T(8,128)(2,1)S(1)}, u32[]{:S(2)}, u32[]{:S(2)}) collective-permute-start(bf16[384,128]{1,0:T(8,128)(2,1)S(1)} %get-tuple-element.81), channel_id=1, source_target_pairs={{0,4},{1,5},{2,6},{3,7},{4,0},{5,1},{6,2},{7,3},{8,12},{9,13},{10,... | collective-permute-start | bytes 294920 | tf_op jit(solution)/shard_map/ppermute | solution.py:399
  24.3 9.2 %collective-permute-start.7 = (bf16[96,128]{1,0:T(8,128)(2,1)S(1)}, bf16[96,128]{1,0:T(8,128)(2,1)S(1)}, u32[]{:S(2)}, u32[]{:S(2)}) collective-permute-start(bf16[96,128]{1,0:T(8,128)(2,1)S(1)} %get-tuple-element.86), channel_id=1, source_target_pairs={{0,1},{1,0},{2,3},{3,2},{4,5},{5,4},{6,7},{7,6},{8,9},{9,8},{10,11... | collective-permute-start | bytes 73736 | tf_op jit(solution)/shard_map/ppermute | solution.py:399
  30.2 4.2 %collective-permute-start.8 = (bf16[96,128]{1,0:T(8,128)(2,1)S(1)}, bf16[96,128]{1,0:T(8,128)(2,1)S(1)}, u32[]{:S(2)}, u32[]{:S(2)}) collective-permute-start(bf16[96,128]{1,0:T(8,128)(2,1)S(1)} %get-tuple-element.87), channel_id=1, source_target_pairs={{0,2},{1,3},{2,0},{3,1},{4,6},{5,7},{6,4},{7,5},{8,10},{9,11},{10,... | collective-permute-start | bytes 73736 | tf_op jit(solution)/shard_map/ppermute | solution.py:399
  32.6 4.7 %collective-permute-start.9 = (bf16[96,128]{1,0:T(8,128)(2,1)S(1)}, bf16[96,128]{1,0:T(8,128)(2,1)S(1)}, u32[]{:S(2)}, u32[]{:S(2)}) collective-permute-start(bf16[96,128]{1,0:T(8,128)(2,1)S(1)} %get-tuple-element.88), channel_id=1, source_target_pairs={{0,3},{1,2},{2,1},{3,0},{4,7},{5,6},{6,5},{7,4},{8,11},{9,10},{10,... | collective-permute-start | bytes 73736 | tf_op jit(solution)/shard_map/ppermute | solution.py:399
  33.3 23.2 %copy-start.3 = (f32[12,24,128]{2,1,0:T(8,128)S(1)}, f32[12,24,128]{2,1,0:T(8,128)}, u32[]{:S(2)}) copy-start(f32[12,24,128]{2,1,0:T(8,128)} %param.5) | copy-start | bytes 442372
  33.3 13.6 %collective-permute-start.11 = (bf16[1152,128]{1,0:T(8,128)(2,1)S(1)}, bf16[1152,128]{1,0:T(8,128)(2,1)S(1)}, u32[]{:S(2)}, u32[]{:S(2)}) collective-permute-start(bf16[1152,128]{1,0:T(8,128)(2,1)S(1)} %core_sum.1.y_ref), channel_id=1, source_target_pairs={{0,4},{1,9},{2,18},{3,27},{4,0},{5,13},{6,22},{7,31},{8,16},{9,25}... | collective-permute-start | bytes 884744 | tf_op jit(solution)/shard_map/ppermute | solution.py:399
  37.3 5.8 %collective-permute-start.14 = (bf16[96,128]{1,0:T(8,128)(2,1)S(1)}, bf16[96,128]{1,0:T(8,128)(2,1)S(1)}, u32[]{:S(2)}, u32[]{:S(2)}) collective-permute-start(bf16[96,128]{1,0:T(8,128)(2,1)S(1)} %fusion), channel_id=1, source_target_pairs={{0,24},{1,25},{2,26},{3,27},{4,28},{5,29},{6,30},{7,31},{8,16},{9,... | collective-permute-start | bytes 73736 | tf_op jit(solution)/shard_map/ppermute | solution.py:399
  40.9 4.7 %collective-permute-start.13 = (bf16[96,128]{1,0:T(8,128)(2,1)S(1)}, bf16[96,128]{1,0:T(8,128)(2,1)S(1)}, u32[]{:S(2)}, u32[]{:S(2)}) collective-permute-start(bf16[96,128]{1,0:T(8,128)(2,1)S(1)} %fusion), channel_id=1, source_target_pairs={{0,16},{1,17},{2,18},{3,19},{4,20},{5,21},{6,22},{7,23},{8,24},{9,... | collective-permute-start | bytes 73736 | tf_op jit(solution)/shard_map/ppermute | solution.py:399
  41.0 4.7 %collective-permute-start.12 = (bf16[96,128]{1,0:T(8,128)(2,1)S(1)}, bf16[96,128]{1,0:T(8,128)(2,1)S(1)}, u32[]{:S(2)}, u32[]{:S(2)}) collective-permute-start(bf16[96,128]{1,0:T(8,128)(2,1)S(1)} %fusion), channel_id=1, source_target_pairs={{0,8},{1,9},{2,10},{3,11},{4,12},{5,13},{6,14},{7,15},{8,0},{9,1},... | collective-permute-start | bytes 73736 | tf_op jit(solution)/shard_map/ppermute | solution.py:399
  41.8 5.2 %collective-permute-start.16 = (f32[288,128]{1,0:T(8,128)S(1)}, f32[288,128]{1,0:T(8,128)S(1)}, u32[]{:S(2)}, u32[]{:S(2)}) collective-permute-start(f32[288,128]{1,0:T(8,128)S(1)} %get-tuple-element.95.own_out_ref), channel_id=1, source_target_pairs={{0,4},{1,5},{2,6},{3,7},{4,0},{5,1},{6,2},{7,3},{8,10},{9,11},{10,... | collective-permute-start | bytes 442376 | tf_op jit(solution)/shard_map/ppermute | solution.py:399
  45.7 1.3 %collective-permute-start.15 = (bf16[96,128]{1,0:T(8,128)(2,1)S(1)}, bf16[96,128]{1,0:T(8,128)(2,1)S(1)}, u32[]{:S(2)}, u32[]{:S(2)}) collective-permute-start(bf16[96,128]{1,0:T(8,128)(2,1)S(1)} %add_convert_fusion.chunk_ref), channel_id=1, source_target_pairs={{0,4},{1,5},{2,6},{3,7},{4,0},{5,1},{6,2},{7,3},{8,12},{9,13},{10,... | collective-permute-start | bytes 73736 | tf_op jit(solution)/shard_map/ppermute | solution.py:399
  47.1 5.8 %collective-permute-start.17 = (bf16[480,128]{1,0:T(8,128)(2,1)S(1)}, bf16[480,128]{1,0:T(8,128)(2,1)S(1)}, u32[]{:S(2)}, u32[]{:S(2)}) collective-permute-start(bf16[480,128]{1,0:T(8,128)(2,1)S(1)} %get-tuple-element.99), channel_id=1, source_target_pairs={{0,1},{1,0},{2,3},{3,2},{4,5},{5,4},{6,7},{7,6},{8,9},{9,8},{10,11... | collective-permute-start | bytes 368648 | tf_op jit(solution)/shard_map/ppermute | solution.py:399
  48.0 7.5 %collective-permute-start.18 = (bf16[480,128]{1,0:T(8,128)(2,1)S(1)}, bf16[480,128]{1,0:T(8,128)(2,1)S(1)}, u32[]{:S(2)}, u32[]{:S(2)}) collective-permute-start(bf16[480,128]{1,0:T(8,128)(2,1)S(1)} %get-tuple-element.100), channel_id=1, source_target_pairs={{0,2},{1,3},{2,0},{3,1},{4,6},{5,7},{6,4},{7,5},{8,10},{9,11},{10,... | collective-permute-start | bytes 368648 | tf_op jit(solution)/shard_map/ppermute | solution.py:399
  50.2 6.2 %collective-permute-start.19 = (bf16[480,128]{1,0:T(8,128)(2,1)S(1)}, bf16[480,128]{1,0:T(8,128)(2,1)S(1)}, u32[]{:S(2)}, u32[]{:S(2)}) collective-permute-start(bf16[480,128]{1,0:T(8,128)(2,1)S(1)} %get-tuple-element.101), channel_id=1, source_target_pairs={{0,3},{1,2},{2,1},{3,0},{4,7},{5,6},{6,5},{7,4},{8,11},{9,10},{10,... | collective-permute-start | bytes 368648 | tf_op jit(solution)/shard_map/ppermute | solution.py:399
  (4 other events, 14.6 us)

commit v4 on v3

--- a/solution.py
+++ b/solution.py
@@ -63,17 +63,17 @@
     low_ref[...] = layer_norm(pair_ref[...])[0].astype(BF16)
 
 
-def project_block(projected, valid_ref, row, block, sizes, index, v_ref, a_ref, b_ref):
+def mask_kernel(valid_ref, mask_ref):
+    spot = lax.broadcasted_iota(jnp.int32, (SEG, mask_ref.shape[1]), 0)
+    for g in range(mask_ref.shape[0] // SEG):
+        mask_ref[tile(g), :] = jnp.where(spot < valid_ref[g], 1.0, 0.0)
+
+
+def project_block(projected, mask_ref, row, block, sizes, index, v_ref, a_ref, b_ref):
     row_len, col_len, width = sizes
-    spot = lax.broadcasted_iota(jnp.int32, (SEG, width), 0)
-    groups = col_len // SEG
-    keep_col = jnp.concatenate(
-        [jnp.where(spot < valid_ref[block * groups + g], 1.0, 0.0) for g in range(groups)], axis=0
-    )
+    keep_col = mask_ref[pl.ds(pl.multiple_of(block * col_len, SEG), col_len), :]
     for i in range(row_len):
-        token = row * row_len + i
-        valid = (token & (SEG - 1)) < valid_ref[token >> 3]
-        keep = keep_col * jnp.where(valid, 1.0, 0.0)
+        keep = keep_col * mask_ref[pl.ds(row * row_len + i, 1), :]
         part = projected[i * col_len : (i + 1) * col_len]
         gate = sigmoid(part[:, :width])
         kept = keep * gate
@@ -83,7 +83,7 @@
         b_ref[index + (i,)] = kept
 
 
-def project_kernel(side, cols, sizes, valid_ref, x_ref, home_ref, w_ref, *refs):
+def project_kernel(side, cols, sizes, mask_ref, x_ref, home_ref, w_ref, *refs):
     row_len, col_len, width = sizes
     area = row_len * col_len
     row, core, col, step, pair = place(cols)
@@ -102,7 +102,7 @@
             refs[-4][rows, :] = used
         projected = dot(used, w_ref[:, base : base + 2 * width])
         index = (half, d) if side else (d,)
-        project_block(projected, valid_ref, row, col ^ d, sizes, index, *outs)
+        project_block(projected, mask_ref, row, col ^ d, sizes, index, *outs)
 
     by_fours(cols, one)
 
@@ -314,8 +314,7 @@
         chunk_refs[d - 1][...] = sum_ref[col ^ d].astype(BF16)
 
 
-def row_sum_kernel(cols, area, gx_ref, got_ref, y_ref, chunk_ref, swapped_ref, own_ref, *send_refs):
-    chunk = chunk_ref.shape[0]
+def row_sum_kernel(cols, area, gx_ref, got_ref, y_ref, chunk_ref, own_ref, *send_refs):
     row, core, col, step, pair = place(cols)
     stays = pair == row >> 1
 
@@ -326,36 +325,42 @@
     own_ref[...] = total(0)
     for d in range(1, cols):
         send_refs[d - 1][:area, :] = total(d).astype(BF16)
-        send_refs[d - 1][area : area + chunk, :] = chunk_ref[...]
-        send_refs[d - 1][area + chunk :, :] = swapped_ref[...]
-
-
-def final_kernel(
-    cols, area, own_ref, pair_ref, chunk_ref, swapped_ref, home_ref, own_out_ref, *rest
-):
-    got_refs = rest[: cols - 1]
-    grad_ref, proj_ref, out_ref, home_out_ref, order_ref = rest[cols - 1 :]
-    chunk, width = chunk_ref.shape
+        send_refs[d - 1][area:, :] = chunk_ref[...]
+
+
+def join_kernel(cols, area, chunk_ref, *rest):
+    got_refs, (half_ref, order_ref) = rest[: cols - 1], rest[cols - 1 :]
+    col = lax.axis_index("col")
+    order_ref[col] = chunk_ref[...].astype(F32)
+    for d in range(1, cols):
+        order_ref[col ^ d] = got_refs[d - 1][area:, :].astype(F32)
+    half_ref[...] = order_ref[...].reshape(half_ref.shape).astype(BF16)
+
+
+def pair_grad_kernel(cols, area, own_ref, pair_ref, home_ref, own_out_ref, *rest):
+    got_refs, (grad_ref, out_ref) = rest[:-2], rest[-2:]
     row, core, col, step, pair = place(cols)
-    home_out_ref[...] = jnp.where(step == 0, own_out_ref[...], home_ref[...])
+    out_ref[...] = jnp.where(step == 0, own_out_ref[...], home_ref[...])
     total = own_ref[...]
-    order_ref[core, col] = chunk_ref[...].astype(F32)
-    order_ref[1 - core, col] = swapped_ref[...].astype(F32)
-    for d in range(1, cols):
-        got = got_refs[d - 1]
+    for got in got_refs:
         total = total + got[:area, :].astype(F32)
-        order_ref[core, col ^ d] = got[area : area + chunk, :].astype(F32)
-        order_ref[1 - core, col ^ d] = got[area + chunk :, :].astype(F32)
     normed, scaled = layer_norm(pair_ref[...])
     grad_ref[...] = norm_back(total, normed, scaled)
-    whole = order_ref[...].reshape(6 * width, width)
-    for n in range(5):
-        proj_ref[:, n * width : (n + 1) * width] = whole[n * width : (n + 1) * width]
-    out_ref[...] = whole[5 * width :]
-
-
-def call(kernel, name, micros, out_shape, args, scratch=(), smem=0, aliases=None):
-    specs = [pl.BlockSpec(memory_space=pltpu.SMEM if n < smem else pltpu.VMEM) for n in range(len(args))]
+
+
+def weights_kernel(width, mine_ref, other_ref, proj_ref, out_ref):
+    first = (lax.axis_index("row") & 1) == 0
+    mine, other = mine_ref[...].astype(F32), other_ref[...].astype(F32)
+    low, high = jnp.where(first, mine, other), jnp.where(first, other, mine)
+    for n in range(3):
+        proj_ref[:, n * width : (n + 1) * width] = low[n * width : (n + 1) * width]
+    for n in range(2):
+        proj_ref[:, (3 + n) * width : (4 + n) * width] = high[n * width : (n + 1) * width]
+    out_ref[...] = high[2 * width :]
+
+
+def call(kernel, name, micros, out_shape, args, scratch=(), aliases=None, space=pltpu.VMEM):
+    specs = [pl.BlockSpec(memory_space=space) for _ in args]
     total = sum(_bytes(ref) for ref in [*args, *out_shape, *scratch])
     return pl.pallas_call(
         kernel,
@@ -421,15 +426,17 @@
     blocks = [low] + [in_plane(low, d) for d in range(1, cols)]
     x = jnp.concatenate(blocks, axis=0)
     got_x = permute(x, lambda z, core, col: (flip(col ^ z, cols), core, col))
-    cot, x = lax.optimization_barrier((cot, x))
+    cot, x, block_valid = lax.optimization_barrier((cot, x, block_valid))
     got_cot = to_pair(cot)
+    (mask,) = call(
+        mask_kernel, "mask", 0.1, [like(col_len * cols, width)], [block_valid], space=pltpu.SMEM
+    )
     left = call(
         functools.partial(project_kernel, 0, cols, sizes),
         "left",
         0.9,
         [like(cols, row_len, col_len, width)] * 3,
-        [block_valid, x, x, proj_weight],
-        smem=1,
+        [mask, x, x, proj_weight],
     )
     out_gate, cot, back, update_low = call(
         functools.partial(gate_kernel, cols, area, width),
@@ -446,16 +453,14 @@
         "right_own",
         0.9,
         right_shape,
-        [block_valid, got_x, x, proj_weight],
-        smem=1,
+        [mask, got_x, x, proj_weight],
     )
     other_x, *right = call(
         functools.partial(project_kernel, 2, cols, sizes),
         "right_other",
         0.9,
         right_shape,
-        [block_valid, swapped_x, got_x, proj_weight, *right],
-        smem=1,
+        [mask, swapped_x, got_x, proj_weight, *right],
         aliases={4: 1, 5: 2, 6: 3},
     )
     flat = pltpu.VMEM((row_len, col_len, width), F32)
@@ -530,23 +535,38 @@
     for d in range(1, cols):
         mine = mine + across(low_mine, d).astype(F32)
     low_mine = mine.astype(BF16)
-    swapped = swap(low_mine)
-    swapped, home = lax.optimization_barrier((swapped, home))
+    low_mine, home = lax.optimization_barrier((low_mine, home))
     own, *sends = call(
         functools.partial(row_sum_kernel, cols, area),
         "row_sum",
         0.1,
-        [like(area, width)] + [like(area + 2 * chunk, width, dtype=BF16)] * (cols - 1),
-        [gx, back_y, y, low_mine, swapped],
+        [like(area, width)] + [like(area + chunk, width, dtype=BF16)] * (cols - 1),
+        [gx, back_y, y, low_mine],
     )
     gets = [in_plane(sends[d - 1], d) for d in range(1, cols)]
-    pair_grad, proj_grad, out_grad, pair_out = call(
-        functools.partial(final_kernel, cols, area),
-        "final",
+    (half_w,) = call(
+        functools.partial(join_kernel, cols, area),
+        "join",
+        0.1,
+        [like(half, width, dtype=BF16)],
+        [low_mine, *gets],
+        [pltpu.VMEM((cols, chunk, width), F32)],
+    )
+    other_w = swap(half_w)
+    half_w, own = lax.optimization_barrier((half_w, own))
+    pair_grad, pair_out = call(
+        functools.partial(pair_grad_kernel, cols, area),
+        "pair_grad",
         1.0,
-        [like(area, width), like(*proj_weight.shape), like(width, width), like(area, width)],
-        [own, pair, low_mine, swapped, home, pair_out, *gets],
-        [pltpu.VMEM((2, cols, chunk, width), F32)],
+        [like(area, width)] * 2,
+        [own, pair, home, pair_out, *gets],
+    )
+    proj_grad, out_grad = call(
+        functools.partial(weights_kernel, width),
+        "weights",
+        0.8,
+        [like(*proj_weight.shape), like(width, width)],
+        [half_w, other_w],
     )
     shape = pair_input.shape
     return pair_out.reshape(shape), pair_grad.reshape(shape), proj_grad, out_grad

time: 57.7 us -> 56.2 us (0.974)
  waiting for transfers between devices: 20.7 us -> 19.8 us
    ppermute x20, waiting for transfers between devices: 20.7 us -> 19.8 us  [permute(): return lax.ppermute(value, ('row', 'col'), pairs)]
    pallas_call x15 -> x18, Pallas kernels: 11 us -> 10.5 us  [call(): pl.pallas_call(kernel, out_shape=tuple(out_shape), in_specs=specs, out_sp...]
    unnamed x16 -> x14, local copies, waits for them, and re-layouts: 2.54 us -> 2.49 us
  transfers between devices with their start and end apart: 20 -> 20, of which waited for: 13 -> 13; matrix products, arithmetic and copies ran while one was open for 0% -> 0% of each run, Pallas kernels for 5% -> 6%
where the time goes in v4:
time: 56.2 us; the launch traced here: 56 us
  starting transfers between devices  22.3 us (40%)
  waiting for transfers between devices  19.8 us (35%)
  Pallas kernels  10.5 us (19%)
  local copies, waits for them, and re-layouts  2.49 us (4%)
  between operations  0.88 us (2%)
    ppermute x20, starting transfers between devices, permute(): return lax.ppermute(value, ('row', 'col'), pairs)  22.3 us
    ppermute x20, waiting for transfers between devices, permute(): return lax.ppermute(value, ('row', 'col'), pairs)  19.8 us
    pallas_call x18, Pallas kernels, call(): pl.pallas_call(kernel, out_shape=tuple(out_shape), in_specs=specs, out_sp...  10.5 us
    unnamed x14, local copies, waits for them, and re-layouts  2.49 us
  transfers between devices with their start and end apart: 20, of which 13 were waited for; matrix products, arithmetic and copies ran while one was open for 0% of the time, Pallas kernels for 6%

profile of v4, /device:TPU:0, one launch (start us, length us, event | category | flops | bytes accessed | tf_op | source)
XLA Modules:
  0.0 56.0 jit_solution(5915067475088453124)
XLA Ops:
  0.6 0.9 %copy-done.2 = f32[12,24,128]{2,1,0:T(8,128)S(1)} copy-done((f32[12,24,128]{2,1,0:T(8,128)S(1)}, f32[12,24,128]{2,1,0:T(8,128)}, u32[]{:S(2)}) %copy-start.2) | copy-done | bytes 147480
  1.8 4.0 %collective-permute-start.2 = (bf16[288,128]{1,0:T(8,128)(2,1)S(1)}, bf16[288,128]{1,0:T(8,128)(2,1)S(1)}, u32[]{:S(2)}, u32[]{:S(2)}) collective-permute-start(bf16[288,128]{1,0:T(8,128)(2,1)S(1)} %norm.1), channel_id=1, source_target_pairs={{0,3},{1,2},{2,1},{3,0},{4,7},{5,6},{6,5},{7,4},{8,11},{9,10},{10,... | collective-permute-start | bytes 221192 | tf_op jit(solution)/shard_map/ppermute | solution.py:404
  6.4 1.7 %collective-permute-done.2 = bf16[288,128]{1,0:T(8,128)(2,1)S(1)} collective-permute-done((bf16[288,128]{1,0:T(8,128)(2,1)S(1)}, bf16[288,128]{1,0:T(8,128)(2,1)S(1)}, u32[]{:S(2)}, u32[]{:S(2)}) %collective-permute-start.2) | collective-permute-done | bytes 73760 | tf_op jit(solution)/shard_map/ppermute | solution.py:404
  8.1 2.0 %collective-permute-done.1 = bf16[288,128]{1,0:T(8,128)(2,1)S(1)} collective-permute-done((bf16[288,128]{1,0:T(8,128)(2,1)S(1)}, bf16[288,128]{1,0:T(8,128)(2,1)S(1)}, u32[]{:S(2)}, u32[]{:S(2)}) %collective-permute-start.1) | collective-permute-done | bytes 73760 | tf_op jit(solution)/shard_map/ppermute | solution.py:404
  12.4 0.9 %copy-done = bf16[128,640]{1,0:T(8,128)(2,1)S(1)} copy-done((bf16[128,640]{1,0:T(8,128)(2,1)S(1)}, bf16[128,640]{1,0:T(8,128)(2,1)}, u32[]{:S(2)}) %copy-start) | copy-done | bytes 163864
  14.5 1.1 %collective-permute-done.5.x_ref = bf16[1152,128]{1,0:T(8,128)(2,1)S(1)} collective-permute-done((bf16[1152,128]{1,0:T(8,128)(2,1)S(1)}, bf16[1152,128]{1,0:T(8,128)(2,1)S(1)}, u32[]{:S(2)}, u32[]{:S(2)}) %collective-permute-start.5) | collective-permute-done | bytes 294944 | tf_op jit(solution)/shard_map/ppermute | solution.py:404
  16.0 2.1 %mix.1 = (bf16[288,128]{1,0:T(8,128)(2,1)S(1)}, f32[12,24,8,128]{3,2,1,0:T(8,128)S(1)}) custom-call(f32[4,12,24,128]{3,2,1,0:T(8,128)S(1)} %get-tuple-element.65.lv_ref, f32[2,4,12,24,128]{4,3,2,1,0:T(8,128)S(1)} %get-tuple-element.72.rv_ref, f32[288,128]{1,0:T(8,128)S(1)} %get-tuple-element.75.back_ref), custom_call_target="tpu_custom_call" | custom-call | bytes 6642000 | tf_op jit(solution)/shard_map/mix/pallas_call | solution.py:365
  18.1 2.7 %grads.1 = (bf16[1152,256]{1,0:T(8,128)(2,1)S(1)}, bf16[2,1152,256]{2,1,0:T(8,128)(2,1)S(1)}) custom-call(f32[4,12,24,128]{3,2,1,0:T(8,128)S(1)} %get-tuple-element.65.lv_ref, f32[4,12,24,128]{3,2,1,0:T(8,128)S(1)} %get-tuple-element.66.la_ref, f32[4,12,24,128]{3,2,1,0:T(8,128)S(1)} %get-tuple-element.67.lb_ref, ...), custom_call_target="tpu_custom_call" | custom-call | bytes 11070000 | tf_op jit(solution)/shard_map/grads/pallas_call | solution.py:365
  22.4 1.2 %collective-permute-done.6.got_ref = bf16[384,128]{1,0:T(8,128)(2,1)S(1)} collective-permute-done((bf16[384,128]{1,0:T(8,128)(2,1)S(1)}, bf16[384,128]{1,0:T(8,128)(2,1)S(1)}, u32[]{:S(2)}, u32[]{:S(2)}) %collective-permute-start.6) | collective-permute-done | bytes 98336 | tf_op jit(solution)/shard_map/ppermute | solution.py:404
  23.6 5.9 %collective-permute-start.7 = (bf16[96,128]{1,0:T(8,128)(2,1)S(1)}, bf16[96,128]{1,0:T(8,128)(2,1)S(1)}, u32[]{:S(2)}, u32[]{:S(2)}) collective-permute-start(bf16[96,128]{1,0:T(8,128)(2,1)S(1)} %get-tuple-element.90), channel_id=1, source_target_pairs={{0,1},{1,0},{2,3},{3,2},{4,5},{5,4},{6,7},{7,6},{8,9},{9,8},{10,11... | collective-permute-start | bytes 73736 | tf_op jit(solution)/shard_map/ppermute | solution.py:404
  29.5 2.4 %collective-permute-start.8 = (bf16[96,128]{1,0:T(8,128)(2,1)S(1)}, bf16[96,128]{1,0:T(8,128)(2,1)S(1)}, u32[]{:S(2)}, u32[]{:S(2)}) collective-permute-start(bf16[96,128]{1,0:T(8,128)(2,1)S(1)} %get-tuple-element.91), channel_id=1, source_target_pairs={{0,2},{1,3},{2,0},{3,1},{4,6},{5,7},{6,4},{7,5},{8,10},{9,11},{10,... | collective-permute-start | bytes 73736 | tf_op jit(solution)/shard_map/ppermute | solution.py:404
  32.8 1.0 %collective-permute-done.8 = bf16[96,128]{1,0:T(8,128)(2,1)S(1)} collective-permute-done((bf16[96,128]{1,0:T(8,128)(2,1)S(1)}, bf16[96,128]{1,0:T(8,128)(2,1)S(1)}, u32[]{:S(2)}, u32[]{:S(2)}) %collective-permute-start.8) | collective-permute-done | bytes 24608 | tf_op jit(solution)/shard_map/ppermute | solution.py:404
  33.8 2.9 %collective-permute-done.9 = bf16[96,128]{1,0:T(8,128)(2,1)S(1)} collective-permute-done((bf16[96,128]{1,0:T(8,128)(2,1)S(1)}, bf16[96,128]{1,0:T(8,128)(2,1)S(1)}, u32[]{:S(2)}, u32[]{:S(2)}) %collective-permute-start.9) | collective-permute-done | bytes 24608 | tf_op jit(solution)/shard_map/ppermute | solution.py:404
  36.7 3.6 %collective-permute-start.12 = (bf16[96,128]{1,0:T(8,128)(2,1)S(1)}, bf16[96,128]{1,0:T(8,128)(2,1)S(1)}, u32[]{:S(2)}, u32[]{:S(2)}) collective-permute-start(bf16[96,128]{1,0:T(8,128)(2,1)S(1)} %fusion), channel_id=1, source_target_pairs={{0,24},{1,25},{2,26},{3,27},{4,28},{5,29},{6,30},{7,31},{8,16},{9,... | collective-permute-start | bytes 73736 | tf_op jit(solution)/shard_map/ppermute | solution.py:404
  40.3 0.8 %collective-permute-start.10 = (bf16[96,128]{1,0:T(8,128)(2,1)S(1)}, bf16[96,128]{1,0:T(8,128)(2,1)S(1)}, u32[]{:S(2)}, u32[]{:S(2)}) collective-permute-start(bf16[96,128]{1,0:T(8,128)(2,1)S(1)} %fusion), channel_id=1, source_target_pairs={{0,8},{1,9},{2,10},{3,11},{4,12},{5,13},{6,14},{7,15},{8,0},{9,1},... | collective-permute-start | bytes 73736 | tf_op jit(solution)/shard_map/ppermute | solution.py:404
  41.2 1.3 %collective-permute-done.12 = bf16[96,128]{1,0:T(8,128)(2,1)S(1)} collective-permute-done((bf16[96,128]{1,0:T(8,128)(2,1)S(1)}, bf16[96,128]{1,0:T(8,128)(2,1)S(1)}, u32[]{:S(2)}, u32[]{:S(2)}) %collective-permute-start.12) | collective-permute-done | bytes 24608 | tf_op jit(solution)/shard_map/ppermute | solution.py:404
  42.5 2.6 %collective-permute-done.11 = bf16[96,128]{1,0:T(8,128)(2,1)S(1)} collective-permute-done((bf16[96,128]{1,0:T(8,128)(2,1)S(1)}, bf16[96,128]{1,0:T(8,128)(2,1)S(1)}, u32[]{:S(2)}, u32[]{:S(2)}) %collective-permute-start.11) | collective-permute-done | bytes 24608 | tf_op jit(solution)/shard_map/ppermute | solution.py:404
  45.2 0.9 %collective-permute-start.16 = (bf16[384,128]{1,0:T(8,128)(2,1)S(1)}, bf16[384,128]{1,0:T(8,128)(2,1)S(1)}, u32[]{:S(2)}, u32[]{:S(2)}) collective-permute-start(bf16[384,128]{1,0:T(8,128)(2,1)S(1)} %get-tuple-element.101), channel_id=1, source_target_pairs={{0,1},{1,0},{2,3},{3,2},{4,5},{5,4},{6,7},{7,6},{8,9},{9,8},{10,11... | collective-permute-start | bytes 294920 | tf_op jit(solution)/shard_map/ppermute | solution.py:404
  46.1 2.2 %collective-permute-start.17 = (bf16[384,128]{1,0:T(8,128)(2,1)S(1)}, bf16[384,128]{1,0:T(8,128)(2,1)S(1)}, u32[]{:S(2)}, u32[]{:S(2)}) collective-permute-start(bf16[384,128]{1,0:T(8,128)(2,1)S(1)} %get-tuple-element.102), channel_id=1, source_target_pairs={{0,2},{1,3},{2,0},{3,1},{4,6},{5,7},{6,4},{7,5},{8,10},{9,11},{10,... | collective-permute-start | bytes 294920 | tf_op jit(solution)/shard_map/ppermute | solution.py:404
  48.8 1.1 %collective-permute-done.16.rest_0_ = bf16[384,128]{1,0:T(8,128)(2,1)S(1)} collective-permute-done((bf16[384,128]{1,0:T(8,128)(2,1)S(1)}, bf16[384,128]{1,0:T(8,128)(2,1)S(1)}, u32[]{:S(2)}, u32[]{:S(2)}) %collective-permute-start.16) | collective-permute-done | bytes 98336 | tf_op jit(solution)/shard_map/ppermute | solution.py:404
  49.9 2.4 %collective-permute-done.17.rest_1_ = bf16[384,128]{1,0:T(8,128)(2,1)S(1)} collective-permute-done((bf16[384,128]{1,0:T(8,128)(2,1)S(1)}, bf16[384,128]{1,0:T(8,128)(2,1)S(1)}, u32[]{:S(2)}, u32[]{:S(2)}) %collective-permute-start.17) | collective-permute-done | bytes 98336 | tf_op jit(solution)/shard_map/ppermute | solution.py:404
  52.3 1.5 %collective-permute-done.18.rest_2_ = bf16[384,128]{1,0:T(8,128)(2,1)S(1)} collective-permute-done((bf16[384,128]{1,0:T(8,128)(2,1)S(1)}, bf16[384,128]{1,0:T(8,128)(2,1)S(1)}, u32[]{:S(2)}, u32[]{:S(2)}) %collective-permute-start.18) | collective-permute-done | bytes 98336 | tf_op jit(solution)/shard_map/ppermute | solution.py:404
  54.0 0.9 %pair_grad.1 = (f32[288,128]{1,0:T(8,128)}, f32[288,128]{1,0:T(8,128)}) custom-call(f32[288,128]{1,0:T(8,128)S(1)} %get-tuple-element.105.own_ref, f32[288,128]{1,0:T(8,128)S(1)} %bitcast.5, f32[288,128]{1,0:T(8,128)S(1)} %collective-permute-done.13.home_ref, f32[288,128]{1,0:T(8,128)S(1)} %get-tuple-element.97.own_out_ref, ...), custom_call_target="tpu_custom_call" | custom-call | bytes 3690000 | tf_op jit(solution)/shard_map/pair_grad/pallas_call | solution.py:365
  55.2 0.8 %weights.1 = (f32[128,640]{1,0:T(8,128)}, f32[128,128]{1,0:T(8,128)}) custom-call(bf16[384,128]{1,0:T(8,128)(2,1)S(1)} %join.1.mine_ref, bf16[384,128]{1,0:T(8,128)(2,1)S(1)} %collective-permute-done.19.other_ref), custom_call_target="tpu_custom_call" | custom-call | bytes 2952000 | tf_op jit(solution)/shard_map/weights/pallas_call | solution.py:365
  (51 shorter events, 8.0 us)
Async XLA Ops:
  1.5 12.1 %copy-start.4 = (f32[12,24,128]{2,1,0:T(8,128)S(1)}, f32[12,24,128]{2,1,0:T(8,128)}, u32[]{:S(2)}) copy-start(f32[12,24,128]{2,1,0:T(8,128)} %param.9) | copy-start | bytes 442372
  1.5 12.1 %copy-start.5 = (bf16[128,128]{1,0:T(8,128)(2,1)S(1)}, bf16[128,128]{1,0:T(8,128)(2,1)}, u32[]{:S(2)}) copy-start(bf16[128,128]{1,0:T(8,128)(2,1)} %wout_ref.3) | copy-start | bytes 98308
  1.5 12.6 %copy-start.1 = (bf16[128,640]{1,0:T(8,128)(2,1)S(1)}, bf16[128,640]{1,0:T(8,128)(2,1)}, u32[]{:S(2)}) copy-start(bf16[128,640]{1,0:T(8,128)(2,1)} %w_ref.13) | copy-start | bytes 491524
  1.8 6.3 %collective-permute-start.2 = (bf16[288,128]{1,0:T(8,128)(2,1)S(1)}, bf16[288,128]{1,0:T(8,128)(2,1)S(1)}, u32[]{:S(2)}, u32[]{:S(2)}) collective-permute-start(bf16[288,128]{1,0:T(8,128)(2,1)S(1)} %norm.1), channel_id=1, source_target_pairs={{0,3},{1,2},{2,1},{3,0},{4,7},{5,6},{6,5},{7,4},{8,11},{9,10},{10,... | collective-permute-start | bytes 221192 | tf_op jit(solution)/shard_map/ppermute | solution.py:404
  5.7 4.4 %collective-permute-start.1 = (bf16[288,128]{1,0:T(8,128)(2,1)S(1)}, bf16[288,128]{1,0:T(8,128)(2,1)S(1)}, u32[]{:S(2)}, u32[]{:S(2)}) collective-permute-start(bf16[288,128]{1,0:T(8,128)(2,1)S(1)} %norm.1), channel_id=1, source_target_pairs={{0,2},{1,3},{2,0},{3,1},{4,6},{5,7},{6,4},{7,5},{8,10},{9,11},{10,... | collective-permute-start | bytes 221192 | tf_op jit(solution)/shard_map/ppermute | solution.py:404
  6.2 4.4 %collective-permute-start = (bf16[288,128]{1,0:T(8,128)(2,1)S(1)}, bf16[288,128]{1,0:T(8,128)(2,1)S(1)}, u32[]{:S(2)}, u32[]{:S(2)}) collective-permute-start(bf16[288,128]{1,0:T(8,128)(2,1)S(1)} %norm.1), channel_id=1, source_target_pairs={{0,1},{1,0},{2,3},{3,2},{4,5},{5,4},{6,7},{7,6},{8,9},{9,8},{10,11... | collective-permute-start | bytes 221192 | tf_op jit(solution)/shard_map/ppermute | solution.py:404
  10.6 3.4 %collective-permute-start.4 = (bf16[1152,128]{1,0:T(8,128)(2,1)S(1)}, bf16[1152,128]{1,0:T(8,128)(2,1)S(1)}, u32[]{:S(2)}, u32[]{:S(2)}) collective-permute-start(bf16[1152,128]{1,0:T(8,128)(2,1)S(1)} %pad_maximum_fusion.x_ref.home_ref), channel_id=1, source_target_pairs={{0,4},{1,17},{2,10},{3,27},{4,0},{5,21},{6,14},{7,31},{8,16},{9,1}... | collective-permute-start | bytes 884744 | tf_op jit(solution)/shard_map/ppermute | solution.py:404
  10.7 3.0 %collective-permute-start.3 = (f32[288,128]{1,0:T(8,128)}, f32[288,128]{1,0:T(8,128)S(1)}, u32[]{:S(2)}, u32[]{:S(2)}) collective-permute-start(f32[288,128]{1,0:T(8,128)} %bitcast.6), channel_id=1, source_target_pairs={{0,4},{1,5},{2,6},{3,7},{4,0},{5,1},{6,2},{7,3},{8,10},{9,11},{10,... | collective-permute-start | bytes 442376 | tf_op jit(solution)/shard_map/ppermute | solution.py:404
  14.0 1.6 %collective-permute-start.5 = (bf16[1152,128]{1,0:T(8,128)(2,1)S(1)}, bf16[1152,128]{1,0:T(8,128)(2,1)S(1)}, u32[]{:S(2)}, u32[]{:S(2)}) collective-permute-start(bf16[1152,128]{1,0:T(8,128)(2,1)S(1)} %collective-permute-done.4.x_ref.home_ref), channel_id=1, source_target_pairs={{0,4},{1,5},{2,6},{3,7},{4,0},{5,1},{6,2},{7,3},{8,12},{9,13},{10,... | collective-permute-start | bytes 884744 | tf_op jit(solution)/shard_map/ppermute | solution.py:404
  21.8 10.8 %collective-permute-start.14 = (bf16[1152,128]{1,0:T(8,128)(2,1)S(1)}, bf16[1152,128]{1,0:T(8,128)(2,1)S(1)}, u32[]{:S(2)}, u32[]{:S(2)}) collective-permute-start(bf16[1152,128]{1,0:T(8,128)(2,1)S(1)} %back_other.1), channel_id=1, source_target_pairs={{0,4},{1,5},{2,6},{3,7},{4,0},{5,1},{6,2},{7,3},{8,12},{9,13},{10,... | collective-permute-start | bytes 884744 | tf_op jit(solution)/shard_map/ppermute | solution.py:404
  22.0 1.6 %collective-permute-start.6 = (bf16[384,128]{1,0:T(8,128)(2,1)S(1)}, bf16[384,128]{1,0:T(8,128)(2,1)S(1)}, u32[]{:S(2)}, u32[]{:S(2)}) collective-permute-start(bf16[384,128]{1,0:T(8,128)(2,1)S(1)} %get-tuple-element.85), channel_id=1, source_target_pairs={{0,4},{1,5},{2,6},{3,7},{4,0},{5,1},{6,2},{7,3},{8,12},{9,13},{10,... | collective-permute-start | bytes 294920 | tf_op jit(solution)/shard_map/ppermute | solution.py:404
  23.6 9.1 %collective-permute-start.7 = (bf16[96,128]{1,0:T(8,128)(2,1)S(1)}, bf16[96,128]{1,0:T(8,128)(2,1)S(1)}, u32[]{:S(2)}, u32[]{:S(2)}) collective-permute-start(bf16[96,128]{1,0:T(8,128)(2,1)S(1)} %get-tuple-element.90), channel_id=1, source_target_pairs={{0,1},{1,0},{2,3},{3,2},{4,5},{5,4},{6,7},{7,6},{8,9},{9,8},{10,11... | collective-permute-start | bytes 73736 | tf_op jit(solution)/shard_map/ppermute | solution.py:404
  29.5 4.2 %collective-permute-start.8 = (bf16[96,128]{1,0:T(8,128)(2,1)S(1)}, bf16[96,128]{1,0:T(8,128)(2,1)S(1)}, u32[]{:S(2)}, u32[]{:S(2)}) collective-permute-start(bf16[96,128]{1,0:T(8,128)(2,1)S(1)} %get-tuple-element.91), channel_id=1, source_target_pairs={{0,2},{1,3},{2,0},{3,1},{4,6},{5,7},{6,4},{7,5},{8,10},{9,11},{10,... | collective-permute-start | bytes 73736 | tf_op jit(solution)/shard_map/ppermute | solution.py:404
  31.9 4.7 %collective-permute-start.9 = (bf16[96,128]{1,0:T(8,128)(2,1)S(1)}, bf16[96,128]{1,0:T(8,128)(2,1)S(1)}, u32[]{:S(2)}, u32[]{:S(2)}) collective-permute-start(bf16[96,128]{1,0:T(8,128)(2,1)S(1)} %get-tuple-element.92), channel_id=1, source_target_pairs={{0,3},{1,2},{2,1},{3,0},{4,7},{5,6},{6,5},{7,4},{8,11},{9,10},{10,... | collective-permute-start | bytes 73736 | tf_op jit(solution)/shard_map/ppermute | solution.py:404
  32.7 21.3 %copy-start.3 = (f32[12,24,128]{2,1,0:T(8,128)S(1)}, f32[12,24,128]{2,1,0:T(8,128)}, u32[]{:S(2)}) copy-start(f32[12,24,128]{2,1,0:T(8,128)} %param.5) | copy-start | bytes 442372
  32.7 12.4 %collective-permute-start.15 = (bf16[1152,128]{1,0:T(8,128)(2,1)S(1)}, bf16[1152,128]{1,0:T(8,128)(2,1)S(1)}, u32[]{:S(2)}, u32[]{:S(2)}) collective-permute-start(bf16[1152,128]{1,0:T(8,128)(2,1)S(1)} %core_sum.1.y_ref), channel_id=1, source_target_pairs={{0,4},{1,9},{2,18},{3,27},{4,0},{5,13},{6,22},{7,31},{8,16},{9,25}... | collective-permute-start | bytes 884744 | tf_op jit(solution)/shard_map/ppermute | solution.py:404
  36.7 5.8 %collective-permute-start.12 = (bf16[96,128]{1,0:T(8,128)(2,1)S(1)}, bf16[96,128]{1,0:T(8,128)(2,1)S(1)}, u32[]{:S(2)}, u32[]{:S(2)}) collective-permute-start(bf16[96,128]{1,0:T(8,128)(2,1)S(1)} %fusion), channel_id=1, source_target_pairs={{0,24},{1,25},{2,26},{3,27},{4,28},{5,29},{6,30},{7,31},{8,16},{9,... | collective-permute-start | bytes 73736 | tf_op jit(solution)/shard_map/ppermute | solution.py:404
  40.3 4.7 %collective-permute-start.11 = (bf16[96,128]{1,0:T(8,128)(2,1)S(1)}, bf16[96,128]{1,0:T(8,128)(2,1)S(1)}, u32[]{:S(2)}, u32[]{:S(2)}) collective-permute-start(bf16[96,128]{1,0:T(8,128)(2,1)S(1)} %fusion), channel_id=1, source_target_pairs={{0,16},{1,17},{2,18},{3,19},{4,20},{5,21},{6,22},{7,23},{8,24},{9,... | collective-permute-start | bytes 73736 | tf_op jit(solution)/shard_map/ppermute | solution.py:404
  40.3 4.7 %collective-permute-start.10 = (bf16[96,128]{1,0:T(8,128)(2,1)S(1)}, bf16[96,128]{1,0:T(8,128)(2,1)S(1)}, u32[]{:S(2)}, u32[]{:S(2)}) collective-permute-start(bf16[96,128]{1,0:T(8,128)(2,1)S(1)} %fusion), channel_id=1, source_target_pairs={{0,8},{1,9},{2,10},{3,11},{4,12},{5,13},{6,14},{7,15},{8,0},{9,1},... | collective-permute-start | bytes 73736 | tf_op jit(solution)/shard_map/ppermute | solution.py:404
  41.2 3.9 %collective-permute-start.13 = (f32[288,128]{1,0:T(8,128)S(1)}, f32[288,128]{1,0:T(8,128)S(1)}, u32[]{:S(2)}, u32[]{:S(2)}) collective-permute-start(f32[288,128]{1,0:T(8,128)S(1)} %get-tuple-element.97.own_out_ref), channel_id=1, source_target_pairs={{0,4},{1,5},{2,6},{3,7},{4,0},{5,1},{6,2},{7,3},{8,10},{9,11},{10,... | collective-permute-start | bytes 442376 | tf_op jit(solution)/shard_map/ppermute | solution.py:404
  45.2 4.7 %collective-permute-start.16 = (bf16[384,128]{1,0:T(8,128)(2,1)S(1)}, bf16[384,128]{1,0:T(8,128)(2,1)S(1)}, u32[]{:S(2)}, u32[]{:S(2)}) collective-permute-start(bf16[384,128]{1,0:T(8,128)(2,1)S(1)} %get-tuple-element.101), channel_id=1, source_target_pairs={{0,1},{1,0},{2,3},{3,2},{4,5},{5,4},{6,7},{7,6},{8,9},{9,8},{10,11... | collective-permute-start | bytes 294920 | tf_op jit(solution)/shard_map/ppermute | solution.py:404
  46.1 6.2 %collective-permute-start.17 = (bf16[384,128]{1,0:T(8,128)(2,1)S(1)}, bf16[384,128]{1,0:T(8,128)(2,1)S(1)}, u32[]{:S(2)}, u32[]{:S(2)}) collective-permute-start(bf16[384,128]{1,0:T(8,128)(2,1)S(1)} %get-tuple-element.102), channel_id=1, source_target_pairs={{0,2},{1,3},{2,0},{3,1},{4,6},{5,7},{6,4},{7,5},{8,10},{9,11},{10,... | collective-permute-start | bytes 294920 | tf_op jit(solution)/shard_map/ppermute | solution.py:404
  48.3 5.5 %collective-permute-start.18 = (bf16[384,128]{1,0:T(8,128)(2,1)S(1)}, bf16[384,128]{1,0:T(8,128)(2,1)S(1)}, u32[]{:S(2)}, u32[]{:S(2)}) collective-permute-start(bf16[384,128]{1,0:T(8,128)(2,1)S(1)} %get-tuple-element.103), channel_id=1, source_target_pairs={{0,3},{1,2},{2,1},{3,0},{4,7},{5,6},{6,5},{7,4},{8,11},{9,10},{10,... | collective-permute-start | bytes 294920 | tf_op jit(solution)/shard_map/ppermute | solution.py:404
  53.9 1.4 %collective-permute-start.19 = (bf16[384,128]{1,0:T(8,128)(2,1)S(1)}, bf16[384,128]{1,0:T(8,128)(2,1)S(1)}, u32[]{:S(2)}, u32[]{:S(2)}) collective-permute-start(bf16[384,128]{1,0:T(8,128)(2,1)S(1)} %join.1.mine_ref), channel_id=1, source_target_pairs={{0,4},{1,5},{2,6},{3,7},{4,0},{5,1},{6,2},{7,3},{8,12},{9,13},{10,... | collective-permute-start | bytes 294920 | tf_op jit(solution)/shard_map/ppermute | solution.py:404
  (3 other events, 2.5 us)

commit v5 on v4

--- a/solution.py
+++ b/solution.py
@@ -87,22 +87,19 @@
     row_len, col_len, width = sizes
     area = row_len * col_len
     row, core, col, step, pair = place(cols)
-    half = core if side < 2 else 1 - core
-    row_here = row
+    stays = pair == row >> 1
     if side:
-        row = 2 * pair + half
+        row = 2 * pair + (core if side == 1 else 1 - core)
     base = 2 * width if side else 0
-    outs = refs[-3:]
 
     def one(d):
         rows = rows_of(d, area)
         used = x_ref[rows, :]
         if side:
-            used = jnp.where(pair == row_here >> 1, home_ref[rows, :], used)
-            refs[-4][rows, :] = used
+            used = jnp.where(stays, home_ref[rows, :], used)
+            refs[0][rows, :] = used
         projected = dot(used, w_ref[:, base : base + 2 * width])
-        index = (half, d) if side else (d,)
-        project_block(projected, mask_ref, row, col ^ d, sizes, index, *outs)
+        project_block(projected, mask_ref, row, col ^ d, sizes, (d,), *refs[-3:])
 
     by_fours(cols, one)
 
@@ -140,35 +137,71 @@
     grad_ref[...] = dot_nt(low, wout_ref[...])
 
 
-def mix_kernel(cols, sizes, lv_ref, rv_ref, back_ref, low_ref, wide_ref, mixed_ref, grad_ref):
+def fold(parts):
+    spot = lax.broadcasted_iota(jnp.int32, parts[0].shape, 0)
+    shift = 1
+    while len(parts) > 1:
+        first = (spot & shift) == 0
+        parts = [
+            jnp.where(first, a, b) + pltpu.roll(jnp.where(first, b, a), shift, 0)
+            for a, b in zip(parts[::2], parts[1::2])
+        ]
+        shift *= 2
+    return parts[0]
+
+
+def block_of(row_len):
+    return next(n for n in (6, 4, 2) if row_len % n == 0)
+
+
+def mix_half(cols, sizes, lv_ref, rv_ref, mixed_ref):
+    row_len, col_len, width = sizes
+    groups = col_len // SEG
+    many = block_of(row_len)
+    zero = jnp.zeros((SEG, width), F32)
+
+    def rows(block, carry):
+        start = block * many
+        for jt in range(row_len // 4):
+
+            def over(q, acc):
+                for d in range(4):
+                    for g in range(groups):
+                        left = [lv_ref[4 * q + d, start + a, tile(g), :] for a in range(many)]
+                        right = [rv_ref[4 * q + d, 4 * jt + n, tile(g), :] for n in range(4)]
+                        acc = tuple(
+                            acc[4 * a + n] + left[a] * right[n] for a in range(many) for n in range(4)
+                        )
+                return acc
+
+            acc = (zero,) * (4 * many)
+            acc = over(0, acc) if cols == 4 else lax.fori_loop(0, cols // 4, over, acc)
+            for a in range(0, many, 2):
+                sums = fold(list(acc[4 * a : 4 * a + 8]))
+                mixed_ref[start + a, 4 * jt : 4 * jt + 4, :] = sums[:4]
+                mixed_ref[start + a + 1, 4 * jt : 4 * jt + 4, :] = sums[4:]
+        return carry
+
+    lax.fori_loop(0, row_len // many, rows, 0)
+
+
+def mix_own_kernel(cols, sizes, lv_ref, rv_ref, mixed_ref):
+    mix_half(cols, sizes, lv_ref, rv_ref, mixed_ref)
+
+
+def mix_kernel(
+    cols, sizes, lv_ref, rv_ref, own_ref, back_ref, low_ref, wide_ref, other_ref, grad_ref
+):
     row_len, col_len, width = sizes
     area = row_len * col_len
-    groups = col_len // SEG
-    zero = jnp.zeros((SEG, width), F32)
-
-    def mix_rows(pair_at, carry):
-        for jt in range(groups):
-
-            def over(d, acc):
-                for g in range(groups):
-                    left = [lv_ref[d, 2 * pair_at + a, tile(g), :] for a in range(2)]
-                    right = [
-                        rv_ref[j // row_len, d, j % row_len, tile(g), :]
-                        for j in range(jt * SEG, (jt + 1) * SEG)
-                    ]
-                    acc = tuple(acc[n] + left[n // SEG] * right[n % SEG] for n in range(2 * SEG))
-                return acc
-
-            acc = lax.fori_loop(0, cols, over, (zero,) * (2 * SEG))
-            for a in range(2):
-                mixed_ref[2 * pair_at + a, tile(jt), :] = jnp.concatenate(
-                    [jnp.sum(acc[a * SEG + n], axis=0, keepdims=True) for n in range(SEG)], axis=0
-                )
-        return carry
-
-    lax.fori_loop(0, row_len // 2, mix_rows, 0)
-
-    mixed_norm, mixed_scale = layer_norm(mixed_ref[...].reshape(area, width))
+    mix_half(cols, sizes, lv_ref, rv_ref, other_ref)
+    first = (lax.axis_index("row") & 1) == 0
+    for i in range(row_len):
+        own, other = own_ref[i], other_ref[i]
+        low, high = jnp.where(first, own, other), jnp.where(first, other, own)
+        grad_ref[i, :row_len, :] = low[:row_len]
+        grad_ref[i, row_len:, :] = high[:row_len]
+    mixed_norm, mixed_scale = layer_norm(grad_ref[...].reshape(area, width))
     low_ref[...] = mixed_norm.astype(BF16)
     grad_mixed = norm_back(back_ref[...], mixed_norm, mixed_scale)
     grad_ref[...] = grad_mixed.astype(BF16).astype(F32).reshape(row_len, col_len, width)
@@ -181,63 +214,80 @@
     lax.fori_loop(0, row_len, widen, 0)
 
 
-def gradient(load, count, first, sizes, a_ref, b_ref, index, d_ref, d_index):
+def gradient(load, count, many, first, sizes, a_ref, b_ref, d, d_ref):
     row_len, col_len, width = sizes
     groups = col_len // SEG
-    acc = [[jnp.zeros((SEG, width), F32)] * groups for _ in range(4)]
+    acc = [[jnp.zeros((SEG, width), F32)] * groups for _ in range(many)]
     for n in range(count):
         value, weights = load(n)
-        for a in range(4):
+        for a in range(many):
             for g in range(groups):
                 acc[a][g] = acc[a][g] + value[g] * weights[a]
-    full = [jnp.concatenate(acc[a], axis=0) for a in range(4)]
-    gates = [full[a] * a_ref[index + (first + a,)] for a in range(4)]
-    values = [full[a] * b_ref[index + (first + a,)] for a in range(4)]
-    d_ref[d_index + (slice(0, width),)] = jnp.concatenate(gates, axis=0).astype(BF16)
-    d_ref[d_index + (slice(width, 2 * width),)] = jnp.concatenate(values, axis=0).astype(BF16)
+    full = [jnp.concatenate(acc[a], axis=0) for a in range(many)]
+    gates = [full[a] * a_ref[d, first + a] for a in range(many)]
+    values = [full[a] * b_ref[d, first + a] for a in range(many)]
+    start = pl.multiple_of((d * row_len + first) * col_len, many * col_len)
+    rows = pl.ds(start, many * col_len)
+    d_ref[rows, :width] = jnp.concatenate(gates, axis=0).astype(BF16)
+    d_ref[rows, width:] = jnp.concatenate(values, axis=0).astype(BF16)
 
 
 def grads_kernel(
-    cols, sizes, lv_ref, la_ref, lb_ref, rv_ref, ra_ref, rb_ref, wide_ref, dl_ref, dr_ref
+    cols,
+    sizes,
+    lv_ref,
+    la_ref,
+    lb_ref,
+    ov_ref,
+    oa_ref,
+    ob_ref,
+    rv_ref,
+    ra_ref,
+    rb_ref,
+    wide_ref,
+    dl_ref,
+    do_ref,
+    dr_ref,
 ):
     row_len, col_len, width = sizes
-    area = row_len * col_len
     groups = col_len // SEG
-    quarter = 4 * col_len
-
-    def spot(d, b):
-        return pl.ds(pl.multiple_of(d * area + b * quarter, quarter), quarter)
-
-    for half in range(2):
-
-        def right_back(n, carry):
-            b, d = n // cols, n % cols
-
+    many = block_of(row_len)
+    core = lax.axis_index("row") & 1
+
+    def blocks(one):
+        def at(n, carry):
+            one(n // cols * many, n % cols)
+            return carry
+
+        lax.fori_loop(0, row_len // many * cols, at, 0)
+
+    def right_back(base, a_ref, b_ref, d_ref):
+        def one(first, d):
             def load(i):
                 return (
                     [lv_ref[d, i, tile(g), :] for g in range(groups)],
-                    [wide_ref[i, half * row_len + 4 * b + a] for a in range(4)],
+                    [wide_ref[i, base + first + a] for a in range(many)],
                 )
 
-            where = (half, spot(d, b))
-            gradient(load, row_len, 4 * b, sizes, ra_ref, rb_ref, (half, d), dr_ref, where)
-            return carry
-
-        lax.fori_loop(0, (row_len // 4) * cols, right_back, 0)
-
-    def left_back(n, carry):
-        b, d = n // cols, n % cols
-
-        def load(j):
+            gradient(load, row_len, many, first, sizes, a_ref, b_ref, d, d_ref)
+
+        blocks(one)
+
+    right_back(core * row_len, oa_ref, ob_ref, do_ref)
+    right_back((1 - core) * row_len, ra_ref, rb_ref, dr_ref)
+
+    def left_back(first, d):
+        def load(n):
+            ref = ov_ref if n < row_len else rv_ref
+            j = (core if n < row_len else 1 - core) * row_len + n % row_len
             return (
-                [rv_ref[j // row_len, d, j % row_len, tile(g), :] for g in range(groups)],
-                [wide_ref[4 * b + a, j] for a in range(4)],
+                [ref[d, n % row_len, tile(g), :] for g in range(groups)],
+                [wide_ref[first + a, j] for a in range(many)],
             )
 
-        gradient(load, col_len, 4 * b, sizes, la_ref, lb_ref, (d,), dl_ref, (spot(d, b),))
-        return carry
-
-    lax.fori_loop(0, (row_len // 4) * cols, left_back, 0)
+        gradient(load, col_len, many, first, sizes, la_ref, lb_ref, d, dl_ref)
+
+    blocks(left_back)
 
 
 def weight_sums_kernel(
@@ -248,6 +298,7 @@
     own_x_ref,
     other_x_ref,
     dl_ref,
+    do_ref,
     dr_ref,
     low_ref,
     gate_ref,
@@ -266,7 +317,7 @@
     grad_logit = (cot_ref[...] * update).astype(BF16)
     logit_ref[...] = grad_logit
     left_w = dot_tn(x_ref[...], dl_ref[...])
-    right_w = dot_tn(own_x_ref[...], dr_ref[core]) + dot_tn(other_x_ref[...], dr_ref[1 - core])
+    right_w = dot_tn(own_x_ref[...], do_ref[...]) + dot_tn(other_x_ref[...], dr_ref[...])
     sum_ref[0, :width, :] = left_w[:, :width]
     sum_ref[0, width : 2 * width, :] = left_w[:, width:]
     sum_ref[0, 2 * width :, :] = right_w[:, :width]
@@ -277,13 +328,10 @@
     keep_ref[...] = sum_ref[core]
 
 
-def back_right_kernel(cols, area, width, other, dr_ref, w_ref, part_ref):
-    core = lax.axis_index("row") & 1
-    half = 1 - core if other else core
-
+def back_right_kernel(cols, area, width, dr_ref, w_ref, part_ref):
     def back(d):
         rows = rows_of(d, area)
-        part = dot_nt(dr_ref[half, rows, :], w_ref[:, 2 * width : 4 * width])
+        part = dot_nt(dr_ref[rows, :], w_ref[:, 2 * width : 4 * width])
         part_ref[rows, :] = part.astype(part_ref.dtype)
 
     by_fours(cols, back)
@@ -314,7 +362,7 @@
         chunk_refs[d - 1][...] = sum_ref[col ^ d].astype(BF16)
 
 
-def row_sum_kernel(cols, area, gx_ref, got_ref, y_ref, chunk_ref, own_ref, *send_refs):
+def row_sum_kernel(cols, area, gx_ref, got_ref, y_ref, own_ref, *part_refs):
     row, core, col, step, pair = place(cols)
     stays = pair == row >> 1
 
@@ -324,8 +372,18 @@
 
     own_ref[...] = total(0)
     for d in range(1, cols):
-        send_refs[d - 1][:area, :] = total(d).astype(BF16)
-        send_refs[d - 1][area:, :] = chunk_ref[...]
+        part_refs[d - 1][...] = total(d).astype(BF16)
+
+
+def pack_kernel(cols, area, chunk_ref, *refs):
+    for d in range(cols - 1):
+        refs[cols - 1 + d][:area, :] = refs[d][...]
+        refs[cols - 1 + d][area:, :] = chunk_ref[...]
+
+
+def home_kernel(cols, own_ref, got_ref, out_ref):
+    row, core, col, step, pair = place(cols)
+    out_ref[...] = jnp.where(step == 0, own_ref[...], got_ref[...])
 
 
 def join_kernel(cols, area, chunk_ref, *rest):
@@ -337,10 +395,8 @@
     half_ref[...] = order_ref[...].reshape(half_ref.shape).astype(BF16)
 
 
-def pair_grad_kernel(cols, area, own_ref, pair_ref, home_ref, own_out_ref, *rest):
-    got_refs, (grad_ref, out_ref) = rest[:-2], rest[-2:]
-    row, core, col, step, pair = place(cols)
-    out_ref[...] = jnp.where(step == 0, own_out_ref[...], home_ref[...])
+def pair_grad_kernel(area, own_ref, pair_ref, *rest):
+    got_refs, grad_ref = rest[:-1], rest[-1]
     total = own_ref[...]
     for got in got_refs:
         total = total + got[:area, :].astype(F32)
@@ -359,7 +415,7 @@
     out_ref[...] = high[2 * width :]
 
 
-def call(kernel, name, micros, out_shape, args, scratch=(), aliases=None, space=pltpu.VMEM):
+def call(kernel, name, micros, out_shape, args, scratch=(), space=pltpu.VMEM):
     specs = [pl.BlockSpec(memory_space=space) for _ in args]
     total = sum(_bytes(ref) for ref in [*args, *out_shape, *scratch])
     return pl.pallas_call(
@@ -368,7 +424,6 @@
         in_specs=specs,
         out_specs=tuple(pl.BlockSpec(memory_space=pltpu.VMEM) for _ in out_shape),
         scratch_shapes=list(scratch),
-        input_output_aliases=aliases or {},
         cost_estimate=pl.CostEstimate(
             flops=0, transcendentals=0, bytes_accessed=int(micros * 3_690_000)
         ),
@@ -447,37 +502,43 @@
     )
     left, back, got_x = lax.optimization_barrier((left, back, got_x))
     swapped_x = swap(got_x)
-    right_shape = [like(tall, width, dtype=BF16)] + [like(2, cols, row_len, col_len, width)] * 3
-    own_x, *right = call(
+    right_shape = [like(tall, width, dtype=BF16)] + [like(cols, row_len, col_len, width)] * 3
+    own_x, *own = call(
         functools.partial(project_kernel, 1, cols, sizes),
         "right_own",
-        0.9,
+        0.4,
         right_shape,
         [mask, got_x, x, proj_weight],
     )
+    (mixed_own,) = call(
+        functools.partial(mix_own_kernel, cols, sizes),
+        "mix_own",
+        0.7,
+        [like(row_len, 2 * SEG * (-(-row_len // (2 * SEG))), width)],
+        [left[0], own[0]],
+    )
+    swapped_x, mixed_own = lax.optimization_barrier((swapped_x, mixed_own))
     other_x, *right = call(
         functools.partial(project_kernel, 2, cols, sizes),
         "right_other",
-        0.9,
+        0.4,
         right_shape,
-        [mask, swapped_x, got_x, proj_weight, *right],
-        aliases={4: 1, 5: 2, 6: 3},
-    )
-    flat = pltpu.VMEM((row_len, col_len, width), F32)
+        [mask, swapped_x, got_x, proj_weight],
+    )
     mixed_low, wide = call(
         functools.partial(mix_kernel, cols, sizes),
         "mix",
-        1.8,
+        1.2,
         [like(area, width, dtype=BF16), like(row_len, col_len, SEG, width)],
-        [left[0], right[0], back],
-        [flat, flat],
-    )
-    dl, dr = call(
+        [left[0], right[0], mixed_own, back],
+        [pltpu.VMEM(mixed_own.shape, F32), pltpu.VMEM((row_len, col_len, width), F32)],
+    )
+    dl, do, dr = call(
         functools.partial(grads_kernel, cols, sizes),
         "grads",
-        3.0,
-        [like(tall, 2 * width, dtype=BF16), like(2, tall, 2 * width, dtype=BF16)],
-        [*left, *right, wide],
+        2.5,
+        [like(tall, 2 * width, dtype=BF16)] * 3,
+        [*left, *own, *right, wide],
     )
     send_w, keep_w, pair_out, grad_logit = call(
         functools.partial(weight_sums_kernel, cols, area, width),
@@ -489,13 +550,13 @@
             like(area, width),
             like(area, width, dtype=BF16),
         ],
-        [x, own_x, other_x, dl, dr, mixed_low, out_gate, cot, update_low, out_weight],
+        [x, own_x, other_x, dl, do, dr, mixed_low, out_gate, cot, update_low, out_weight],
         [pltpu.VMEM((2, half, width), F32)],
     )
     got_w = swap(send_w)
     dr, send_w = lax.optimization_barrier((dr, send_w))
     (send_y,) = call(
-        functools.partial(back_right_kernel, cols, area, width, True),
+        functools.partial(back_right_kernel, cols, area, width),
         "back_other",
         0.3,
         [like(tall, width, dtype=BF16)],
@@ -510,13 +571,13 @@
         [keep_w, got_w],
         [pltpu.VMEM((cols, chunk, width), F32)],
     )
-    dr, dl, mine = lax.optimization_barrier((dr, dl, mine))
+    do, dl, mine = lax.optimization_barrier((do, dl, mine))
     (keep_y,) = call(
-        functools.partial(back_right_kernel, cols, area, width, False),
+        functools.partial(back_right_kernel, cols, area, width),
         "back_own",
         0.3,
         [like(tall, width)],
-        [dr, proj_weight],
+        [do, proj_weight],
     )
     (y,) = call(core_sum_kernel, "core_sum", 0.1, [like(tall, width, dtype=BF16)], [keep_y, got_y])
     back_y = permute(y, lambda z, core, col: (col ^ flip(z, cols), core, col))
@@ -532,18 +593,30 @@
     low_mine = mine.astype(BF16)
     low_mine, pair_out, gx = lax.optimization_barrier((low_mine, pair_out, gx))
     home = to_pair(pair_out)
-    for d in range(1, cols):
-        mine = mine + across(low_mine, d).astype(F32)
-    low_mine = mine.astype(BF16)
-    low_mine, home = lax.optimization_barrier((low_mine, home))
-    own, *sends = call(
+    rest, *parts = call(
         functools.partial(row_sum_kernel, cols, area),
         "row_sum",
+        4.0,
+        [like(area, width)] + [like(area, width, dtype=BF16)] * (cols - 1),
+        [gx, back_y, y],
+    )
+    planes_got = [across(low_mine, d) for d in range(1, cols)]
+    *planes_got, rest, home = lax.optimization_barrier((*planes_got, rest, home))
+    for got in planes_got:
+        mine = mine + got.astype(F32)
+    low_mine = mine.astype(BF16)
+    sends = call(
+        functools.partial(pack_kernel, cols, area),
+        "pack",
         0.1,
-        [like(area, width)] + [like(area + chunk, width, dtype=BF16)] * (cols - 1),
-        [gx, back_y, y, low_mine],
+        [like(area + chunk, width, dtype=BF16)] * (cols - 1),
+        [low_mine, *parts],
     )
     gets = [in_plane(sends[d - 1], d) for d in range(1, cols)]
+    (pair_out,) = call(
+        functools.partial(home_kernel, cols), "home", 0.6, [like(area, width)], [pair_out, home]
+    )
+    pair_out, *gets = lax.optimization_barrier((pair_out, *gets))
     (half_w,) = call(
         functools.partial(join_kernel, cols, area),
         "join",
@@ -553,13 +626,13 @@
         [pltpu.VMEM((cols, chunk, width), F32)],
     )
     other_w = swap(half_w)
-    half_w, own = lax.optimization_barrier((half_w, own))
-    pair_grad, pair_out = call(
-        functools.partial(pair_grad_kernel, cols, area),
+    half_w, rest = lax.optimization_barrier((half_w, rest))
+    (pair_grad,) = call(
+        functools.partial(pair_grad_kernel, area),
         "pair_grad",
         1.0,
-        [like(area, width)] * 2,
-        [own, pair, home, pair_out, *gets],
+        [like(area, width)],
+        [rest, pair, *gets],
     )
     proj_grad, out_grad = call(
         functools.partial(weights_kernel, width),

time: 56.2 us -> 55.4 us (0.986)
  waiting for transfers between devices: 19.8 us -> 18.8 us
    ppermute x20, waiting for transfers between devices: 19.8 us -> 18.8 us  [permute(): return lax.ppermute(value, ('row', 'col'), pairs)]
    pallas_call x18 -> x21, Pallas kernels: 10.5 us -> 10.6 us  [call(): pl.pallas_call(kernel, out_shape=tuple(out_shape), in_specs=specs, out_sp...]
  transfers between devices with their start and end apart: 20 -> 20, of which waited for: 13 -> 13; matrix products, arithmetic and copies ran while one was open for 0% -> 0% of each run, Pallas kernels for 6% -> 8%
where the time goes in v5:
time: 55.4 us; the launch traced here: 55.2 us
  starting transfers between devices  22.4 us (40%)
  waiting for transfers between devices  18.8 us (34%)
  Pallas kernels  10.6 us (19%)
  local copies, waits for them, and re-layouts  2.49 us (4%)
  between operations  0.89 us (2%)
    ppermute x20, starting transfers between devices, permute(): return lax.ppermute(value, ('row', 'col'), pairs)  22.4 us
    ppermute x20, waiting for transfers between devices, permute(): return lax.ppermute(value, ('row', 'col'), pairs)  18.8 us
    pallas_call x21, Pallas kernels, call(): pl.pallas_call(kernel, out_shape=tuple(out_shape), in_specs=specs, out_sp...  10.6 us
    unnamed x14, local copies, waits for them, and re-layouts  2.49 us
  transfers between devices with their start and end apart: 20, of which 13 were waited for; matrix products, arithmetic and copies ran while one was open for 0% of the time, Pallas kernels for 8%

profile of v5, /device:TPU:0, one launch (start us, length us, event | category | flops | bytes accessed | tf_op | source)
XLA Modules:
  0.0 55.2 jit_solution(16249528877182426370)
XLA Ops:
  0.6 0.9 %copy-done.2 = f32[12,24,128]{2,1,0:T(8,128)S(1)} copy-done((f32[12,24,128]{2,1,0:T(8,128)S(1)}, f32[12,24,128]{2,1,0:T(8,128)}, u32[]{:S(2)}) %copy-start.2) | copy-done | bytes 147480
  1.8 4.0 %collective-permute-start.2 = (bf16[288,128]{1,0:T(8,128)(2,1)S(1)}, bf16[288,128]{1,0:T(8,128)(2,1)S(1)}, u32[]{:S(2)}, u32[]{:S(2)}) collective-permute-start(bf16[288,128]{1,0:T(8,128)(2,1)S(1)} %norm.1), channel_id=1, source_target_pairs={{0,3},{1,2},{2,1},{3,0},{4,7},{5,6},{6,5},{7,4},{8,11},{9,10},{10,... | collective-permute-start | bytes 221192 | tf_op jit(solution)/shard_map/ppermute | solution.py:459
  6.4 1.7 %collective-permute-done.2 = bf16[288,128]{1,0:T(8,128)(2,1)S(1)} collective-permute-done((bf16[288,128]{1,0:T(8,128)(2,1)S(1)}, bf16[288,128]{1,0:T(8,128)(2,1)S(1)}, u32[]{:S(2)}, u32[]{:S(2)}) %collective-permute-start.2) | collective-permute-done | bytes 73760 | tf_op jit(solution)/shard_map/ppermute | solution.py:459
  8.1 2.0 %collective-permute-done.1 = bf16[288,128]{1,0:T(8,128)(2,1)S(1)} collective-permute-done((bf16[288,128]{1,0:T(8,128)(2,1)S(1)}, bf16[288,128]{1,0:T(8,128)(2,1)S(1)}, u32[]{:S(2)}, u32[]{:S(2)}) %collective-permute-start.1) | collective-permute-done | bytes 73760 | tf_op jit(solution)/shard_map/ppermute | solution.py:459
  11.2 0.7 %copy-done.6 = s32[12]{0:T(128)S(1)} copy-done((s32[12]{0:T(128)S(1)}, s32[12]{0:T(128)}, u32[]{:S(2)}) %copy-start.6) | copy-done | bytes 72
  12.4 0.9 %copy-done = bf16[128,640]{1,0:T(8,128)(2,1)S(1)} copy-done((bf16[128,640]{1,0:T(8,128)(2,1)S(1)}, bf16[128,640]{1,0:T(8,128)(2,1)}, u32[]{:S(2)}) %copy-start) | copy-done | bytes 163864
  16.0 1.0 %mix.1 = (bf16[288,128]{1,0:T(8,128)(2,1)S(1)}, f32[12,24,8,128]{3,2,1,0:T(8,128)S(1)}) custom-call(f32[4,12,24,128]{3,2,1,0:T(8,128)S(1)} %get-tuple-element.76.lv_ref, f32[4,12,24,128]{3,2,1,0:T(8,128)S(1)} %get-tuple-element.84.rv_ref, f32[12,16,128]{2,1,0:T(8,128)S(1)} %mix_own.1.own_ref, f32[288,128]{1,0:T(8,128)S(1)} %get-tuple-element.88.back_ref), custom_call_target="tpu_custom_call" | custom-call | bytes 4428000 | tf_op jit(solution)/shard_map/mix/pallas_call | solution.py:421
  17.0 2.7 %grads.1 = (bf16[1152,256]{1,0:T(8,128)(2,1)S(1)}, bf16[1152,256]{1,0:T(8,128)(2,1)S(1)}, bf16[1152,256]{1,0:T(8,128)(2,1)S(1)}) custom-call(f32[4,12,24,128]{3,2,1,0:T(8,128)S(1)} %get-tuple-element.76.lv_ref, f32[4,12,24,128]{3,2,1,0:T(8,128)S(1)} %get-tuple-element.77.la_ref, f32[4,12,24,128]{3,2,1,0:T(8,128)S(1)} %get-tuple-element.78.lb_ref, ...), custom_call_target="tpu_custom_call" | custom-call | bytes 9225000 | tf_op jit(solution)/shard_map/grads/pallas_call | solution.py:421
  21.2 1.2 %collective-permute-done.6.got_ref = bf16[384,128]{1,0:T(8,128)(2,1)S(1)} collective-permute-done((bf16[384,128]{1,0:T(8,128)(2,1)S(1)}, bf16[384,128]{1,0:T(8,128)(2,1)S(1)}, u32[]{:S(2)}, u32[]{:S(2)}) %collective-permute-start.6) | collective-permute-done | bytes 98336 | tf_op jit(solution)/shard_map/ppermute | solution.py:459
  22.5 5.9 %collective-permute-start.7 = (bf16[96,128]{1,0:T(8,128)(2,1)S(1)}, bf16[96,128]{1,0:T(8,128)(2,1)S(1)}, u32[]{:S(2)}, u32[]{:S(2)}) collective-permute-start(bf16[96,128]{1,0:T(8,128)(2,1)S(1)} %get-tuple-element.103), channel_id=1, source_target_pairs={{0,1},{1,0},{2,3},{3,2},{4,5},{5,4},{6,7},{7,6},{8,9},{9,8},{10,11... | collective-permute-start | bytes 73736 | tf_op jit(solution)/shard_map/ppermute | solution.py:459
  28.3 2.4 %collective-permute-start.8 = (bf16[96,128]{1,0:T(8,128)(2,1)S(1)}, bf16[96,128]{1,0:T(8,128)(2,1)S(1)}, u32[]{:S(2)}, u32[]{:S(2)}) collective-permute-start(bf16[96,128]{1,0:T(8,128)(2,1)S(1)} %get-tuple-element.104), channel_id=1, source_target_pairs={{0,2},{1,3},{2,0},{3,1},{4,6},{5,7},{6,4},{7,5},{8,10},{9,11},{10,... | collective-permute-start | bytes 73736 | tf_op jit(solution)/shard_map/ppermute | solution.py:459
  31.6 1.0 %collective-permute-done.8 = bf16[96,128]{1,0:T(8,128)(2,1)S(1)} collective-permute-done((bf16[96,128]{1,0:T(8,128)(2,1)S(1)}, bf16[96,128]{1,0:T(8,128)(2,1)S(1)}, u32[]{:S(2)}, u32[]{:S(2)}) %collective-permute-start.8) | collective-permute-done | bytes 24608 | tf_op jit(solution)/shard_map/ppermute | solution.py:459
  32.6 2.9 %collective-permute-done.9 = bf16[96,128]{1,0:T(8,128)(2,1)S(1)} collective-permute-done((bf16[96,128]{1,0:T(8,128)(2,1)S(1)}, bf16[96,128]{1,0:T(8,128)(2,1)S(1)}, u32[]{:S(2)}, u32[]{:S(2)}) %collective-permute-start.9) | collective-permute-done | bytes 24608 | tf_op jit(solution)/shard_map/ppermute | solution.py:459
  35.6 3.6 %collective-permute-start.12 = (bf16[96,128]{1,0:T(8,128)(2,1)S(1)}, bf16[96,128]{1,0:T(8,128)(2,1)S(1)}, u32[]{:S(2)}, u32[]{:S(2)}) collective-permute-start(bf16[96,128]{1,0:T(8,128)(2,1)S(1)} %fusion), channel_id=1, source_target_pairs={{0,24},{1,25},{2,26},{3,27},{4,28},{5,29},{6,30},{7,31},{8,16},{9,... | collective-permute-start | bytes 73736 | tf_op jit(solution)/shard_map/ppermute | solution.py:459
  39.2 0.8 %collective-permute-start.10 = (bf16[96,128]{1,0:T(8,128)(2,1)S(1)}, bf16[96,128]{1,0:T(8,128)(2,1)S(1)}, u32[]{:S(2)}, u32[]{:S(2)}) collective-permute-start(bf16[96,128]{1,0:T(8,128)(2,1)S(1)} %fusion), channel_id=1, source_target_pairs={{0,8},{1,9},{2,10},{3,11},{4,12},{5,13},{6,14},{7,15},{8,0},{9,1},... | collective-permute-start | bytes 73736 | tf_op jit(solution)/shard_map/ppermute | solution.py:459
  40.2 1.2 %collective-permute-done.12 = bf16[96,128]{1,0:T(8,128)(2,1)S(1)} collective-permute-done((bf16[96,128]{1,0:T(8,128)(2,1)S(1)}, bf16[96,128]{1,0:T(8,128)(2,1)S(1)}, u32[]{:S(2)}, u32[]{:S(2)}) %collective-permute-start.12) | collective-permute-done | bytes 24608 | tf_op jit(solution)/shard_map/ppermute | solution.py:459
  41.4 2.5 %collective-permute-done.11 = bf16[96,128]{1,0:T(8,128)(2,1)S(1)} collective-permute-done((bf16[96,128]{1,0:T(8,128)(2,1)S(1)}, bf16[96,128]{1,0:T(8,128)(2,1)S(1)}, u32[]{:S(2)}, u32[]{:S(2)}) %collective-permute-start.11) | collective-permute-done | bytes 24608 | tf_op jit(solution)/shard_map/ppermute | solution.py:459
  44.0 1.5 %collective-permute-start.16 = (bf16[384,128]{1,0:T(8,128)(2,1)S(1)}, bf16[384,128]{1,0:T(8,128)(2,1)S(1)}, u32[]{:S(2)}, u32[]{:S(2)}) collective-permute-start(bf16[384,128]{1,0:T(8,128)(2,1)S(1)} %get-tuple-element.122), channel_id=1, source_target_pairs={{0,1},{1,0},{2,3},{3,2},{4,5},{5,4},{6,7},{7,6},{8,9},{9,8},{10,11... | collective-permute-start | bytes 294920 | tf_op jit(solution)/shard_map/ppermute | solution.py:459
  45.5 2.0 %collective-permute-start.17 = (bf16[384,128]{1,0:T(8,128)(2,1)S(1)}, bf16[384,128]{1,0:T(8,128)(2,1)S(1)}, u32[]{:S(2)}, u32[]{:S(2)}) collective-permute-start(bf16[384,128]{1,0:T(8,128)(2,1)S(1)} %get-tuple-element.123), channel_id=1, source_target_pairs={{0,2},{1,3},{2,0},{3,1},{4,6},{5,7},{6,4},{7,5},{8,10},{9,11},{10,... | collective-permute-start | bytes 294920 | tf_op jit(solution)/shard_map/ppermute | solution.py:459
  47.6 0.7 %home.1 = f32[288,128]{1,0:T(8,128)} custom-call(f32[288,128]{1,0:T(8,128)S(1)} %get-tuple-element.109.own_ref, f32[288,128]{1,0:T(8,128)S(1)} %collective-permute-done.15.got_ref), custom_call_target="tpu_custom_call" | custom-call | bytes 2214000 | tf_op jit(solution)/shard_map/home/pallas_call | solution.py:421
  48.8 2.1 %collective-permute-done.17.rest_1_ = bf16[384,128]{1,0:T(8,128)(2,1)S(1)} collective-permute-done((bf16[384,128]{1,0:T(8,128)(2,1)S(1)}, bf16[384,128]{1,0:T(8,128)(2,1)S(1)}, u32[]{:S(2)}, u32[]{:S(2)}) %collective-permute-start.17) | collective-permute-done | bytes 98336 | tf_op jit(solution)/shard_map/ppermute | solution.py:459
  51.0 2.1 %collective-permute-done.18.rest_2_ = bf16[384,128]{1,0:T(8,128)(2,1)S(1)} collective-permute-done((bf16[384,128]{1,0:T(8,128)(2,1)S(1)}, bf16[384,128]{1,0:T(8,128)(2,1)S(1)}, u32[]{:S(2)}, u32[]{:S(2)}) %collective-permute-start.18) | collective-permute-done | bytes 98336 | tf_op jit(solution)/shard_map/ppermute | solution.py:459
  53.2 0.9 %pair_grad.1 = f32[288,128]{1,0:T(8,128)} custom-call(f32[288,128]{1,0:T(8,128)S(1)} %get-tuple-element.130.own_ref, f32[288,128]{1,0:T(8,128)S(1)} %bitcast.5, bf16[384,128]{1,0:T(8,128)(2,1)S(1)} %collective-permute-done.16.rest_0_, bf16[384,128]{1,0:T(8,128)(2,1)S(1)} %collective-permute-done.17.rest_1_, bf16[384,128]{1,0:T(8,128)(2,1)S(1)} %collective-permute-done.18.rest_2_), custom_call_target="tpu_custom_call" | custom-call | bytes 3690000 | tf_op jit(solution)/shard_map/pair_grad/pallas_call | solution.py:421
  54.4 0.8 %weights.1 = (f32[128,640]{1,0:T(8,128)}, f32[128,128]{1,0:T(8,128)}) custom-call(bf16[384,128]{1,0:T(8,128)(2,1)S(1)} %join.1.mine_ref, bf16[384,128]{1,0:T(8,128)(2,1)S(1)} %collective-permute-done.19.other_ref), custom_call_target="tpu_custom_call" | custom-call | bytes 2952000 | tf_op jit(solution)/shard_map/weights/pallas_call | solution.py:421
  (54 shorter events, 8.8 us)
Async XLA Ops:
  1.5 12.1 %copy-start.4 = (f32[12,24,128]{2,1,0:T(8,128)S(1)}, f32[12,24,128]{2,1,0:T(8,128)}, u32[]{:S(2)}) copy-start(f32[12,24,128]{2,1,0:T(8,128)} %param.9) | copy-start | bytes 442372
  1.5 12.1 %copy-start.5 = (bf16[128,128]{1,0:T(8,128)(2,1)S(1)}, bf16[128,128]{1,0:T(8,128)(2,1)}, u32[]{:S(2)}) copy-start(bf16[128,128]{1,0:T(8,128)(2,1)} %wout_ref.3) | copy-start | bytes 98308
  1.5 12.6 %copy-start.1 = (bf16[128,640]{1,0:T(8,128)(2,1)S(1)}, bf16[128,640]{1,0:T(8,128)(2,1)}, u32[]{:S(2)}) copy-start(bf16[128,640]{1,0:T(8,128)(2,1)} %w_ref.13) | copy-start | bytes 491524
  1.8 6.3 %collective-permute-start.2 = (bf16[288,128]{1,0:T(8,128)(2,1)S(1)}, bf16[288,128]{1,0:T(8,128)(2,1)S(1)}, u32[]{:S(2)}, u32[]{:S(2)}) collective-permute-start(bf16[288,128]{1,0:T(8,128)(2,1)S(1)} %norm.1), channel_id=1, source_target_pairs={{0,3},{1,2},{2,1},{3,0},{4,7},{5,6},{6,5},{7,4},{8,11},{9,10},{10,... | collective-permute-start | bytes 221192 | tf_op jit(solution)/shard_map/ppermute | solution.py:459
  5.7 4.4 %collective-permute-start.1 = (bf16[288,128]{1,0:T(8,128)(2,1)S(1)}, bf16[288,128]{1,0:T(8,128)(2,1)S(1)}, u32[]{:S(2)}, u32[]{:S(2)}) collective-permute-start(bf16[288,128]{1,0:T(8,128)(2,1)S(1)} %norm.1), channel_id=1, source_target_pairs={{0,2},{1,3},{2,0},{3,1},{4,6},{5,7},{6,4},{7,5},{8,10},{9,11},{10,... | collective-permute-start | bytes 221192 | tf_op jit(solution)/shard_map/ppermute | solution.py:459
  6.2 4.4 %collective-permute-start = (bf16[288,128]{1,0:T(8,128)(2,1)S(1)}, bf16[288,128]{1,0:T(8,128)(2,1)S(1)}, u32[]{:S(2)}, u32[]{:S(2)}) collective-permute-start(bf16[288,128]{1,0:T(8,128)(2,1)S(1)} %norm.1), channel_id=1, source_target_pairs={{0,1},{1,0},{2,3},{3,2},{4,5},{5,4},{6,7},{7,6},{8,9},{9,8},{10,11... | collective-permute-start | bytes 221192 | tf_op jit(solution)/shard_map/ppermute | solution.py:459
  10.6 3.4 %collective-permute-start.4 = (bf16[1152,128]{1,0:T(8,128)(2,1)S(1)}, bf16[1152,128]{1,0:T(8,128)(2,1)S(1)}, u32[]{:S(2)}, u32[]{:S(2)}) collective-permute-start(bf16[1152,128]{1,0:T(8,128)(2,1)S(1)} %pad_maximum_fusion.x_ref.home_ref), channel_id=1, source_target_pairs={{0,4},{1,17},{2,10},{3,27},{4,0},{5,21},{6,14},{7,31},{8,16},{9,1}... | collective-permute-start | bytes 884744 | tf_op jit(solution)/shard_map/ppermute | solution.py:459
  10.7 3.0 %collective-permute-start.3 = (f32[288,128]{1,0:T(8,128)}, f32[288,128]{1,0:T(8,128)S(1)}, u32[]{:S(2)}, u32[]{:S(2)}) collective-permute-start(f32[288,128]{1,0:T(8,128)} %bitcast.6), channel_id=1, source_target_pairs={{0,4},{1,5},{2,6},{3,7},{4,0},{5,1},{6,2},{7,3},{8,10},{9,11},{10,... | collective-permute-start | bytes 442376 | tf_op jit(solution)/shard_map/ppermute | solution.py:459
  14.0 1.6 %collective-permute-start.5 = (bf16[1152,128]{1,0:T(8,128)(2,1)S(1)}, bf16[1152,128]{1,0:T(8,128)(2,1)S(1)}, u32[]{:S(2)}, u32[]{:S(2)}) collective-permute-start(bf16[1152,128]{1,0:T(8,128)(2,1)S(1)} %collective-permute-done.4.x_ref.home_ref), channel_id=1, source_target_pairs={{0,4},{1,5},{2,6},{3,7},{4,0},{5,1},{6,2},{7,3},{8,12},{9,13},{10,... | collective-permute-start | bytes 884744 | tf_op jit(solution)/shard_map/ppermute | solution.py:459
  20.6 10.8 %collective-permute-start.13 = (bf16[1152,128]{1,0:T(8,128)(2,1)S(1)}, bf16[1152,128]{1,0:T(8,128)(2,1)S(1)}, u32[]{:S(2)}, u32[]{:S(2)}) collective-permute-start(bf16[1152,128]{1,0:T(8,128)(2,1)S(1)} %back_other.1), channel_id=1, source_target_pairs={{0,4},{1,5},{2,6},{3,7},{4,0},{5,1},{6,2},{7,3},{8,12},{9,13},{10,... | collective-permute-start | bytes 884744 | tf_op jit(solution)/shard_map/ppermute | solution.py:459
  20.8 1.6 %collective-permute-start.6 = (bf16[384,128]{1,0:T(8,128)(2,1)S(1)}, bf16[384,128]{1,0:T(8,128)(2,1)S(1)}, u32[]{:S(2)}, u32[]{:S(2)}) collective-permute-start(bf16[384,128]{1,0:T(8,128)(2,1)S(1)} %get-tuple-element.100), channel_id=1, source_target_pairs={{0,4},{1,5},{2,6},{3,7},{4,0},{5,1},{6,2},{7,3},{8,12},{9,13},{10,... | collective-permute-start | bytes 294920 | tf_op jit(solution)/shard_map/ppermute | solution.py:459
  22.5 9.1 %collective-permute-start.7 = (bf16[96,128]{1,0:T(8,128)(2,1)S(1)}, bf16[96,128]{1,0:T(8,128)(2,1)S(1)}, u32[]{:S(2)}, u32[]{:S(2)}) collective-permute-start(bf16[96,128]{1,0:T(8,128)(2,1)S(1)} %get-tuple-element.103), channel_id=1, source_target_pairs={{0,1},{1,0},{2,3},{3,2},{4,5},{5,4},{6,7},{7,6},{8,9},{9,8},{10,11... | collective-permute-start | bytes 73736 | tf_op jit(solution)/shard_map/ppermute | solution.py:459
  28.3 4.2 %collective-permute-start.8 = (bf16[96,128]{1,0:T(8,128)(2,1)S(1)}, bf16[96,128]{1,0:T(8,128)(2,1)S(1)}, u32[]{:S(2)}, u32[]{:S(2)}) collective-permute-start(bf16[96,128]{1,0:T(8,128)(2,1)S(1)} %get-tuple-element.104), channel_id=1, source_target_pairs={{0,2},{1,3},{2,0},{3,1},{4,6},{5,7},{6,4},{7,5},{8,10},{9,11},{10,... | collective-permute-start | bytes 73736 | tf_op jit(solution)/shard_map/ppermute | solution.py:459
  30.8 4.7 %collective-permute-start.9 = (bf16[96,128]{1,0:T(8,128)(2,1)S(1)}, bf16[96,128]{1,0:T(8,128)(2,1)S(1)}, u32[]{:S(2)}, u32[]{:S(2)}) collective-permute-start(bf16[96,128]{1,0:T(8,128)(2,1)S(1)} %get-tuple-element.105), channel_id=1, source_target_pairs={{0,3},{1,2},{2,1},{3,0},{4,7},{5,6},{6,5},{7,4},{8,11},{9,10},{10,... | collective-permute-start | bytes 73736 | tf_op jit(solution)/shard_map/ppermute | solution.py:459
  31.5 8.6 %collective-permute-start.14 = (bf16[1152,128]{1,0:T(8,128)(2,1)S(1)}, bf16[1152,128]{1,0:T(8,128)(2,1)S(1)}, u32[]{:S(2)}, u32[]{:S(2)}) collective-permute-start(bf16[1152,128]{1,0:T(8,128)(2,1)S(1)} %core_sum.1.y_ref), channel_id=1, source_target_pairs={{0,4},{1,9},{2,18},{3,27},{4,0},{5,13},{6,22},{7,31},{8,16},{9,25}... | collective-permute-start | bytes 884744 | tf_op jit(solution)/shard_map/ppermute | solution.py:459
  35.5 17.6 %copy-start.3 = (f32[12,24,128]{2,1,0:T(8,128)S(1)}, f32[12,24,128]{2,1,0:T(8,128)}, u32[]{:S(2)}) copy-start(f32[12,24,128]{2,1,0:T(8,128)} %param.5) | copy-start | bytes 442372
  35.5 8.4 %collective-permute-start.15 = (f32[288,128]{1,0:T(8,128)S(1)}, f32[288,128]{1,0:T(8,128)S(1)}, u32[]{:S(2)}, u32[]{:S(2)}) collective-permute-start(f32[288,128]{1,0:T(8,128)S(1)} %get-tuple-element.109.own_ref), channel_id=1, source_target_pairs={{0,4},{1,5},{2,6},{3,7},{4,0},{5,1},{6,2},{7,3},{8,10},{9,11},{10,... | collective-permute-start | bytes 442376 | tf_op jit(solution)/shard_map/ppermute | solution.py:459
  35.6 5.8 %collective-permute-start.12 = (bf16[96,128]{1,0:T(8,128)(2,1)S(1)}, bf16[96,128]{1,0:T(8,128)(2,1)S(1)}, u32[]{:S(2)}, u32[]{:S(2)}) collective-permute-start(bf16[96,128]{1,0:T(8,128)(2,1)S(1)} %fusion), channel_id=1, source_target_pairs={{0,24},{1,25},{2,26},{3,27},{4,28},{5,29},{6,30},{7,31},{8,16},{9,... | collective-permute-start | bytes 73736 | tf_op jit(solution)/shard_map/ppermute | solution.py:459
  39.2 4.7 %collective-permute-start.11 = (bf16[96,128]{1,0:T(8,128)(2,1)S(1)}, bf16[96,128]{1,0:T(8,128)(2,1)S(1)}, u32[]{:S(2)}, u32[]{:S(2)}) collective-permute-start(bf16[96,128]{1,0:T(8,128)(2,1)S(1)} %fusion), channel_id=1, source_target_pairs={{0,16},{1,17},{2,18},{3,19},{4,20},{5,21},{6,22},{7,23},{8,24},{9,... | collective-permute-start | bytes 73736 | tf_op jit(solution)/shard_map/ppermute | solution.py:459
  39.2 4.7 %collective-permute-start.10 = (bf16[96,128]{1,0:T(8,128)(2,1)S(1)}, bf16[96,128]{1,0:T(8,128)(2,1)S(1)}, u32[]{:S(2)}, u32[]{:S(2)}) collective-permute-start(bf16[96,128]{1,0:T(8,128)(2,1)S(1)} %fusion), channel_id=1, source_target_pairs={{0,8},{1,9},{2,10},{3,11},{4,12},{5,13},{6,14},{7,15},{8,0},{9,1},... | collective-permute-start | bytes 73736 | tf_op jit(solution)/shard_map/ppermute | solution.py:459
  44.0 4.8 %collective-permute-start.16 = (bf16[384,128]{1,0:T(8,128)(2,1)S(1)}, bf16[384,128]{1,0:T(8,128)(2,1)S(1)}, u32[]{:S(2)}, u32[]{:S(2)}) collective-permute-start(bf16[384,128]{1,0:T(8,128)(2,1)S(1)} %get-tuple-element.122), channel_id=1, source_target_pairs={{0,1},{1,0},{2,3},{3,2},{4,5},{5,4},{6,7},{7,6},{8,9},{9,8},{10,11... | collective-permute-start | bytes 294920 | tf_op jit(solution)/shard_map/ppermute | solution.py:459
  45.5 5.5 %collective-permute-start.17 = (bf16[384,128]{1,0:T(8,128)(2,1)S(1)}, bf16[384,128]{1,0:T(8,128)(2,1)S(1)}, u32[]{:S(2)}, u32[]{:S(2)}) collective-permute-start(bf16[384,128]{1,0:T(8,128)(2,1)S(1)} %get-tuple-element.123), channel_id=1, source_target_pairs={{0,2},{1,3},{2,0},{3,1},{4,6},{5,7},{6,4},{7,5},{8,10},{9,11},{10,... | collective-permute-start | bytes 294920 | tf_op jit(solution)/shard_map/ppermute | solution.py:459
  47.5 5.5 %collective-permute-start.18 = (bf16[384,128]{1,0:T(8,128)(2,1)S(1)}, bf16[384,128]{1,0:T(8,128)(2,1)S(1)}, u32[]{:S(2)}, u32[]{:S(2)}) collective-permute-start(bf16[384,128]{1,0:T(8,128)(2,1)S(1)} %get-tuple-element.124), channel_id=1, source_target_pairs={{0,3},{1,2},{2,1},{3,0},{4,7},{5,6},{6,5},{7,4},{8,11},{9,10},{10,... | collective-permute-start | bytes 294920 | tf_op jit(solution)/shard_map/ppermute | solution.py:459
  53.1 1.4 %collective-permute-start.19 = (bf16[384,128]{1,0:T(8,128)(2,1)S(1)}, bf16[384,128]{1,0:T(8,128)(2,1)S(1)}, u32[]{:S(2)}, u32[]{:S(2)}) collective-permute-start(bf16[384,128]{1,0:T(8,128)(2,1)S(1)} %join.1.mine_ref), channel_id=1, source_target_pairs={{0,4},{1,5},{2,6},{3,7},{4,0},{5,1},{6,2},{7,3},{8,12},{9,13},{10,... | collective-permute-start | bytes 294920 | tf_op jit(solution)/shard_map/ppermute | solution.py:459
  (3 other events, 2.5 us)

commit v6 on v5

--- a/solution.py
+++ b/solution.py
@@ -554,7 +554,6 @@
         [pltpu.VMEM((2, half, width), F32)],
     )
     got_w = swap(send_w)
-    dr, send_w = lax.optimization_barrier((dr, send_w))
     (send_y,) = call(
         functools.partial(back_right_kernel, cols, area, width),
         "back_other",
@@ -571,7 +570,7 @@
         [keep_w, got_w],
         [pltpu.VMEM((cols, chunk, width), F32)],
     )
-    do, dl, mine = lax.optimization_barrier((do, dl, mine))
+    dl, mine = lax.optimization_barrier((dl, mine))
     (keep_y,) = call(
         functools.partial(back_right_kernel, cols, area, width),
         "back_own",
@@ -591,8 +590,8 @@
     for d in range(1, cols):
         mine = mine + in_plane(chunks[d - 1], d).astype(F32)
     low_mine = mine.astype(BF16)
-    low_mine, pair_out, gx = lax.optimization_barrier((low_mine, pair_out, gx))
     home = to_pair(pair_out)
+    back_y, home = lax.optimization_barrier((back_y, home))
     rest, *parts = call(
         functools.partial(row_sum_kernel, cols, area),
         "row_sum",
@@ -601,7 +600,7 @@
         [gx, back_y, y],
     )
     planes_got = [across(low_mine, d) for d in range(1, cols)]
-    *planes_got, rest, home = lax.optimization_barrier((*planes_got, rest, home))
+    *planes_got, rest = lax.optimization_barrier((*planes_got, rest))
     for got in planes_got:
         mine = mine + got.astype(F32)
     low_mine = mine.astype(BF16)

time: 55.4 us -> 53.3 us (0.962)
  waiting for transfers between devices: 18.8 us -> 13.4 us
  starting transfers between devices: 22.4 us -> 25.7 us
    ppermute x20, waiting for transfers between devices: 18.8 us -> 13.4 us  [permute(): return lax.ppermute(value, ('row', 'col'), pairs)]
    ppermute x20, starting transfers between devices: 22.4 us -> 25.7 us  [permute(): return lax.ppermute(value, ('row', 'col'), pairs)]
  transfers between devices with their start and end apart: 20 -> 20, of which waited for: 13 -> 14; matrix products, arithmetic and copies ran while one was open for 0% -> 0% of each run, Pallas kernels for 8% -> 10%
where the time goes in v6:
time: 53.3 us; the launch traced here: 53.1 us
  starting transfers between devices  25.7 us (48%)
  waiting for transfers between devices  13.4 us (25%)
  Pallas kernels  10.6 us (20%)
  local copies, waits for them, and re-layouts  2.49 us (5%)
  between operations  0.87 us (2%)
    ppermute x20, starting transfers between devices, permute(): return lax.ppermute(value, ('row', 'col'), pairs)  25.7 us
    ppermute x20, waiting for transfers between devices, permute(): return lax.ppermute(value, ('row', 'col'), pairs)  13.4 us
    pallas_call x21, Pallas kernels, call(): pl.pallas_call(kernel, out_shape=tuple(out_shape), in_specs=specs, out_sp...  10.6 us
    unnamed x14, local copies, waits for them, and re-layouts  2.49 us
  transfers between devices with their start and end apart: 20, of which 14 were waited for; matrix products, arithmetic and copies ran while one was open for 0% of the time, Pallas kernels for 10%

profile of v6, /device:TPU:0, one launch (start us, length us, event | category | flops | bytes accessed | tf_op | source)
XLA Modules:
  0.0 53.1 jit_solution(16275166271313552551)
XLA Ops:
  0.6 0.9 %copy-done.2 = f32[12,24,128]{2,1,0:T(8,128)S(1)} copy-done((f32[12,24,128]{2,1,0:T(8,128)S(1)}, f32[12,24,128]{2,1,0:T(8,128)}, u32[]{:S(2)}) %copy-start.2) | copy-done | bytes 147480
  1.8 4.0 %collective-permute-start.2 = (bf16[288,128]{1,0:T(8,128)(2,1)S(1)}, bf16[288,128]{1,0:T(8,128)(2,1)S(1)}, u32[]{:S(2)}, u32[]{:S(2)}) collective-permute-start(bf16[288,128]{1,0:T(8,128)(2,1)S(1)} %norm.1), channel_id=1, source_target_pairs={{0,3},{1,2},{2,1},{3,0},{4,7},{5,6},{6,5},{7,4},{8,11},{9,10},{10,... | collective-permute-start | bytes 221192 | tf_op jit(solution)/shard_map/ppermute | solution.py:459
  6.4 1.7 %collective-permute-done.2 = bf16[288,128]{1,0:T(8,128)(2,1)S(1)} collective-permute-done((bf16[288,128]{1,0:T(8,128)(2,1)S(1)}, bf16[288,128]{1,0:T(8,128)(2,1)S(1)}, u32[]{:S(2)}, u32[]{:S(2)}) %collective-permute-start.2) | collective-permute-done | bytes 73760 | tf_op jit(solution)/shard_map/ppermute | solution.py:459
  8.1 2.0 %collective-permute-done.1 = bf16[288,128]{1,0:T(8,128)(2,1)S(1)} collective-permute-done((bf16[288,128]{1,0:T(8,128)(2,1)S(1)}, bf16[288,128]{1,0:T(8,128)(2,1)S(1)}, u32[]{:S(2)}, u32[]{:S(2)}) %collective-permute-start.1) | collective-permute-done | bytes 73760 | tf_op jit(solution)/shard_map/ppermute | solution.py:459
  11.2 0.7 %copy-done.6 = s32[12]{0:T(128)S(1)} copy-done((s32[12]{0:T(128)S(1)}, s32[12]{0:T(128)}, u32[]{:S(2)}) %copy-start.6) | copy-done | bytes 72
  11.8 0.5 %mask.1.mask_ref = f32[96,128]{1,0:T(8,128)S(1)} custom-call(s32[12]{0:T(128)S(1)} %copy-done.6), custom_call_target="tpu_custom_call" | custom-call | bytes 369000 | tf_op jit(solution)/shard_map/mask/pallas_call | solution.py:421
  12.4 0.9 %copy-done = bf16[128,640]{1,0:T(8,128)(2,1)S(1)} copy-done((bf16[128,640]{1,0:T(8,128)(2,1)S(1)}, bf16[128,640]{1,0:T(8,128)(2,1)}, u32[]{:S(2)}) %copy-start) | copy-done | bytes 163864
  14.5 0.5 %mix_own.1.own_ref = f32[12,16,128]{2,1,0:T(8,128)S(1)} custom-call(f32[4,12,24,128]{3,2,1,0:T(8,128)S(1)} %get-tuple-element.74.lv_ref, f32[4,12,24,128]{3,2,1,0:T(8,128)S(1)} %get-tuple-element.75.rv_ref.ov_ref), custom_call_target="tpu_custom_call" | custom-call | bytes 2583000 | tf_op jit(solution)/shard_map/mix_own/pallas_call | solution.py:421
  15.1 0.6 %collective-permute-done.5.x_ref = bf16[1152,128]{1,0:T(8,128)(2,1)S(1)} collective-permute-done((bf16[1152,128]{1,0:T(8,128)(2,1)S(1)}, bf16[1152,128]{1,0:T(8,128)(2,1)S(1)}, u32[]{:S(2)}, u32[]{:S(2)}) %collective-permute-start.5) | collective-permute-done | bytes 294944 | tf_op jit(solution)/shard_map/ppermute | solution.py:459
  16.0 1.0 %mix.1 = (bf16[288,128]{1,0:T(8,128)(2,1)S(1)}, f32[12,24,8,128]{3,2,1,0:T(8,128)S(1)}) custom-call(f32[4,12,24,128]{3,2,1,0:T(8,128)S(1)} %get-tuple-element.74.lv_ref, f32[4,12,24,128]{3,2,1,0:T(8,128)S(1)} %get-tuple-element.82.rv_ref, f32[12,16,128]{2,1,0:T(8,128)S(1)} %mix_own.1.own_ref, f32[288,128]{1,0:T(8,128)S(1)} %get-tuple-element.86.back_ref), custom_call_target="tpu_custom_call" | custom-call | bytes 4428000 | tf_op jit(solution)/shard_map/mix/pallas_call | solution.py:421
  17.0 2.7 %grads.1 = (bf16[1152,256]{1,0:T(8,128)(2,1)S(1)}, bf16[1152,256]{1,0:T(8,128)(2,1)S(1)}, bf16[1152,256]{1,0:T(8,128)(2,1)S(1)}) custom-call(f32[4,12,24,128]{3,2,1,0:T(8,128)S(1)} %get-tuple-element.74.lv_ref, f32[4,12,24,128]{3,2,1,0:T(8,128)S(1)} %get-tuple-element.78.la_ref, f32[4,12,24,128]{3,2,1,0:T(8,128)S(1)} %get-tuple-element.79.lb_ref, ...), custom_call_target="tpu_custom_call" | custom-call | bytes 9225000 | tf_op jit(solution)/shard_map/grads/pallas_call | solution.py:421
  20.2 0.6 %weight_sums.1 = (bf16[384,128]{1,0:T(8,128)(2,1)S(1)}, f32[384,128]{1,0:T(8,128)S(1)}, f32[288,128]{1,0:T(8,128)S(1)}, bf16[288,128]{1,0:T(8,128)(2,1)S(1)}) custom-call(bf16[1152,128]{1,0:T(8,128)(2,1)S(1)} %pad_maximum_fusion.x_ref.home_ref, bf16[1152,128]{1,0:T(8,128)(2,1)S(1)} %get-tuple-element.73.own_x_ref, ...), custom_call_target="tpu_custom_call" | custom-call | bytes 2214000 | tf_op jit(solution)/shard_map/weight_sums/pallas_call | solution.py:421
  22.2 7.9 %collective-permute-start.10 = (bf16[96,128]{1,0:T(8,128)(2,1)S(1)}, bf16[96,128]{1,0:T(8,128)(2,1)S(1)}, u32[]{:S(2)}, u32[]{:S(2)}) collective-permute-start(bf16[96,128]{1,0:T(8,128)(2,1)S(1)} %get-tuple-element.101), channel_id=1, source_target_pairs={{0,1},{1,0},{2,3},{3,2},{4,5},{5,4},{6,7},{7,6},{8,9},{9,8},{10,11... | collective-permute-start | bytes 73736 | tf_op jit(solution)/shard_map/ppermute | solution.py:459
  30.1 3.6 %collective-permute-start.11 = (bf16[96,128]{1,0:T(8,128)(2,1)S(1)}, bf16[96,128]{1,0:T(8,128)(2,1)S(1)}, u32[]{:S(2)}, u32[]{:S(2)}) collective-permute-start(bf16[96,128]{1,0:T(8,128)(2,1)S(1)} %get-tuple-element.102), channel_id=1, source_target_pairs={{0,2},{1,3},{2,0},{3,1},{4,6},{5,7},{6,4},{7,5},{8,10},{9,11},{10,... | collective-permute-start | bytes 73736 | tf_op jit(solution)/shard_map/ppermute | solution.py:459
  33.7 1.8 %collective-permute-done.11 = bf16[96,128]{1,0:T(8,128)(2,1)S(1)} collective-permute-done((bf16[96,128]{1,0:T(8,128)(2,1)S(1)}, bf16[96,128]{1,0:T(8,128)(2,1)S(1)}, u32[]{:S(2)}, u32[]{:S(2)}) %collective-permute-start.11) | collective-permute-done | bytes 24608 | tf_op jit(solution)/shard_map/ppermute | solution.py:459
  35.5 2.9 %collective-permute-done.12 = bf16[96,128]{1,0:T(8,128)(2,1)S(1)} collective-permute-done((bf16[96,128]{1,0:T(8,128)(2,1)S(1)}, bf16[96,128]{1,0:T(8,128)(2,1)S(1)}, u32[]{:S(2)}, u32[]{:S(2)}) %collective-permute-start.12) | collective-permute-done | bytes 24608 | tf_op jit(solution)/shard_map/ppermute | solution.py:459
  38.5 0.8 %collective-permute-start.15 = (bf16[96,128]{1,0:T(8,128)(2,1)S(1)}, bf16[96,128]{1,0:T(8,128)(2,1)S(1)}, u32[]{:S(2)}, u32[]{:S(2)}) collective-permute-start(bf16[96,128]{1,0:T(8,128)(2,1)S(1)} %fusion), channel_id=1, source_target_pairs={{0,24},{1,25},{2,26},{3,27},{4,28},{5,29},{6,30},{7,31},{8,16},{9,... | collective-permute-start | bytes 73736 | tf_op jit(solution)/shard_map/ppermute | solution.py:459
  39.2 3.7 %collective-permute-start.13 = (bf16[96,128]{1,0:T(8,128)(2,1)S(1)}, bf16[96,128]{1,0:T(8,128)(2,1)S(1)}, u32[]{:S(2)}, u32[]{:S(2)}) collective-permute-start(bf16[96,128]{1,0:T(8,128)(2,1)S(1)} %fusion), channel_id=1, source_target_pairs={{0,8},{1,9},{2,10},{3,11},{4,12},{5,13},{6,14},{7,15},{8,0},{9,1},... | collective-permute-start | bytes 73736 | tf_op jit(solution)/shard_map/ppermute | solution.py:459
  43.4 0.8 %collective-permute-done.15 = bf16[96,128]{1,0:T(8,128)(2,1)S(1)} collective-permute-done((bf16[96,128]{1,0:T(8,128)(2,1)S(1)}, bf16[96,128]{1,0:T(8,128)(2,1)S(1)}, u32[]{:S(2)}, u32[]{:S(2)}) %collective-permute-start.15) | collective-permute-done | bytes 24608 | tf_op jit(solution)/shard_map/ppermute | solution.py:459
  45.4 2.9 %collective-permute-start.18 = (bf16[384,128]{1,0:T(8,128)(2,1)S(1)}, bf16[384,128]{1,0:T(8,128)(2,1)S(1)}, u32[]{:S(2)}, u32[]{:S(2)}) collective-permute-start(bf16[384,128]{1,0:T(8,128)(2,1)S(1)} %get-tuple-element.116), channel_id=1, source_target_pairs={{0,3},{1,2},{2,1},{3,0},{4,7},{5,6},{6,5},{7,4},{8,11},{9,10},{10,... | collective-permute-start | bytes 294920 | tf_op jit(solution)/shard_map/ppermute | solution.py:459
  48.4 0.7 %home.1 = f32[288,128]{1,0:T(8,128)} custom-call(f32[288,128]{1,0:T(8,128)S(1)} %get-tuple-element.95.own_ref, f32[288,128]{1,0:T(8,128)S(1)} %collective-permute-done.8.got_ref), custom_call_target="tpu_custom_call" | custom-call | bytes 2214000 | tf_op jit(solution)/shard_map/home/pallas_call | solution.py:421
  49.8 1.2 %collective-permute-done.18.rest_2_ = bf16[384,128]{1,0:T(8,128)(2,1)S(1)} collective-permute-done((bf16[384,128]{1,0:T(8,128)(2,1)S(1)}, bf16[384,128]{1,0:T(8,128)(2,1)S(1)}, u32[]{:S(2)}, u32[]{:S(2)}) %collective-permute-start.18) | collective-permute-done | bytes 98336 | tf_op jit(solution)/shard_map/ppermute | solution.py:459
  51.1 0.9 %pair_grad.1 = f32[288,128]{1,0:T(8,128)} custom-call(f32[288,128]{1,0:T(8,128)S(1)} %get-tuple-element.122.own_ref, f32[288,128]{1,0:T(8,128)S(1)} %bitcast.5, bf16[384,128]{1,0:T(8,128)(2,1)S(1)} %collective-permute-done.16.rest_0_, bf16[384,128]{1,0:T(8,128)(2,1)S(1)} %collective-permute-done.17.rest_1_, bf16[384,128]{1,0:T(8,128)(2,1)S(1)} %collective-permute-done.18.rest_2_), custom_call_target="tpu_custom_call" | custom-call | bytes 3690000 | tf_op jit(solution)/shard_map/pair_grad/pallas_call | solution.py:421
  52.4 0.8 %weights.1 = (f32[128,640]{1,0:T(8,128)}, f32[128,128]{1,0:T(8,128)}) custom-call(bf16[384,128]{1,0:T(8,128)(2,1)S(1)} %join.1.mine_ref, bf16[384,128]{1,0:T(8,128)(2,1)S(1)} %collective-permute-done.19.other_ref), custom_call_target="tpu_custom_call" | custom-call | bytes 2952000 | tf_op jit(solution)/shard_map/weights/pallas_call | solution.py:421
  (54 shorter events, 8.2 us)
Async XLA Ops:
  1.5 12.1 %copy-start.4 = (f32[12,24,128]{2,1,0:T(8,128)S(1)}, f32[12,24,128]{2,1,0:T(8,128)}, u32[]{:S(2)}) copy-start(f32[12,24,128]{2,1,0:T(8,128)} %param.9) | copy-start | bytes 442372
  1.5 12.1 %copy-start.5 = (bf16[128,128]{1,0:T(8,128)(2,1)S(1)}, bf16[128,128]{1,0:T(8,128)(2,1)}, u32[]{:S(2)}) copy-start(bf16[128,128]{1,0:T(8,128)(2,1)} %wout_ref.3) | copy-start | bytes 98308
  1.5 12.6 %copy-start.1 = (bf16[128,640]{1,0:T(8,128)(2,1)S(1)}, bf16[128,640]{1,0:T(8,128)(2,1)}, u32[]{:S(2)}) copy-start(bf16[128,640]{1,0:T(8,128)(2,1)} %w_ref.13) | copy-start | bytes 491524
  1.8 6.3 %collective-permute-start.2 = (bf16[288,128]{1,0:T(8,128)(2,1)S(1)}, bf16[288,128]{1,0:T(8,128)(2,1)S(1)}, u32[]{:S(2)}, u32[]{:S(2)}) collective-permute-start(bf16[288,128]{1,0:T(8,128)(2,1)S(1)} %norm.1), channel_id=1, source_target_pairs={{0,3},{1,2},{2,1},{3,0},{4,7},{5,6},{6,5},{7,4},{8,11},{9,10},{10,... | collective-permute-start | bytes 221192 | tf_op jit(solution)/shard_map/ppermute | solution.py:459
  5.7 4.4 %collective-permute-start.1 = (bf16[288,128]{1,0:T(8,128)(2,1)S(1)}, bf16[288,128]{1,0:T(8,128)(2,1)S(1)}, u32[]{:S(2)}, u32[]{:S(2)}) collective-permute-start(bf16[288,128]{1,0:T(8,128)(2,1)S(1)} %norm.1), channel_id=1, source_target_pairs={{0,2},{1,3},{2,0},{3,1},{4,6},{5,7},{6,4},{7,5},{8,10},{9,11},{10,... | collective-permute-start | bytes 221192 | tf_op jit(solution)/shard_map/ppermute | solution.py:459
  6.2 4.4 %collective-permute-start = (bf16[288,128]{1,0:T(8,128)(2,1)S(1)}, bf16[288,128]{1,0:T(8,128)(2,1)S(1)}, u32[]{:S(2)}, u32[]{:S(2)}) collective-permute-start(bf16[288,128]{1,0:T(8,128)(2,1)S(1)} %norm.1), channel_id=1, source_target_pairs={{0,1},{1,0},{2,3},{3,2},{4,5},{5,4},{6,7},{7,6},{8,9},{9,8},{10,11... | collective-permute-start | bytes 221192 | tf_op jit(solution)/shard_map/ppermute | solution.py:459
  10.6 3.4 %collective-permute-start.4 = (bf16[1152,128]{1,0:T(8,128)(2,1)S(1)}, bf16[1152,128]{1,0:T(8,128)(2,1)S(1)}, u32[]{:S(2)}, u32[]{:S(2)}) collective-permute-start(bf16[1152,128]{1,0:T(8,128)(2,1)S(1)} %pad_maximum_fusion.x_ref.home_ref), channel_id=1, source_target_pairs={{0,4},{1,17},{2,10},{3,27},{4,0},{5,21},{6,14},{7,31},{8,16},{9,1}... | collective-permute-start | bytes 884744 | tf_op jit(solution)/shard_map/ppermute | solution.py:459
  10.7 3.0 %collective-permute-start.3 = (f32[288,128]{1,0:T(8,128)}, f32[288,128]{1,0:T(8,128)S(1)}, u32[]{:S(2)}, u32[]{:S(2)}) collective-permute-start(f32[288,128]{1,0:T(8,128)} %bitcast.6), channel_id=1, source_target_pairs={{0,4},{1,5},{2,6},{3,7},{4,0},{5,1},{6,2},{7,3},{8,10},{9,11},{10,... | collective-permute-start | bytes 442376 | tf_op jit(solution)/shard_map/ppermute | solution.py:459
  14.0 1.6 %collective-permute-start.5 = (bf16[1152,128]{1,0:T(8,128)(2,1)S(1)}, bf16[1152,128]{1,0:T(8,128)(2,1)S(1)}, u32[]{:S(2)}, u32[]{:S(2)}) collective-permute-start(bf16[1152,128]{1,0:T(8,128)(2,1)S(1)} %collective-permute-done.4.x_ref.home_ref), channel_id=1, source_target_pairs={{0,4},{1,5},{2,6},{3,7},{4,0},{5,1},{6,2},{7,3},{8,12},{9,13},{10,... | collective-permute-start | bytes 884744 | tf_op jit(solution)/shard_map/ppermute | solution.py:459
  20.0 1.6 %collective-permute-start.6 = (bf16[1152,128]{1,0:T(8,128)(2,1)S(1)}, bf16[1152,128]{1,0:T(8,128)(2,1)S(1)}, u32[]{:S(2)}, u32[]{:S(2)}) collective-permute-start(bf16[1152,128]{1,0:T(8,128)(2,1)S(1)} %back_other.1), channel_id=1, source_target_pairs={{0,4},{1,5},{2,6},{3,7},{4,0},{5,1},{6,2},{7,3},{8,12},{9,13},{10,... | collective-permute-start | bytes 884744 | tf_op jit(solution)/shard_map/ppermute | solution.py:459
  20.8 1.4 %collective-permute-start.9 = (bf16[384,128]{1,0:T(8,128)(2,1)S(1)}, bf16[384,128]{1,0:T(8,128)(2,1)S(1)}, u32[]{:S(2)}, u32[]{:S(2)}) collective-permute-start(bf16[384,128]{1,0:T(8,128)(2,1)S(1)} %get-tuple-element.98), channel_id=1, source_target_pairs={{0,4},{1,5},{2,6},{3,7},{4,0},{5,1},{6,2},{7,3},{8,12},{9,13},{10,... | collective-permute-start | bytes 294920 | tf_op jit(solution)/shard_map/ppermute | solution.py:459
  21.8 21.5 %collective-permute-start.7 = (bf16[1152,128]{1,0:T(8,128)(2,1)S(1)}, bf16[1152,128]{1,0:T(8,128)(2,1)S(1)}, u32[]{:S(2)}, u32[]{:S(2)}) collective-permute-start(bf16[1152,128]{1,0:T(8,128)(2,1)S(1)} %core_sum.1.y_ref), channel_id=1, source_target_pairs={{0,4},{1,9},{2,18},{3,27},{4,0},{5,13},{6,22},{7,31},{8,16},{9,25}... | collective-permute-start | bytes 884744 | tf_op jit(solution)/shard_map/ppermute | solution.py:459
  22.2 11.5 %collective-permute-start.10 = (bf16[96,128]{1,0:T(8,128)(2,1)S(1)}, bf16[96,128]{1,0:T(8,128)(2,1)S(1)}, u32[]{:S(2)}, u32[]{:S(2)}) collective-permute-start(bf16[96,128]{1,0:T(8,128)(2,1)S(1)} %get-tuple-element.101), channel_id=1, source_target_pairs={{0,1},{1,0},{2,3},{3,2},{4,5},{5,4},{6,7},{7,6},{8,9},{9,8},{10,11... | collective-permute-start | bytes 73736 | tf_op jit(solution)/shard_map/ppermute | solution.py:459
  30.1 5.4 %collective-permute-start.11 = (bf16[96,128]{1,0:T(8,128)(2,1)S(1)}, bf16[96,128]{1,0:T(8,128)(2,1)S(1)}, u32[]{:S(2)}, u32[]{:S(2)}) collective-permute-start(bf16[96,128]{1,0:T(8,128)(2,1)S(1)} %get-tuple-element.102), channel_id=1, source_target_pairs={{0,2},{1,3},{2,0},{3,1},{4,6},{5,7},{6,4},{7,5},{8,10},{9,11},{10,... | collective-permute-start | bytes 73736 | tf_op jit(solution)/shard_map/ppermute | solution.py:459
  33.7 4.7 %collective-permute-start.12 = (bf16[96,128]{1,0:T(8,128)(2,1)S(1)}, bf16[96,128]{1,0:T(8,128)(2,1)S(1)}, u32[]{:S(2)}, u32[]{:S(2)}) collective-permute-start(bf16[96,128]{1,0:T(8,128)(2,1)S(1)} %get-tuple-element.103), channel_id=1, source_target_pairs={{0,3},{1,2},{2,1},{3,0},{4,7},{5,6},{6,5},{7,4},{8,11},{9,10},{10,... | collective-permute-start | bytes 73736 | tf_op jit(solution)/shard_map/ppermute | solution.py:459
  33.7 9.6 %collective-permute-start.8 = (f32[288,128]{1,0:T(8,128)S(1)}, f32[288,128]{1,0:T(8,128)S(1)}, u32[]{:S(2)}, u32[]{:S(2)}) collective-permute-start(f32[288,128]{1,0:T(8,128)S(1)} %get-tuple-element.95.own_ref), channel_id=1, source_target_pairs={{0,4},{1,5},{2,6},{3,7},{4,0},{5,1},{6,2},{7,3},{8,10},{9,11},{10,... | collective-permute-start | bytes 442376 | tf_op jit(solution)/shard_map/ppermute | solution.py:459
  38.5 5.8 %collective-permute-start.15 = (bf16[96,128]{1,0:T(8,128)(2,1)S(1)}, bf16[96,128]{1,0:T(8,128)(2,1)S(1)}, u32[]{:S(2)}, u32[]{:S(2)}) collective-permute-start(bf16[96,128]{1,0:T(8,128)(2,1)S(1)} %fusion), channel_id=1, source_target_pairs={{0,24},{1,25},{2,26},{3,27},{4,28},{5,29},{6,30},{7,31},{8,16},{9,... | collective-permute-start | bytes 73736 | tf_op jit(solution)/shard_map/ppermute | solution.py:459
  39.2 5.0 %collective-permute-start.14 = (bf16[96,128]{1,0:T(8,128)(2,1)S(1)}, bf16[96,128]{1,0:T(8,128)(2,1)S(1)}, u32[]{:S(2)}, u32[]{:S(2)}) collective-permute-start(bf16[96,128]{1,0:T(8,128)(2,1)S(1)} %fusion), channel_id=1, source_target_pairs={{0,16},{1,17},{2,18},{3,19},{4,20},{5,21},{6,22},{7,23},{8,24},{9,... | collective-permute-start | bytes 73736 | tf_op jit(solution)/shard_map/ppermute | solution.py:459
  39.2 5.5 %collective-permute-start.13 = (bf16[96,128]{1,0:T(8,128)(2,1)S(1)}, bf16[96,128]{1,0:T(8,128)(2,1)S(1)}, u32[]{:S(2)}, u32[]{:S(2)}) collective-permute-start(bf16[96,128]{1,0:T(8,128)(2,1)S(1)} %fusion), channel_id=1, source_target_pairs={{0,8},{1,9},{2,10},{3,11},{4,12},{5,13},{6,14},{7,15},{8,0},{9,1},... | collective-permute-start | bytes 73736 | tf_op jit(solution)/shard_map/ppermute | solution.py:459
  43.3 7.8 %copy-start.3 = (f32[12,24,128]{2,1,0:T(8,128)S(1)}, f32[12,24,128]{2,1,0:T(8,128)}, u32[]{:S(2)}) copy-start(f32[12,24,128]{2,1,0:T(8,128)} %param.5) | copy-start | bytes 442372
  44.8 4.7 %collective-permute-start.16 = (bf16[384,128]{1,0:T(8,128)(2,1)S(1)}, bf16[384,128]{1,0:T(8,128)(2,1)S(1)}, u32[]{:S(2)}, u32[]{:S(2)}) collective-permute-start(bf16[384,128]{1,0:T(8,128)(2,1)S(1)} %get-tuple-element.114), channel_id=1, source_target_pairs={{0,1},{1,0},{2,3},{3,2},{4,5},{5,4},{6,7},{7,6},{8,9},{9,8},{10,11... | collective-permute-start | bytes 294920 | tf_op jit(solution)/shard_map/ppermute | solution.py:459
  45.2 4.6 %collective-permute-start.17 = (bf16[384,128]{1,0:T(8,128)(2,1)S(1)}, bf16[384,128]{1,0:T(8,128)(2,1)S(1)}, u32[]{:S(2)}, u32[]{:S(2)}) collective-permute-start(bf16[384,128]{1,0:T(8,128)(2,1)S(1)} %get-tuple-element.115), channel_id=1, source_target_pairs={{0,2},{1,3},{2,0},{3,1},{4,6},{5,7},{6,4},{7,5},{8,10},{9,11},{10,... | collective-permute-start | bytes 294920 | tf_op jit(solution)/shard_map/ppermute | solution.py:459
  45.4 5.5 %collective-permute-start.18 = (bf16[384,128]{1,0:T(8,128)(2,1)S(1)}, bf16[384,128]{1,0:T(8,128)(2,1)S(1)}, u32[]{:S(2)}, u32[]{:S(2)}) collective-permute-start(bf16[384,128]{1,0:T(8,128)(2,1)S(1)} %get-tuple-element.116), channel_id=1, source_target_pairs={{0,3},{1,2},{2,1},{3,0},{4,7},{5,6},{6,5},{7,4},{8,11},{9,10},{10,... | collective-permute-start | bytes 294920 | tf_op jit(solution)/shard_map/ppermute | solution.py:459
  51.0 1.4 %collective-permute-start.19 = (bf16[384,128]{1,0:T(8,128)(2,1)S(1)}, bf16[384,128]{1,0:T(8,128)(2,1)S(1)}, u32[]{:S(2)}, u32[]{:S(2)}) collective-permute-start(bf16[384,128]{1,0:T(8,128)(2,1)S(1)} %join.1.mine_ref), channel_id=1, source_target_pairs={{0,4},{1,5},{2,6},{3,7},{4,0},{5,1},{6,2},{7,3},{8,12},{9,13},{10,... | collective-permute-start | bytes 294920 | tf_op jit(solution)/shard_map/ppermute | solution.py:459
  (3 other events, 2.5 us)

commit v7 on v6

--- a/solution.py
+++ b/solution.py
@@ -151,7 +151,7 @@
 
 
 def block_of(row_len):
-    return next(n for n in (6, 4, 2) if row_len % n == 0)
+    return next(n for n in (4, 2) if row_len % n == 0)
 
 
 def mix_half(cols, sizes, lv_ref, rv_ref, mixed_ref):
@@ -160,8 +160,7 @@
     many = block_of(row_len)
     zero = jnp.zeros((SEG, width), F32)
 
-    def rows(block, carry):
-        start = block * many
+    for start in range(0, row_len, many):
         for jt in range(row_len // 4):
 
             def over(q, acc):
@@ -180,9 +179,6 @@
                 sums = fold(list(acc[4 * a : 4 * a + 8]))
                 mixed_ref[start + a, 4 * jt : 4 * jt + 4, :] = sums[:4]
                 mixed_ref[start + a + 1, 4 * jt : 4 * jt + 4, :] = sums[4:]
-        return carry
-
-    lax.fori_loop(0, row_len // many, rows, 0)
 
 
 def mix_own_kernel(cols, sizes, lv_ref, rv_ref, mixed_ref):
@@ -206,12 +202,9 @@
     grad_mixed = norm_back(back_ref[...], mixed_norm, mixed_scale)
     grad_ref[...] = grad_mixed.astype(BF16).astype(F32).reshape(row_len, col_len, width)
 
-    def widen(i, carry):
+    for i in range(row_len):
         for j in range(col_len):
             wide_ref[i, j] = jnp.broadcast_to(grad_ref[i, j : j + 1, :], (SEG, width))
-        return carry
-
-    lax.fori_loop(0, row_len, widen, 0)
 
 
 def gradient(load, count, many, first, sizes, a_ref, b_ref, d, d_ref):
@@ -226,8 +219,8 @@
     full = [jnp.concatenate(acc[a], axis=0) for a in range(many)]
     gates = [full[a] * a_ref[d, first + a] for a in range(many)]
     values = [full[a] * b_ref[d, first + a] for a in range(many)]
-    start = pl.multiple_of((d * row_len + first) * col_len, many * col_len)
-    rows = pl.ds(start, many * col_len)
+    start = (d * row_len + first) * col_len
+    rows = pl.ds(start if isinstance(start, int) else pl.multiple_of(start, many * col_len), many * col_len)
     d_ref[rows, :width] = jnp.concatenate(gates, axis=0).astype(BF16)
     d_ref[rows, width:] = jnp.concatenate(values, axis=0).astype(BF16)
 
@@ -255,11 +248,8 @@
     core = lax.axis_index("row") & 1
 
     def blocks(one):
-        def at(n, carry):
-            one(n // cols * many, n % cols)
-            return carry
-
-        lax.fori_loop(0, row_len // many * cols, at, 0)
+        for first in range(0, row_len, many):
+            by_fours(cols, functools.partial(one, first))
 
     def right_back(base, a_ref, b_ref, d_ref):
         def one(first, d):
@@ -381,9 +371,12 @@
         refs[cols - 1 + d][area:, :] = chunk_ref[...]
 
 
-def home_kernel(cols, own_ref, got_ref, out_ref):
+def home_kernel(cols, own_ref, got_ref, pair_ref, out_ref, normed_ref, scaled_ref):
     row, core, col, step, pair = place(cols)
     out_ref[...] = jnp.where(step == 0, own_ref[...], got_ref[...])
+    normed, scaled = layer_norm(pair_ref[...])
+    normed_ref[...] = normed
+    scaled_ref[...] = jnp.broadcast_to(scaled, normed.shape)
 
 
 def join_kernel(cols, area, chunk_ref, *rest):
@@ -395,13 +388,12 @@
     half_ref[...] = order_ref[...].reshape(half_ref.shape).astype(BF16)
 
 
-def pair_grad_kernel(area, own_ref, pair_ref, *rest):
+def pair_grad_kernel(area, own_ref, normed_ref, scaled_ref, *rest):
     got_refs, grad_ref = rest[:-1], rest[-1]
     total = own_ref[...]
     for got in got_refs:
         total = total + got[:area, :].astype(F32)
-    normed, scaled = layer_norm(pair_ref[...])
-    grad_ref[...] = norm_back(total, normed, scaled)
+    grad_ref[...] = norm_back(total, normed_ref[...], scaled_ref[...])
 
 
 def weights_kernel(width, mine_ref, other_ref, proj_ref, out_ref):
@@ -612,8 +604,12 @@
         [low_mine, *parts],
     )
     gets = [in_plane(sends[d - 1], d) for d in range(1, cols)]
-    (pair_out,) = call(
-        functools.partial(home_kernel, cols), "home", 0.6, [like(area, width)], [pair_out, home]
+    pair_out, normed, scaled = call(
+        functools.partial(home_kernel, cols),
+        "home",
+        0.6,
+        [like(area, width)] * 3,
+        [pair_out, home, pair],
     )
     pair_out, *gets = lax.optimization_barrier((pair_out, *gets))
     (half_w,) = call(
@@ -631,7 +627,7 @@
         "pair_grad",
         1.0,
         [like(area, width)],
-        [rest, pair, *gets],
+        [rest, normed, scaled, *gets],
     )
     proj_grad, out_grad = call(
         functools.partial(weights_kernel, width),

time: 53.3 us -> 52.7 us (0.989)
  Pallas kernels: 10.6 us -> 9.88 us
    pallas_call x21, Pallas kernels: 10.6 us -> 9.88 us  [call(): pl.pallas_call(kernel, out_shape=tuple(out_shape), in_specs=specs, out_sp...]
where the time goes in v7:
time: 52.7 us; the launch traced here: 52.5 us
  starting transfers between devices  25.7 us (49%)
  waiting for transfers between devices  13.5 us (26%)
  Pallas kernels  9.88 us (19%)
  local copies, waits for them, and re-layouts  2.49 us (5%)
  between operations  0.86 us (2%)
    ppermute x20, starting transfers between devices, permute(): return lax.ppermute(value, ('row', 'col'), pairs)  25.7 us
    ppermute x20, waiting for transfers between devices, permute(): return lax.ppermute(value, ('row', 'col'), pairs)  13.5 us
    pallas_call x21, Pallas kernels, call(): pl.pallas_call(kernel, out_shape=tuple(out_shape), in_specs=specs, out_sp...  9.88 us
    unnamed x14, local copies, waits for them, and re-layouts  2.49 us
  transfers between devices with their start and end apart: 20, of which 14 were waited for; matrix products, arithmetic and copies ran while one was open for 0% of the time, Pallas kernels for 10%

profile of v7, /device:TPU:0, one launch (start us, length us, event | category | flops | bytes accessed | tf_op | source)
XLA Modules:
  0.0 52.5 jit_solution(14014218016761637478)
XLA Ops:
  0.6 0.9 %copy-done.2 = f32[12,24,128]{2,1,0:T(8,128)S(1)} copy-done((f32[12,24,128]{2,1,0:T(8,128)S(1)}, f32[12,24,128]{2,1,0:T(8,128)}, u32[]{:S(2)}) %copy-start.2) | copy-done | bytes 147480
  1.8 4.0 %collective-permute-start.2 = (bf16[288,128]{1,0:T(8,128)(2,1)S(1)}, bf16[288,128]{1,0:T(8,128)(2,1)S(1)}, u32[]{:S(2)}, u32[]{:S(2)}) collective-permute-start(bf16[288,128]{1,0:T(8,128)(2,1)S(1)} %norm.1), channel_id=1, source_target_pairs={{0,3},{1,2},{2,1},{3,0},{4,7},{5,6},{6,5},{7,4},{8,11},{9,10},{10,... | collective-permute-start | bytes 221192 | tf_op jit(solution)/shard_map/ppermute | solution.py:451
  6.4 1.7 %collective-permute-done.2 = bf16[288,128]{1,0:T(8,128)(2,1)S(1)} collective-permute-done((bf16[288,128]{1,0:T(8,128)(2,1)S(1)}, bf16[288,128]{1,0:T(8,128)(2,1)S(1)}, u32[]{:S(2)}, u32[]{:S(2)}) %collective-permute-start.2) | collective-permute-done | bytes 73760 | tf_op jit(solution)/shard_map/ppermute | solution.py:451
  8.1 2.0 %collective-permute-done.1 = bf16[288,128]{1,0:T(8,128)(2,1)S(1)} collective-permute-done((bf16[288,128]{1,0:T(8,128)(2,1)S(1)}, bf16[288,128]{1,0:T(8,128)(2,1)S(1)}, u32[]{:S(2)}, u32[]{:S(2)}) %collective-permute-start.1) | collective-permute-done | bytes 73760 | tf_op jit(solution)/shard_map/ppermute | solution.py:451
  11.2 0.7 %copy-done.6 = s32[12]{0:T(128)S(1)} copy-done((s32[12]{0:T(128)S(1)}, s32[12]{0:T(128)}, u32[]{:S(2)}) %copy-start.6) | copy-done | bytes 72
  11.8 0.5 %mask.1.mask_ref = f32[96,128]{1,0:T(8,128)S(1)} custom-call(s32[12]{0:T(128)S(1)} %copy-done.6), custom_call_target="tpu_custom_call" | custom-call | bytes 369000 | tf_op jit(solution)/shard_map/mask/pallas_call | solution.py:413
  12.4 0.9 %copy-done = bf16[128,640]{1,0:T(8,128)(2,1)S(1)} copy-done((bf16[128,640]{1,0:T(8,128)(2,1)S(1)}, bf16[128,640]{1,0:T(8,128)(2,1)}, u32[]{:S(2)}) %copy-start) | copy-done | bytes 163864
  14.5 0.5 mix_own.1.own_ref
  15.0 0.6 %collective-permute-done.5.x_ref = bf16[1152,128]{1,0:T(8,128)(2,1)S(1)} collective-permute-done((bf16[1152,128]{1,0:T(8,128)(2,1)S(1)}, bf16[1152,128]{1,0:T(8,128)(2,1)S(1)}, u32[]{:S(2)}, u32[]{:S(2)}) %collective-permute-start.5) | collective-permute-done | bytes 294944 | tf_op jit(solution)/shard_map/ppermute | solution.py:451
  16.0 0.9 %mix.1 = (bf16[288,128]{1,0:T(8,128)(2,1)S(1)}, f32[12,24,8,128]{3,2,1,0:T(8,128)S(1)}) custom-call(f32[4,12,24,128]{3,2,1,0:T(8,128)S(1)} %get-tuple-element.77.lv_ref, f32[4,12,24,128]{3,2,1,0:T(8,128)S(1)} %get-tuple-element.85.rv_ref, f32[12,16,128]{2,1,0:T(8,128)S(1)} %mix_own.1.own_ref, f32[288,128]{1,0:T(8,128)S(1)} %get-tuple-element.89.back_ref), custom_call_target="tpu_custom_call" | custom-call | bytes 4428000 | tf_op jit(solution)/shard_map/mix/pallas_call | solution.py:413
  16.9 2.2 %grads.1 = (bf16[1152,256]{1,0:T(8,128)(2,1)S(1)}, bf16[1152,256]{1,0:T(8,128)(2,1)S(1)}, bf16[1152,256]{1,0:T(8,128)(2,1)S(1)}) custom-call(f32[4,12,24,128]{3,2,1,0:T(8,128)S(1)} %get-tuple-element.77.lv_ref, f32[4,12,24,128]{3,2,1,0:T(8,128)S(1)} %get-tuple-element.81.la_ref, f32[4,12,24,128]{3,2,1,0:T(8,128)S(1)} %get-tuple-element.82.lb_ref, ...), custom_call_target="tpu_custom_call" | custom-call | bytes 9225000 | tf_op jit(solution)/shard_map/grads/pallas_call | solution.py:413
  19.6 0.6 %weight_sums.1 = (bf16[384,128]{1,0:T(8,128)(2,1)S(1)}, f32[384,128]{1,0:T(8,128)S(1)}, f32[288,128]{1,0:T(8,128)S(1)}, bf16[288,128]{1,0:T(8,128)(2,1)S(1)}) custom-call(bf16[1152,128]{1,0:T(8,128)(2,1)S(1)} %pad_maximum_fusion.x_ref.home_ref, bf16[1152,128]{1,0:T(8,128)(2,1)S(1)} %get-tuple-element.76.own_x_ref, ...), custom_call_target="tpu_custom_call" | custom-call | bytes 2214000 | tf_op jit(solution)/shard_map/weight_sums/pallas_call | solution.py:413
  21.6 7.9 %collective-permute-start.10 = (bf16[96,128]{1,0:T(8,128)(2,1)S(1)}, bf16[96,128]{1,0:T(8,128)(2,1)S(1)}, u32[]{:S(2)}, u32[]{:S(2)}) collective-permute-start(bf16[96,128]{1,0:T(8,128)(2,1)S(1)} %get-tuple-element.105), channel_id=1, source_target_pairs={{0,1},{1,0},{2,3},{3,2},{4,5},{5,4},{6,7},{7,6},{8,9},{9,8},{10,11... | collective-permute-start | bytes 73736 | tf_op jit(solution)/shard_map/ppermute | solution.py:451
  29.5 3.6 %collective-permute-start.11 = (bf16[96,128]{1,0:T(8,128)(2,1)S(1)}, bf16[96,128]{1,0:T(8,128)(2,1)S(1)}, u32[]{:S(2)}, u32[]{:S(2)}) collective-permute-start(bf16[96,128]{1,0:T(8,128)(2,1)S(1)} %get-tuple-element.106), channel_id=1, source_target_pairs={{0,2},{1,3},{2,0},{3,1},{4,6},{5,7},{6,4},{7,5},{8,10},{9,11},{10,... | collective-permute-start | bytes 73736 | tf_op jit(solution)/shard_map/ppermute | solution.py:451
  33.1 1.8 %collective-permute-done.11 = bf16[96,128]{1,0:T(8,128)(2,1)S(1)} collective-permute-done((bf16[96,128]{1,0:T(8,128)(2,1)S(1)}, bf16[96,128]{1,0:T(8,128)(2,1)S(1)}, u32[]{:S(2)}, u32[]{:S(2)}) %collective-permute-start.11) | collective-permute-done | bytes 24608 | tf_op jit(solution)/shard_map/ppermute | solution.py:451
  34.9 2.9 %collective-permute-done.12 = bf16[96,128]{1,0:T(8,128)(2,1)S(1)} collective-permute-done((bf16[96,128]{1,0:T(8,128)(2,1)S(1)}, bf16[96,128]{1,0:T(8,128)(2,1)S(1)}, u32[]{:S(2)}, u32[]{:S(2)}) %collective-permute-start.12) | collective-permute-done | bytes 24608 | tf_op jit(solution)/shard_map/ppermute | solution.py:451
  37.8 0.8 %collective-permute-start.15 = (bf16[96,128]{1,0:T(8,128)(2,1)S(1)}, bf16[96,128]{1,0:T(8,128)(2,1)S(1)}, u32[]{:S(2)}, u32[]{:S(2)}) collective-permute-start(bf16[96,128]{1,0:T(8,128)(2,1)S(1)} %fusion), channel_id=1, source_target_pairs={{0,24},{1,25},{2,26},{3,27},{4,28},{5,29},{6,30},{7,31},{8,16},{9,... | collective-permute-start | bytes 73736 | tf_op jit(solution)/shard_map/ppermute | solution.py:451
  38.6 3.7 %collective-permute-start.13 = (bf16[96,128]{1,0:T(8,128)(2,1)S(1)}, bf16[96,128]{1,0:T(8,128)(2,1)S(1)}, u32[]{:S(2)}, u32[]{:S(2)}) collective-permute-start(bf16[96,128]{1,0:T(8,128)(2,1)S(1)} %fusion), channel_id=1, source_target_pairs={{0,8},{1,9},{2,10},{3,11},{4,12},{5,13},{6,14},{7,15},{8,0},{9,1},... | collective-permute-start | bytes 73736 | tf_op jit(solution)/shard_map/ppermute | solution.py:451
  42.8 0.8 %collective-permute-done.15 = bf16[96,128]{1,0:T(8,128)(2,1)S(1)} collective-permute-done((bf16[96,128]{1,0:T(8,128)(2,1)S(1)}, bf16[96,128]{1,0:T(8,128)(2,1)S(1)}, u32[]{:S(2)}, u32[]{:S(2)}) %collective-permute-start.15) | collective-permute-done | bytes 24608 | tf_op jit(solution)/shard_map/ppermute | solution.py:451
  44.8 2.9 %collective-permute-start.18 = (bf16[384,128]{1,0:T(8,128)(2,1)S(1)}, bf16[384,128]{1,0:T(8,128)(2,1)S(1)}, u32[]{:S(2)}, u32[]{:S(2)}) collective-permute-start(bf16[384,128]{1,0:T(8,128)(2,1)S(1)} %get-tuple-element.120), channel_id=1, source_target_pairs={{0,3},{1,2},{2,1},{3,0},{4,7},{5,6},{6,5},{7,4},{8,11},{9,10},{10,... | collective-permute-start | bytes 294920 | tf_op jit(solution)/shard_map/ppermute | solution.py:451
  47.7 0.8 %home.1 = (f32[288,128]{1,0:T(8,128)}, f32[288,128]{1,0:T(8,128)S(1)}, f32[288,128]{1,0:T(8,128)S(1)}) custom-call(f32[288,128]{1,0:T(8,128)S(1)} %get-tuple-element.98.own_ref, f32[288,128]{1,0:T(8,128)S(1)} %collective-permute-done.8.got_ref, f32[288,128]{1,0:T(8,128)S(1)} %bitcast.5), custom_call_target="tpu_custom_call" | custom-call | bytes 2214000 | tf_op jit(solution)/shard_map/home/pallas_call | solution.py:413
  49.1 1.2 %collective-permute-done.18.rest_2_ = bf16[384,128]{1,0:T(8,128)(2,1)S(1)} collective-permute-done((bf16[384,128]{1,0:T(8,128)(2,1)S(1)}, bf16[384,128]{1,0:T(8,128)(2,1)S(1)}, u32[]{:S(2)}, u32[]{:S(2)}) %collective-permute-start.18) | collective-permute-done | bytes 98336 | tf_op jit(solution)/shard_map/ppermute | solution.py:451
  50.4 0.8 %pair_grad.1 = f32[288,128]{1,0:T(8,128)} custom-call(f32[288,128]{1,0:T(8,128)S(1)} %get-tuple-element.126.own_ref, f32[288,128]{1,0:T(8,128)S(1)} %get-tuple-element.127.normed_ref, f32[288,128]{1,0:T(8,128)S(1)} %get-tuple-element.128.scaled_ref, bf16[384,128]{1,0:T(8,128)(2,1)S(1)} %collective-permute-done.16.rest_0_, ...), custom_call_target="tpu_custom_call" | custom-call | bytes 3690000 | tf_op jit(solution)/shard_map/pair_grad/pallas_call | solution.py:413
  51.7 0.8 %weights.1 = (f32[128,640]{1,0:T(8,128)}, f32[128,128]{1,0:T(8,128)}) custom-call(bf16[384,128]{1,0:T(8,128)(2,1)S(1)} %join.1.mine_ref, bf16[384,128]{1,0:T(8,128)(2,1)S(1)} %collective-permute-done.19.other_ref), custom_call_target="tpu_custom_call" | custom-call | bytes 2952000 | tf_op jit(solution)/shard_map/weights/pallas_call | solution.py:413
  (54 shorter events, 8.2 us)
Async XLA Ops:
  1.5 12.1 %copy-start.4 = (f32[12,24,128]{2,1,0:T(8,128)S(1)}, f32[12,24,128]{2,1,0:T(8,128)}, u32[]{:S(2)}) copy-start(f32[12,24,128]{2,1,0:T(8,128)} %param.9) | copy-start | bytes 442372
  1.5 12.1 %copy-start.5 = (bf16[128,128]{1,0:T(8,128)(2,1)S(1)}, bf16[128,128]{1,0:T(8,128)(2,1)}, u32[]{:S(2)}) copy-start(bf16[128,128]{1,0:T(8,128)(2,1)} %wout_ref.3) | copy-start | bytes 98308
  1.5 12.6 %copy-start.1 = (bf16[128,640]{1,0:T(8,128)(2,1)S(1)}, bf16[128,640]{1,0:T(8,128)(2,1)}, u32[]{:S(2)}) copy-start(bf16[128,640]{1,0:T(8,128)(2,1)} %w_ref.13) | copy-start | bytes 491524
  1.8 6.3 %collective-permute-start.2 = (bf16[288,128]{1,0:T(8,128)(2,1)S(1)}, bf16[288,128]{1,0:T(8,128)(2,1)S(1)}, u32[]{:S(2)}, u32[]{:S(2)}) collective-permute-start(bf16[288,128]{1,0:T(8,128)(2,1)S(1)} %norm.1), channel_id=1, source_target_pairs={{0,3},{1,2},{2,1},{3,0},{4,7},{5,6},{6,5},{7,4},{8,11},{9,10},{10,... | collective-permute-start | bytes 221192 | tf_op jit(solution)/shard_map/ppermute | solution.py:451
  5.7 4.4 %collective-permute-start.1 = (bf16[288,128]{1,0:T(8,128)(2,1)S(1)}, bf16[288,128]{1,0:T(8,128)(2,1)S(1)}, u32[]{:S(2)}, u32[]{:S(2)}) collective-permute-start(bf16[288,128]{1,0:T(8,128)(2,1)S(1)} %norm.1), channel_id=1, source_target_pairs={{0,2},{1,3},{2,0},{3,1},{4,6},{5,7},{6,4},{7,5},{8,10},{9,11},{10,... | collective-permute-start | bytes 221192 | tf_op jit(solution)/shard_map/ppermute | solution.py:451
  6.2 4.4 %collective-permute-start = (bf16[288,128]{1,0:T(8,128)(2,1)S(1)}, bf16[288,128]{1,0:T(8,128)(2,1)S(1)}, u32[]{:S(2)}, u32[]{:S(2)}) collective-permute-start(bf16[288,128]{1,0:T(8,128)(2,1)S(1)} %norm.1), channel_id=1, source_target_pairs={{0,1},{1,0},{2,3},{3,2},{4,5},{5,4},{6,7},{7,6},{8,9},{9,8},{10,11... | collective-permute-start | bytes 221192 | tf_op jit(solution)/shard_map/ppermute | solution.py:451
  10.6 3.4 %collective-permute-start.4 = (bf16[1152,128]{1,0:T(8,128)(2,1)S(1)}, bf16[1152,128]{1,0:T(8,128)(2,1)S(1)}, u32[]{:S(2)}, u32[]{:S(2)}) collective-permute-start(bf16[1152,128]{1,0:T(8,128)(2,1)S(1)} %pad_maximum_fusion.x_ref.home_ref), channel_id=1, source_target_pairs={{0,4},{1,17},{2,10},{3,27},{4,0},{5,21},{6,14},{7,31},{8,16},{9,1}... | collective-permute-start | bytes 884744 | tf_op jit(solution)/shard_map/ppermute | solution.py:451
  10.7 3.0 %collective-permute-start.3 = (f32[288,128]{1,0:T(8,128)}, f32[288,128]{1,0:T(8,128)S(1)}, u32[]{:S(2)}, u32[]{:S(2)}) collective-permute-start(f32[288,128]{1,0:T(8,128)} %bitcast.6), channel_id=1, source_target_pairs={{0,4},{1,5},{2,6},{3,7},{4,0},{5,1},{6,2},{7,3},{8,10},{9,11},{10,... | collective-permute-start | bytes 442376 | tf_op jit(solution)/shard_map/ppermute | solution.py:451
  14.0 1.6 %collective-permute-start.5 = (bf16[1152,128]{1,0:T(8,128)(2,1)S(1)}, bf16[1152,128]{1,0:T(8,128)(2,1)S(1)}, u32[]{:S(2)}, u32[]{:S(2)}) collective-permute-start(bf16[1152,128]{1,0:T(8,128)(2,1)S(1)} %collective-permute-done.4.x_ref.home_ref), channel_id=1, source_target_pairs={{0,4},{1,5},{2,6},{3,7},{4,0},{5,1},{6,2},{7,3},{8,12},{9,13},{10,... | collective-permute-start | bytes 884744 | tf_op jit(solution)/shard_map/ppermute | solution.py:451
  19.4 1.6 %collective-permute-start.6 = (bf16[1152,128]{1,0:T(8,128)(2,1)S(1)}, bf16[1152,128]{1,0:T(8,128)(2,1)S(1)}, u32[]{:S(2)}, u32[]{:S(2)}) collective-permute-start(bf16[1152,128]{1,0:T(8,128)(2,1)S(1)} %back_other.1), channel_id=1, source_target_pairs={{0,4},{1,5},{2,6},{3,7},{4,0},{5,1},{6,2},{7,3},{8,12},{9,13},{10,... | collective-permute-start | bytes 884744 | tf_op jit(solution)/shard_map/ppermute | solution.py:451
  20.2 1.4 %collective-permute-start.9 = (bf16[384,128]{1,0:T(8,128)(2,1)S(1)}, bf16[384,128]{1,0:T(8,128)(2,1)S(1)}, u32[]{:S(2)}, u32[]{:S(2)}) collective-permute-start(bf16[384,128]{1,0:T(8,128)(2,1)S(1)} %get-tuple-element.102), channel_id=1, source_target_pairs={{0,4},{1,5},{2,6},{3,7},{4,0},{5,1},{6,2},{7,3},{8,12},{9,13},{10,... | collective-permute-start | bytes 294920 | tf_op jit(solution)/shard_map/ppermute | solution.py:451
  21.1 21.5 %collective-permute-start.7 = (bf16[1152,128]{1,0:T(8,128)(2,1)S(1)}, bf16[1152,128]{1,0:T(8,128)(2,1)S(1)}, u32[]{:S(2)}, u32[]{:S(2)}) collective-permute-start(bf16[1152,128]{1,0:T(8,128)(2,1)S(1)} %core_sum.1.y_ref), channel_id=1, source_target_pairs={{0,4},{1,9},{2,18},{3,27},{4,0},{5,13},{6,22},{7,31},{8,16},{9,25}... | collective-permute-start | bytes 884744 | tf_op jit(solution)/shard_map/ppermute | solution.py:451
  21.6 11.5 %collective-permute-start.10 = (bf16[96,128]{1,0:T(8,128)(2,1)S(1)}, bf16[96,128]{1,0:T(8,128)(2,1)S(1)}, u32[]{:S(2)}, u32[]{:S(2)}) collective-permute-start(bf16[96,128]{1,0:T(8,128)(2,1)S(1)} %get-tuple-element.105), channel_id=1, source_target_pairs={{0,1},{1,0},{2,3},{3,2},{4,5},{5,4},{6,7},{7,6},{8,9},{9,8},{10,11... | collective-permute-start | bytes 73736 | tf_op jit(solution)/shard_map/ppermute | solution.py:451
  29.5 5.4 %collective-permute-start.11 = (bf16[96,128]{1,0:T(8,128)(2,1)S(1)}, bf16[96,128]{1,0:T(8,128)(2,1)S(1)}, u32[]{:S(2)}, u32[]{:S(2)}) collective-permute-start(bf16[96,128]{1,0:T(8,128)(2,1)S(1)} %get-tuple-element.106), channel_id=1, source_target_pairs={{0,2},{1,3},{2,0},{3,1},{4,6},{5,7},{6,4},{7,5},{8,10},{9,11},{10,... | collective-permute-start | bytes 73736 | tf_op jit(solution)/shard_map/ppermute | solution.py:451
  33.1 4.7 %collective-permute-start.12 = (bf16[96,128]{1,0:T(8,128)(2,1)S(1)}, bf16[96,128]{1,0:T(8,128)(2,1)S(1)}, u32[]{:S(2)}, u32[]{:S(2)}) collective-permute-start(bf16[96,128]{1,0:T(8,128)(2,1)S(1)} %get-tuple-element.107), channel_id=1, source_target_pairs={{0,3},{1,2},{2,1},{3,0},{4,7},{5,6},{6,5},{7,4},{8,11},{9,10},{10,... | collective-permute-start | bytes 73736 | tf_op jit(solution)/shard_map/ppermute | solution.py:451
  33.1 9.6 %collective-permute-start.8 = (f32[288,128]{1,0:T(8,128)S(1)}, f32[288,128]{1,0:T(8,128)S(1)}, u32[]{:S(2)}, u32[]{:S(2)}) collective-permute-start(f32[288,128]{1,0:T(8,128)S(1)} %get-tuple-element.98.own_ref), channel_id=1, source_target_pairs={{0,4},{1,5},{2,6},{3,7},{4,0},{5,1},{6,2},{7,3},{8,10},{9,11},{10,... | collective-permute-start | bytes 442376 | tf_op jit(solution)/shard_map/ppermute | solution.py:451
  37.8 5.8 %collective-permute-start.15 = (bf16[96,128]{1,0:T(8,128)(2,1)S(1)}, bf16[96,128]{1,0:T(8,128)(2,1)S(1)}, u32[]{:S(2)}, u32[]{:S(2)}) collective-permute-start(bf16[96,128]{1,0:T(8,128)(2,1)S(1)} %fusion), channel_id=1, source_target_pairs={{0,24},{1,25},{2,26},{3,27},{4,28},{5,29},{6,30},{7,31},{8,16},{9,... | collective-permute-start | bytes 73736 | tf_op jit(solution)/shard_map/ppermute | solution.py:451
  38.6 5.0 %collective-permute-start.14 = (bf16[96,128]{1,0:T(8,128)(2,1)S(1)}, bf16[96,128]{1,0:T(8,128)(2,1)S(1)}, u32[]{:S(2)}, u32[]{:S(2)}) collective-permute-start(bf16[96,128]{1,0:T(8,128)(2,1)S(1)} %fusion), channel_id=1, source_target_pairs={{0,16},{1,17},{2,18},{3,19},{4,20},{5,21},{6,22},{7,23},{8,24},{9,... | collective-permute-start | bytes 73736 | tf_op jit(solution)/shard_map/ppermute | solution.py:451
  38.6 5.5 %collective-permute-start.13 = (bf16[96,128]{1,0:T(8,128)(2,1)S(1)}, bf16[96,128]{1,0:T(8,128)(2,1)S(1)}, u32[]{:S(2)}, u32[]{:S(2)}) collective-permute-start(bf16[96,128]{1,0:T(8,128)(2,1)S(1)} %fusion), channel_id=1, source_target_pairs={{0,8},{1,9},{2,10},{3,11},{4,12},{5,13},{6,14},{7,15},{8,0},{9,1},... | collective-permute-start | bytes 73736 | tf_op jit(solution)/shard_map/ppermute | solution.py:451
  42.6 5.1 %copy-start.3 = (f32[12,24,128]{2,1,0:T(8,128)S(1)}, f32[12,24,128]{2,1,0:T(8,128)}, u32[]{:S(2)}) copy-start(f32[12,24,128]{2,1,0:T(8,128)} %param.5) | copy-start | bytes 442372
  44.2 4.7 %collective-permute-start.16 = (bf16[384,128]{1,0:T(8,128)(2,1)S(1)}, bf16[384,128]{1,0:T(8,128)(2,1)S(1)}, u32[]{:S(2)}, u32[]{:S(2)}) collective-permute-start(bf16[384,128]{1,0:T(8,128)(2,1)S(1)} %get-tuple-element.118), channel_id=1, source_target_pairs={{0,1},{1,0},{2,3},{3,2},{4,5},{5,4},{6,7},{7,6},{8,9},{9,8},{10,11... | collective-permute-start | bytes 294920 | tf_op jit(solution)/shard_map/ppermute | solution.py:451
  44.5 4.6 %collective-permute-start.17 = (bf16[384,128]{1,0:T(8,128)(2,1)S(1)}, bf16[384,128]{1,0:T(8,128)(2,1)S(1)}, u32[]{:S(2)}, u32[]{:S(2)}) collective-permute-start(bf16[384,128]{1,0:T(8,128)(2,1)S(1)} %get-tuple-element.119), channel_id=1, source_target_pairs={{0,2},{1,3},{2,0},{3,1},{4,6},{5,7},{6,4},{7,5},{8,10},{9,11},{10,... | collective-permute-start | bytes 294920 | tf_op jit(solution)/shard_map/ppermute | solution.py:451
  44.8 5.5 %collective-permute-start.18 = (bf16[384,128]{1,0:T(8,128)(2,1)S(1)}, bf16[384,128]{1,0:T(8,128)(2,1)S(1)}, u32[]{:S(2)}, u32[]{:S(2)}) collective-permute-start(bf16[384,128]{1,0:T(8,128)(2,1)S(1)} %get-tuple-element.120), channel_id=1, source_target_pairs={{0,3},{1,2},{2,1},{3,0},{4,7},{5,6},{6,5},{7,4},{8,11},{9,10},{10,... | collective-permute-start | bytes 294920 | tf_op jit(solution)/shard_map/ppermute | solution.py:451
  50.3 1.4 %collective-permute-start.19 = (bf16[384,128]{1,0:T(8,128)(2,1)S(1)}, bf16[384,128]{1,0:T(8,128)(2,1)S(1)}, u32[]{:S(2)}, u32[]{:S(2)}) collective-permute-start(bf16[384,128]{1,0:T(8,128)(2,1)S(1)} %join.1.mine_ref), channel_id=1, source_target_pairs={{0,4},{1,5},{2,6},{3,7},{4,0},{5,1},{6,2},{7,3},{8,12},{9,13},{10,... | collective-permute-start | bytes 294920 | tf_op jit(solution)/shard_map/ppermute | solution.py:451
  (3 other events, 2.5 us)

commit v8 on v7

--- a/solution.py
+++ b/solution.py
@@ -102,6 +102,8 @@
         project_block(projected, mask_ref, row, col ^ d, sizes, (d,), *refs[-3:])
 
     by_fours(cols, one)
+    if side == 0:
+        refs[0][...] = x_ref[...].T
 
 
 def tile(g):
@@ -285,6 +287,7 @@
     area,
     width,
     x_ref,
+    x_turned_ref,
     own_x_ref,
     other_x_ref,
     dl_ref,
@@ -306,7 +309,7 @@
     out_ref[...] = gate_ref[...] * update
     grad_logit = (cot_ref[...] * update).astype(BF16)
     logit_ref[...] = grad_logit
-    left_w = dot_tn(x_ref[...], dl_ref[...])
+    left_w = dot(x_turned_ref[...], dl_ref[...])
     right_w = dot_tn(own_x_ref[...], do_ref[...]) + dot_tn(other_x_ref[...], dr_ref[...])
     sum_ref[0, :width, :] = left_w[:, :width]
     sum_ref[0, width : 2 * width, :] = left_w[:, width:]
@@ -478,11 +481,11 @@
     (mask,) = call(
         mask_kernel, "mask", 0.1, [like(col_len * cols, width)], [block_valid], space=pltpu.SMEM
     )
-    left = call(
+    x_turned, *left = call(
         functools.partial(project_kernel, 0, cols, sizes),
         "left",
         0.9,
-        [like(cols, row_len, col_len, width)] * 3,
+        [like(width, tall, dtype=BF16)] + [like(cols, row_len, col_len, width)] * 3,
         [mask, x, x, proj_weight],
     )
     out_gate, cot, back, update_low = call(
@@ -542,7 +545,7 @@
             like(area, width),
             like(area, width, dtype=BF16),
         ],
-        [x, own_x, other_x, dl, do, dr, mixed_low, out_gate, cot, update_low, out_weight],
+        [x, x_turned, own_x, other_x, dl, do, dr, mixed_low, out_gate, cot, update_low, out_weight],
         [pltpu.VMEM((2, half, width), F32)],
     )
     got_w = swap(send_w)

time: 52.7 us -> 52.7 us (level)
  no operation moved by 1% of the time
where the time goes in v8:
time: 52.7 us; the launch traced here: 52.5 us
  starting transfers between devices  25.7 us (49%)
  waiting for transfers between devices  13.5 us (26%)
  Pallas kernels  9.84 us (19%)
  local copies, waits for them, and re-layouts  2.49 us (5%)
  between operations  0.88 us (2%)
    ppermute x20, starting transfers between devices, permute(): return lax.ppermute(value, ('row', 'col'), pairs)  25.7 us
    ppermute x20, waiting for transfers between devices, permute(): return lax.ppermute(value, ('row', 'col'), pairs)  13.5 us
    pallas_call x21, Pallas kernels, call(): pl.pallas_call(kernel, out_shape=tuple(out_shape), in_specs=specs, out_sp...  9.84 us
    unnamed x14, local copies, waits for them, and re-layouts  2.49 us
  transfers between devices with their start and end apart: 20, of which 14 were waited for; matrix products, arithmetic and copies ran while one was open for 0% of the time, Pallas kernels for 10%

profile of v8, /device:TPU:0, one launch (start us, length us, event | category | flops | bytes accessed | tf_op | source)
XLA Modules:
  0.0 52.5 jit_solution(2008604910021150962)
XLA Ops:
  0.6 0.9 %copy-done.2 = f32[12,24,128]{2,1,0:T(8,128)S(1)} copy-done((f32[12,24,128]{2,1,0:T(8,128)S(1)}, f32[12,24,128]{2,1,0:T(8,128)}, u32[]{:S(2)}) %copy-start.2) | copy-done | bytes 147480
  1.8 4.0 %collective-permute-start.2 = (bf16[288,128]{1,0:T(8,128)(2,1)S(1)}, bf16[288,128]{1,0:T(8,128)(2,1)S(1)}, u32[]{:S(2)}, u32[]{:S(2)}) collective-permute-start(bf16[288,128]{1,0:T(8,128)(2,1)S(1)} %norm.1), channel_id=1, source_target_pairs={{0,3},{1,2},{2,1},{3,0},{4,7},{5,6},{6,5},{7,4},{8,11},{9,10},{10,... | collective-permute-start | bytes 221192 | tf_op jit(solution)/shard_map/ppermute | solution.py:454
  6.4 1.7 %collective-permute-done.2 = bf16[288,128]{1,0:T(8,128)(2,1)S(1)} collective-permute-done((bf16[288,128]{1,0:T(8,128)(2,1)S(1)}, bf16[288,128]{1,0:T(8,128)(2,1)S(1)}, u32[]{:S(2)}, u32[]{:S(2)}) %collective-permute-start.2) | collective-permute-done | bytes 73760 | tf_op jit(solution)/shard_map/ppermute | solution.py:454
  8.1 2.0 %collective-permute-done.1 = bf16[288,128]{1,0:T(8,128)(2,1)S(1)} collective-permute-done((bf16[288,128]{1,0:T(8,128)(2,1)S(1)}, bf16[288,128]{1,0:T(8,128)(2,1)S(1)}, u32[]{:S(2)}, u32[]{:S(2)}) %collective-permute-start.1) | collective-permute-done | bytes 73760 | tf_op jit(solution)/shard_map/ppermute | solution.py:454
  11.2 0.7 %copy-done.6 = s32[12]{0:T(128)S(1)} copy-done((s32[12]{0:T(128)S(1)}, s32[12]{0:T(128)}, u32[]{:S(2)}) %copy-start.6) | copy-done | bytes 72
  11.8 0.5 %mask.1.mask_ref = f32[96,128]{1,0:T(8,128)S(1)} custom-call(s32[12]{0:T(128)S(1)} %copy-done.6), custom_call_target="tpu_custom_call" | custom-call | bytes 369000 | tf_op jit(solution)/shard_map/mask/pallas_call | solution.py:416
  12.4 0.9 %copy-done = bf16[128,640]{1,0:T(8,128)(2,1)S(1)} copy-done((bf16[128,640]{1,0:T(8,128)(2,1)S(1)}, bf16[128,640]{1,0:T(8,128)(2,1)}, u32[]{:S(2)}) %copy-start) | copy-done | bytes 163864
  15.1 0.6 %collective-permute-done.5.x_ref = bf16[1152,128]{1,0:T(8,128)(2,1)S(1)} collective-permute-done((bf16[1152,128]{1,0:T(8,128)(2,1)S(1)}, bf16[1152,128]{1,0:T(8,128)(2,1)S(1)}, u32[]{:S(2)}, u32[]{:S(2)}) %collective-permute-start.5) | collective-permute-done | bytes 294944 | tf_op jit(solution)/shard_map/ppermute | solution.py:454
  16.0 0.9 %mix.1 = (bf16[288,128]{1,0:T(8,128)(2,1)S(1)}, f32[12,24,8,128]{3,2,1,0:T(8,128)S(1)}) custom-call(f32[4,12,24,128]{3,2,1,0:T(8,128)S(1)} %get-tuple-element.79.lv_ref, f32[4,12,24,128]{3,2,1,0:T(8,128)S(1)} %get-tuple-element.87.rv_ref, f32[12,16,128]{2,1,0:T(8,128)S(1)} %mix_own.1.own_ref, f32[288,128]{1,0:T(8,128)S(1)} %get-tuple-element.91.back_ref), custom_call_target="tpu_custom_call" | custom-call | bytes 4428000 | tf_op jit(solution)/shard_map/mix/pallas_call | solution.py:416
  16.9 2.2 %grads.1 = (bf16[1152,256]{1,0:T(8,128)(2,1)S(1)}, bf16[1152,256]{1,0:T(8,128)(2,1)S(1)}, bf16[1152,256]{1,0:T(8,128)(2,1)S(1)}) custom-call(f32[4,12,24,128]{3,2,1,0:T(8,128)S(1)} %get-tuple-element.79.lv_ref, f32[4,12,24,128]{3,2,1,0:T(8,128)S(1)} %get-tuple-element.83.la_ref, f32[4,12,24,128]{3,2,1,0:T(8,128)S(1)} %get-tuple-element.84.lb_ref, ...), custom_call_target="tpu_custom_call" | custom-call | bytes 9225000 | tf_op jit(solution)/shard_map/grads/pallas_call | solution.py:416
  19.6 0.5 %weight_sums.1 = (bf16[384,128]{1,0:T(8,128)(2,1)S(1)}, f32[384,128]{1,0:T(8,128)S(1)}, f32[288,128]{1,0:T(8,128)S(1)}, bf16[288,128]{1,0:T(8,128)(2,1)S(1)}) custom-call(bf16[1152,128]{1,0:T(8,128)(2,1)S(1)} %pad_maximum_fusion.x_ref.home_ref, bf16[128,1152]{1,0:T(8,128)(2,1)S(1)} %get-tuple-element.71.x_turned_ref, ...), custom_call_target="tpu_custom_call" | custom-call | bytes 2214000 | tf_op jit(solution)/shard_map/weight_sums/pallas_call | solution.py:416
  21.6 7.9 %collective-permute-start.10 = (bf16[96,128]{1,0:T(8,128)(2,1)S(1)}, bf16[96,128]{1,0:T(8,128)(2,1)S(1)}, u32[]{:S(2)}, u32[]{:S(2)}) collective-permute-start(bf16[96,128]{1,0:T(8,128)(2,1)S(1)} %get-tuple-element.107), channel_id=1, source_target_pairs={{0,1},{1,0},{2,3},{3,2},{4,5},{5,4},{6,7},{7,6},{8,9},{9,8},{10,11... | collective-permute-start | bytes 73736 | tf_op jit(solution)/shard_map/ppermute | solution.py:454
  29.5 3.6 %collective-permute-start.11 = (bf16[96,128]{1,0:T(8,128)(2,1)S(1)}, bf16[96,128]{1,0:T(8,128)(2,1)S(1)}, u32[]{:S(2)}, u32[]{:S(2)}) collective-permute-start(bf16[96,128]{1,0:T(8,128)(2,1)S(1)} %get-tuple-element.108), channel_id=1, source_target_pairs={{0,2},{1,3},{2,0},{3,1},{4,6},{5,7},{6,4},{7,5},{8,10},{9,11},{10,... | collective-permute-start | bytes 73736 | tf_op jit(solution)/shard_map/ppermute | solution.py:454
  33.1 1.8 %collective-permute-done.11 = bf16[96,128]{1,0:T(8,128)(2,1)S(1)} collective-permute-done((bf16[96,128]{1,0:T(8,128)(2,1)S(1)}, bf16[96,128]{1,0:T(8,128)(2,1)S(1)}, u32[]{:S(2)}, u32[]{:S(2)}) %collective-permute-start.11) | collective-permute-done | bytes 24608 | tf_op jit(solution)/shard_map/ppermute | solution.py:454
  34.9 2.9 %collective-permute-done.12 = bf16[96,128]{1,0:T(8,128)(2,1)S(1)} collective-permute-done((bf16[96,128]{1,0:T(8,128)(2,1)S(1)}, bf16[96,128]{1,0:T(8,128)(2,1)S(1)}, u32[]{:S(2)}, u32[]{:S(2)}) %collective-permute-start.12) | collective-permute-done | bytes 24608 | tf_op jit(solution)/shard_map/ppermute | solution.py:454
  37.8 0.7 %collective-permute-start.15 = (bf16[96,128]{1,0:T(8,128)(2,1)S(1)}, bf16[96,128]{1,0:T(8,128)(2,1)S(1)}, u32[]{:S(2)}, u32[]{:S(2)}) collective-permute-start(bf16[96,128]{1,0:T(8,128)(2,1)S(1)} %fusion), channel_id=1, source_target_pairs={{0,24},{1,25},{2,26},{3,27},{4,28},{5,29},{6,30},{7,31},{8,16},{9,... | collective-permute-start | bytes 73736 | tf_op jit(solution)/shard_map/ppermute | solution.py:454
  38.6 3.7 %collective-permute-start.13 = (bf16[96,128]{1,0:T(8,128)(2,1)S(1)}, bf16[96,128]{1,0:T(8,128)(2,1)S(1)}, u32[]{:S(2)}, u32[]{:S(2)}) collective-permute-start(bf16[96,128]{1,0:T(8,128)(2,1)S(1)} %fusion), channel_id=1, source_target_pairs={{0,8},{1,9},{2,10},{3,11},{4,12},{5,13},{6,14},{7,15},{8,0},{9,1},... | collective-permute-start | bytes 73736 | tf_op jit(solution)/shard_map/ppermute | solution.py:454
  42.8 0.8 %collective-permute-done.15 = bf16[96,128]{1,0:T(8,128)(2,1)S(1)} collective-permute-done((bf16[96,128]{1,0:T(8,128)(2,1)S(1)}, bf16[96,128]{1,0:T(8,128)(2,1)S(1)}, u32[]{:S(2)}, u32[]{:S(2)}) %collective-permute-start.15) | collective-permute-done | bytes 24608 | tf_op jit(solution)/shard_map/ppermute | solution.py:454
  43.6 0.5 %collective-permute-done.13 = bf16[96,128]{1,0:T(8,128)(2,1)S(1)} collective-permute-done((bf16[96,128]{1,0:T(8,128)(2,1)S(1)}, bf16[96,128]{1,0:T(8,128)(2,1)S(1)}, u32[]{:S(2)}, u32[]{:S(2)}) %collective-permute-start.13) | collective-permute-done | bytes 24608 | tf_op jit(solution)/shard_map/ppermute | solution.py:454
  44.8 2.9 %collective-permute-start.18 = (bf16[384,128]{1,0:T(8,128)(2,1)S(1)}, bf16[384,128]{1,0:T(8,128)(2,1)S(1)}, u32[]{:S(2)}, u32[]{:S(2)}) collective-permute-start(bf16[384,128]{1,0:T(8,128)(2,1)S(1)} %get-tuple-element.122), channel_id=1, source_target_pairs={{0,3},{1,2},{2,1},{3,0},{4,7},{5,6},{6,5},{7,4},{8,11},{9,10},{10,... | collective-permute-start | bytes 294920 | tf_op jit(solution)/shard_map/ppermute | solution.py:454
  47.7 0.8 %home.1 = (f32[288,128]{1,0:T(8,128)}, f32[288,128]{1,0:T(8,128)S(1)}, f32[288,128]{1,0:T(8,128)S(1)}) custom-call(f32[288,128]{1,0:T(8,128)S(1)} %get-tuple-element.100.own_ref, f32[288,128]{1,0:T(8,128)S(1)} %collective-permute-done.8.got_ref, f32[288,128]{1,0:T(8,128)S(1)} %bitcast.5), custom_call_target="tpu_custom_call" | custom-call | bytes 2214000 | tf_op jit(solution)/shard_map/home/pallas_call | solution.py:416
  49.1 1.2 %collective-permute-done.18.rest_2_ = bf16[384,128]{1,0:T(8,128)(2,1)S(1)} collective-permute-done((bf16[384,128]{1,0:T(8,128)(2,1)S(1)}, bf16[384,128]{1,0:T(8,128)(2,1)S(1)}, u32[]{:S(2)}, u32[]{:S(2)}) %collective-permute-start.18) | collective-permute-done | bytes 98336 | tf_op jit(solution)/shard_map/ppermute | solution.py:454
  50.4 0.8 %pair_grad.1 = f32[288,128]{1,0:T(8,128)} custom-call(f32[288,128]{1,0:T(8,128)S(1)} %get-tuple-element.128.own_ref, f32[288,128]{1,0:T(8,128)S(1)} %get-tuple-element.129.normed_ref, f32[288,128]{1,0:T(8,128)S(1)} %get-tuple-element.130.scaled_ref, bf16[384,128]{1,0:T(8,128)(2,1)S(1)} %collective-permute-done.16.rest_0_, ...), custom_call_target="tpu_custom_call" | custom-call | bytes 3690000 | tf_op jit(solution)/shard_map/pair_grad/pallas_call | solution.py:416
  51.7 0.8 %weights.1 = (f32[128,640]{1,0:T(8,128)}, f32[128,128]{1,0:T(8,128)}) custom-call(bf16[384,128]{1,0:T(8,128)(2,1)S(1)} %join.1.mine_ref, bf16[384,128]{1,0:T(8,128)(2,1)S(1)} %collective-permute-done.19.other_ref), custom_call_target="tpu_custom_call" | custom-call | bytes 2952000 | tf_op jit(solution)/shard_map/weights/pallas_call | solution.py:416
  (54 shorter events, 8.3 us)
Async XLA Ops:
  1.5 12.1 %copy-start.4 = (f32[12,24,128]{2,1,0:T(8,128)S(1)}, f32[12,24,128]{2,1,0:T(8,128)}, u32[]{:S(2)}) copy-start(f32[12,24,128]{2,1,0:T(8,128)} %param.9) | copy-start | bytes 442372
  1.5 12.1 %copy-start.5 = (bf16[128,128]{1,0:T(8,128)(2,1)S(1)}, bf16[128,128]{1,0:T(8,128)(2,1)}, u32[]{:S(2)}) copy-start(bf16[128,128]{1,0:T(8,128)(2,1)} %wout_ref.3) | copy-start | bytes 98308
  1.8 6.3 %collective-permute-start.2 = (bf16[288,128]{1,0:T(8,128)(2,1)S(1)}, bf16[288,128]{1,0:T(8,128)(2,1)S(1)}, u32[]{:S(2)}, u32[]{:S(2)}) collective-permute-start(bf16[288,128]{1,0:T(8,128)(2,1)S(1)} %norm.1), channel_id=1, source_target_pairs={{0,3},{1,2},{2,1},{3,0},{4,7},{5,6},{6,5},{7,4},{8,11},{9,10},{10,... | collective-permute-start | bytes 221192 | tf_op jit(solution)/shard_map/ppermute | solution.py:454
  5.7 4.4 %collective-permute-start.1 = (bf16[288,128]{1,0:T(8,128)(2,1)S(1)}, bf16[288,128]{1,0:T(8,128)(2,1)S(1)}, u32[]{:S(2)}, u32[]{:S(2)}) collective-permute-start(bf16[288,128]{1,0:T(8,128)(2,1)S(1)} %norm.1), channel_id=1, source_target_pairs={{0,2},{1,3},{2,0},{3,1},{4,6},{5,7},{6,4},{7,5},{8,10},{9,11},{10,... | collective-permute-start | bytes 221192 | tf_op jit(solution)/shard_map/ppermute | solution.py:454
  6.2 4.4 %collective-permute-start = (bf16[288,128]{1,0:T(8,128)(2,1)S(1)}, bf16[288,128]{1,0:T(8,128)(2,1)S(1)}, u32[]{:S(2)}, u32[]{:S(2)}) collective-permute-start(bf16[288,128]{1,0:T(8,128)(2,1)S(1)} %norm.1), channel_id=1, source_target_pairs={{0,1},{1,0},{2,3},{3,2},{4,5},{5,4},{6,7},{7,6},{8,9},{9,8},{10,11... | collective-permute-start | bytes 221192 | tf_op jit(solution)/shard_map/ppermute | solution.py:454
  10.6 3.4 %collective-permute-start.4 = (bf16[1152,128]{1,0:T(8,128)(2,1)S(1)}, bf16[1152,128]{1,0:T(8,128)(2,1)S(1)}, u32[]{:S(2)}, u32[]{:S(2)}) collective-permute-start(bf16[1152,128]{1,0:T(8,128)(2,1)S(1)} %pad_maximum_fusion.x_ref.home_ref), channel_id=1, source_target_pairs={{0,4},{1,17},{2,10},{3,27},{4,0},{5,21},{6,14},{7,31},{8,16},{9,1}... | collective-permute-start | bytes 884744 | tf_op jit(solution)/shard_map/ppermute | solution.py:454
  10.7 3.0 %collective-permute-start.3 = (f32[288,128]{1,0:T(8,128)}, f32[288,128]{1,0:T(8,128)S(1)}, u32[]{:S(2)}, u32[]{:S(2)}) collective-permute-start(f32[288,128]{1,0:T(8,128)} %bitcast.6), channel_id=1, source_target_pairs={{0,4},{1,5},{2,6},{3,7},{4,0},{5,1},{6,2},{7,3},{8,10},{9,11},{10,... | collective-permute-start | bytes 442376 | tf_op jit(solution)/shard_map/ppermute | solution.py:454
  14.0 1.6 %collective-permute-start.5 = (bf16[1152,128]{1,0:T(8,128)(2,1)S(1)}, bf16[1152,128]{1,0:T(8,128)(2,1)S(1)}, u32[]{:S(2)}, u32[]{:S(2)}) collective-permute-start(bf16[1152,128]{1,0:T(8,128)(2,1)S(1)} %collective-permute-done.4.x_ref.home_ref), channel_id=1, source_target_pairs={{0,4},{1,5},{2,6},{3,7},{4,0},{5,1},{6,2},{7,3},{8,12},{9,13},{10,... | collective-permute-start | bytes 884744 | tf_op jit(solution)/shard_map/ppermute | solution.py:454
  16.9 2.2 %copy-start.1 = (bf16[128,640]{1,0:T(8,128)(2,1)S(1)}, bf16[128,640]{1,0:T(8,128)(2,1)}, u32[]{:S(2)}) copy-start(bf16[128,640]{1,0:T(8,128)(2,1)} %w_ref.13) | copy-start | bytes 491524
  19.4 1.6 %collective-permute-start.6 = (bf16[1152,128]{1,0:T(8,128)(2,1)S(1)}, bf16[1152,128]{1,0:T(8,128)(2,1)S(1)}, u32[]{:S(2)}, u32[]{:S(2)}) collective-permute-start(bf16[1152,128]{1,0:T(8,128)(2,1)S(1)} %back_other.1), channel_id=1, source_target_pairs={{0,4},{1,5},{2,6},{3,7},{4,0},{5,1},{6,2},{7,3},{8,12},{9,13},{10,... | collective-permute-start | bytes 884744 | tf_op jit(solution)/shard_map/ppermute | solution.py:454
  20.2 1.4 %collective-permute-start.9 = (bf16[384,128]{1,0:T(8,128)(2,1)S(1)}, bf16[384,128]{1,0:T(8,128)(2,1)S(1)}, u32[]{:S(2)}, u32[]{:S(2)}) collective-permute-start(bf16[384,128]{1,0:T(8,128)(2,1)S(1)} %get-tuple-element.104), channel_id=1, source_target_pairs={{0,4},{1,5},{2,6},{3,7},{4,0},{5,1},{6,2},{7,3},{8,12},{9,13},{10,... | collective-permute-start | bytes 294920 | tf_op jit(solution)/shard_map/ppermute | solution.py:454
  21.1 21.5 %collective-permute-start.7 = (bf16[1152,128]{1,0:T(8,128)(2,1)S(1)}, bf16[1152,128]{1,0:T(8,128)(2,1)S(1)}, u32[]{:S(2)}, u32[]{:S(2)}) collective-permute-start(bf16[1152,128]{1,0:T(8,128)(2,1)S(1)} %core_sum.1.y_ref), channel_id=1, source_target_pairs={{0,4},{1,9},{2,18},{3,27},{4,0},{5,13},{6,22},{7,31},{8,16},{9,25}... | collective-permute-start | bytes 884744 | tf_op jit(solution)/shard_map/ppermute | solution.py:454
  21.6 11.5 %collective-permute-start.10 = (bf16[96,128]{1,0:T(8,128)(2,1)S(1)}, bf16[96,128]{1,0:T(8,128)(2,1)S(1)}, u32[]{:S(2)}, u32[]{:S(2)}) collective-permute-start(bf16[96,128]{1,0:T(8,128)(2,1)S(1)} %get-tuple-element.107), channel_id=1, source_target_pairs={{0,1},{1,0},{2,3},{3,2},{4,5},{5,4},{6,7},{7,6},{8,9},{9,8},{10,11... | collective-permute-start | bytes 73736 | tf_op jit(solution)/shard_map/ppermute | solution.py:454
  29.5 5.4 %collective-permute-start.11 = (bf16[96,128]{1,0:T(8,128)(2,1)S(1)}, bf16[96,128]{1,0:T(8,128)(2,1)S(1)}, u32[]{:S(2)}, u32[]{:S(2)}) collective-permute-start(bf16[96,128]{1,0:T(8,128)(2,1)S(1)} %get-tuple-element.108), channel_id=1, source_target_pairs={{0,2},{1,3},{2,0},{3,1},{4,6},{5,7},{6,4},{7,5},{8,10},{9,11},{10,... | collective-permute-start | bytes 73736 | tf_op jit(solution)/shard_map/ppermute | solution.py:454
  33.1 4.7 %collective-permute-start.12 = (bf16[96,128]{1,0:T(8,128)(2,1)S(1)}, bf16[96,128]{1,0:T(8,128)(2,1)S(1)}, u32[]{:S(2)}, u32[]{:S(2)}) collective-permute-start(bf16[96,128]{1,0:T(8,128)(2,1)S(1)} %get-tuple-element.109), channel_id=1, source_target_pairs={{0,3},{1,2},{2,1},{3,0},{4,7},{5,6},{6,5},{7,4},{8,11},{9,10},{10,... | collective-permute-start | bytes 73736 | tf_op jit(solution)/shard_map/ppermute | solution.py:454
  33.1 9.6 %collective-permute-start.8 = (f32[288,128]{1,0:T(8,128)S(1)}, f32[288,128]{1,0:T(8,128)S(1)}, u32[]{:S(2)}, u32[]{:S(2)}) collective-permute-start(f32[288,128]{1,0:T(8,128)S(1)} %get-tuple-element.100.own_ref), channel_id=1, source_target_pairs={{0,4},{1,5},{2,6},{3,7},{4,0},{5,1},{6,2},{7,3},{8,10},{9,11},{10,... | collective-permute-start | bytes 442376 | tf_op jit(solution)/shard_map/ppermute | solution.py:454
  37.8 5.7 %collective-permute-start.15 = (bf16[96,128]{1,0:T(8,128)(2,1)S(1)}, bf16[96,128]{1,0:T(8,128)(2,1)S(1)}, u32[]{:S(2)}, u32[]{:S(2)}) collective-permute-start(bf16[96,128]{1,0:T(8,128)(2,1)S(1)} %fusion), channel_id=1, source_target_pairs={{0,24},{1,25},{2,26},{3,27},{4,28},{5,29},{6,30},{7,31},{8,16},{9,... | collective-permute-start | bytes 73736 | tf_op jit(solution)/shard_map/ppermute | solution.py:454
  38.6 5.0 %collective-permute-start.14 = (bf16[96,128]{1,0:T(8,128)(2,1)S(1)}, bf16[96,128]{1,0:T(8,128)(2,1)S(1)}, u32[]{:S(2)}, u32[]{:S(2)}) collective-permute-start(bf16[96,128]{1,0:T(8,128)(2,1)S(1)} %fusion), channel_id=1, source_target_pairs={{0,16},{1,17},{2,18},{3,19},{4,20},{5,21},{6,22},{7,23},{8,24},{9,... | collective-permute-start | bytes 73736 | tf_op jit(solution)/shard_map/ppermute | solution.py:454
  38.6 5.5 %collective-permute-start.13 = (bf16[96,128]{1,0:T(8,128)(2,1)S(1)}, bf16[96,128]{1,0:T(8,128)(2,1)S(1)}, u32[]{:S(2)}, u32[]{:S(2)}) collective-permute-start(bf16[96,128]{1,0:T(8,128)(2,1)S(1)} %fusion), channel_id=1, source_target_pairs={{0,8},{1,9},{2,10},{3,11},{4,12},{5,13},{6,14},{7,15},{8,0},{9,1},... | collective-permute-start | bytes 73736 | tf_op jit(solution)/shard_map/ppermute | solution.py:454
  42.6 5.1 %copy-start.3 = (f32[12,24,128]{2,1,0:T(8,128)S(1)}, f32[12,24,128]{2,1,0:T(8,128)}, u32[]{:S(2)}) copy-start(f32[12,24,128]{2,1,0:T(8,128)} %param.5) | copy-start | bytes 442372
  44.2 4.7 %collective-permute-start.16 = (bf16[384,128]{1,0:T(8,128)(2,1)S(1)}, bf16[384,128]{1,0:T(8,128)(2,1)S(1)}, u32[]{:S(2)}, u32[]{:S(2)}) collective-permute-start(bf16[384,128]{1,0:T(8,128)(2,1)S(1)} %get-tuple-element.120), channel_id=1, source_target_pairs={{0,1},{1,0},{2,3},{3,2},{4,5},{5,4},{6,7},{7,6},{8,9},{9,8},{10,11... | collective-permute-start | bytes 294920 | tf_op jit(solution)/shard_map/ppermute | solution.py:454
  44.5 4.6 %collective-permute-start.17 = (bf16[384,128]{1,0:T(8,128)(2,1)S(1)}, bf16[384,128]{1,0:T(8,128)(2,1)S(1)}, u32[]{:S(2)}, u32[]{:S(2)}) collective-permute-start(bf16[384,128]{1,0:T(8,128)(2,1)S(1)} %get-tuple-element.121), channel_id=1, source_target_pairs={{0,2},{1,3},{2,0},{3,1},{4,6},{5,7},{6,4},{7,5},{8,10},{9,11},{10,... | collective-permute-start | bytes 294920 | tf_op jit(solution)/shard_map/ppermute | solution.py:454
  44.8 5.5 %collective-permute-start.18 = (bf16[384,128]{1,0:T(8,128)(2,1)S(1)}, bf16[384,128]{1,0:T(8,128)(2,1)S(1)}, u32[]{:S(2)}, u32[]{:S(2)}) collective-permute-start(bf16[384,128]{1,0:T(8,128)(2,1)S(1)} %get-tuple-element.122), channel_id=1, source_target_pairs={{0,3},{1,2},{2,1},{3,0},{4,7},{5,6},{6,5},{7,4},{8,11},{9,10},{10,... | collective-permute-start | bytes 294920 | tf_op jit(solution)/shard_map/ppermute | solution.py:454
  50.4 1.4 %collective-permute-start.19 = (bf16[384,128]{1,0:T(8,128)(2,1)S(1)}, bf16[384,128]{1,0:T(8,128)(2,1)S(1)}, u32[]{:S(2)}, u32[]{:S(2)}) collective-permute-start(bf16[384,128]{1,0:T(8,128)(2,1)S(1)} %join.1.mine_ref), channel_id=1, source_target_pairs={{0,4},{1,5},{2,6},{3,7},{4,0},{5,1},{6,2},{7,3},{8,12},{9,13},{10,... | collective-permute-start | bytes 294920 | tf_op jit(solution)/shard_map/ppermute | solution.py:454
  (3 other events, 2.5 us)

commit v9 on v8

--- a/solution.py
+++ b/solution.py
@@ -586,7 +586,6 @@
         mine = mine + in_plane(chunks[d - 1], d).astype(F32)
     low_mine = mine.astype(BF16)
     home = to_pair(pair_out)
-    back_y, home = lax.optimization_barrier((back_y, home))
     rest, *parts = call(
         functools.partial(row_sum_kernel, cols, area),
         "row_sum",
@@ -595,7 +594,7 @@
         [gx, back_y, y],
     )
     planes_got = [across(low_mine, d) for d in range(1, cols)]
-    *planes_got, rest = lax.optimization_barrier((*planes_got, rest))
+    *planes_got, rest, home = lax.optimization_barrier((*planes_got, rest, home))
     for got in planes_got:
         mine = mine + got.astype(F32)
     low_mine = mine.astype(BF16)

time: 52.7 us -> 52.7 us (level)
  no operation moved by 1% of the time
where the time goes in v9:
time: 52.7 us; the launch traced here: 52.5 us
  starting transfers between devices  25.7 us (49%)
  waiting for transfers between devices  13.5 us (26%)
  Pallas kernels  9.84 us (19%)
  local copies, waits for them, and re-layouts  2.49 us (5%)
  between operations  0.87 us (2%)
    ppermute x20, starting transfers between devices, permute(): return lax.ppermute(value, ('row', 'col'), pairs)  25.7 us
    ppermute x20, waiting for transfers between devices, permute(): return lax.ppermute(value, ('row', 'col'), pairs)  13.5 us
    pallas_call x21, Pallas kernels, call(): pl.pallas_call(kernel, out_shape=tuple(out_shape), in_specs=specs, out_sp...  9.84 us
    unnamed x14, local copies, waits for them, and re-layouts  2.49 us
  transfers between devices with their start and end apart: 20, of which 14 were waited for; matrix products, arithmetic and copies ran while one was open for 0% of the time, Pallas kernels for 10%

profile of v9, /device:TPU:0, one launch (start us, length us, event | category | flops | bytes accessed | tf_op | source)
XLA Modules:
  0.0 52.5 jit_solution(8971584707927791626)
XLA Ops:
  0.6 0.9 %copy-done.2 = f32[12,24,128]{2,1,0:T(8,128)S(1)} copy-done((f32[12,24,128]{2,1,0:T(8,128)S(1)}, f32[12,24,128]{2,1,0:T(8,128)}, u32[]{:S(2)}) %copy-start.2) | copy-done | bytes 147480
  1.8 4.0 %collective-permute-start.2 = (bf16[288,128]{1,0:T(8,128)(2,1)S(1)}, bf16[288,128]{1,0:T(8,128)(2,1)S(1)}, u32[]{:S(2)}, u32[]{:S(2)}) collective-permute-start(bf16[288,128]{1,0:T(8,128)(2,1)S(1)} %norm.1), channel_id=1, source_target_pairs={{0,3},{1,2},{2,1},{3,0},{4,7},{5,6},{6,5},{7,4},{8,11},{9,10},{10,... | collective-permute-start | bytes 221192 | tf_op jit(solution)/shard_map/ppermute | solution.py:454
  6.4 1.7 %collective-permute-done.2 = bf16[288,128]{1,0:T(8,128)(2,1)S(1)} collective-permute-done((bf16[288,128]{1,0:T(8,128)(2,1)S(1)}, bf16[288,128]{1,0:T(8,128)(2,1)S(1)}, u32[]{:S(2)}, u32[]{:S(2)}) %collective-permute-start.2) | collective-permute-done | bytes 73760 | tf_op jit(solution)/shard_map/ppermute | solution.py:454
  8.1 2.0 %collective-permute-done.1 = bf16[288,128]{1,0:T(8,128)(2,1)S(1)} collective-permute-done((bf16[288,128]{1,0:T(8,128)(2,1)S(1)}, bf16[288,128]{1,0:T(8,128)(2,1)S(1)}, u32[]{:S(2)}, u32[]{:S(2)}) %collective-permute-start.1) | collective-permute-done | bytes 73760 | tf_op jit(solution)/shard_map/ppermute | solution.py:454
  11.2 0.7 %copy-done.6 = s32[12]{0:T(128)S(1)} copy-done((s32[12]{0:T(128)S(1)}, s32[12]{0:T(128)}, u32[]{:S(2)}) %copy-start.6) | copy-done | bytes 72
  11.8 0.5 %mask.1.mask_ref = f32[96,128]{1,0:T(8,128)S(1)} custom-call(s32[12]{0:T(128)S(1)} %copy-done.6), custom_call_target="tpu_custom_call" | custom-call | bytes 369000 | tf_op jit(solution)/shard_map/mask/pallas_call | solution.py:416
  12.4 0.9 %copy-done = bf16[128,640]{1,0:T(8,128)(2,1)S(1)} copy-done((bf16[128,640]{1,0:T(8,128)(2,1)S(1)}, bf16[128,640]{1,0:T(8,128)(2,1)}, u32[]{:S(2)}) %copy-start) | copy-done | bytes 163864
  15.1 0.6 %collective-permute-done.5.x_ref = bf16[1152,128]{1,0:T(8,128)(2,1)S(1)} collective-permute-done((bf16[1152,128]{1,0:T(8,128)(2,1)S(1)}, bf16[1152,128]{1,0:T(8,128)(2,1)S(1)}, u32[]{:S(2)}, u32[]{:S(2)}) %collective-permute-start.5) | collective-permute-done | bytes 294944 | tf_op jit(solution)/shard_map/ppermute | solution.py:454
  16.0 0.9 %mix.1 = (bf16[288,128]{1,0:T(8,128)(2,1)S(1)}, f32[12,24,8,128]{3,2,1,0:T(8,128)S(1)}) custom-call(f32[4,12,24,128]{3,2,1,0:T(8,128)S(1)} %get-tuple-element.78.lv_ref, f32[4,12,24,128]{3,2,1,0:T(8,128)S(1)} %get-tuple-element.86.rv_ref, f32[12,16,128]{2,1,0:T(8,128)S(1)} %mix_own.1.own_ref, f32[288,128]{1,0:T(8,128)S(1)} %get-tuple-element.90.back_ref), custom_call_target="tpu_custom_call" | custom-call | bytes 4428000 | tf_op jit(solution)/shard_map/mix/pallas_call | solution.py:416
  16.9 2.2 %grads.1 = (bf16[1152,256]{1,0:T(8,128)(2,1)S(1)}, bf16[1152,256]{1,0:T(8,128)(2,1)S(1)}, bf16[1152,256]{1,0:T(8,128)(2,1)S(1)}) custom-call(f32[4,12,24,128]{3,2,1,0:T(8,128)S(1)} %get-tuple-element.78.lv_ref, f32[4,12,24,128]{3,2,1,0:T(8,128)S(1)} %get-tuple-element.82.la_ref, f32[4,12,24,128]{3,2,1,0:T(8,128)S(1)} %get-tuple-element.83.lb_ref, ...), custom_call_target="tpu_custom_call" | custom-call | bytes 9225000 | tf_op jit(solution)/shard_map/grads/pallas_call | solution.py:416
  19.6 0.5 %weight_sums.1 = (bf16[384,128]{1,0:T(8,128)(2,1)S(1)}, f32[384,128]{1,0:T(8,128)S(1)}, f32[288,128]{1,0:T(8,128)S(1)}, bf16[288,128]{1,0:T(8,128)(2,1)S(1)}) custom-call(bf16[1152,128]{1,0:T(8,128)(2,1)S(1)} %pad_maximum_fusion.x_ref.home_ref, bf16[128,1152]{1,0:T(8,128)(2,1)S(1)} %get-tuple-element.70.x_turned_ref, ...), custom_call_target="tpu_custom_call" | custom-call | bytes 2214000 | tf_op jit(solution)/shard_map/weight_sums/pallas_call | solution.py:416
  21.6 7.9 %collective-permute-start.7 = (bf16[96,128]{1,0:T(8,128)(2,1)S(1)}, bf16[96,128]{1,0:T(8,128)(2,1)S(1)}, u32[]{:S(2)}, u32[]{:S(2)}) collective-permute-start(bf16[96,128]{1,0:T(8,128)(2,1)S(1)} %get-tuple-element.104), channel_id=1, source_target_pairs={{0,1},{1,0},{2,3},{3,2},{4,5},{5,4},{6,7},{7,6},{8,9},{9,8},{10,11... | collective-permute-start | bytes 73736 | tf_op jit(solution)/shard_map/ppermute | solution.py:454
  29.5 3.6 %collective-permute-start.8 = (bf16[96,128]{1,0:T(8,128)(2,1)S(1)}, bf16[96,128]{1,0:T(8,128)(2,1)S(1)}, u32[]{:S(2)}, u32[]{:S(2)}) collective-permute-start(bf16[96,128]{1,0:T(8,128)(2,1)S(1)} %get-tuple-element.105), channel_id=1, source_target_pairs={{0,2},{1,3},{2,0},{3,1},{4,6},{5,7},{6,4},{7,5},{8,10},{9,11},{10,... | collective-permute-start | bytes 73736 | tf_op jit(solution)/shard_map/ppermute | solution.py:454
  33.1 1.8 %collective-permute-done.8 = bf16[96,128]{1,0:T(8,128)(2,1)S(1)} collective-permute-done((bf16[96,128]{1,0:T(8,128)(2,1)S(1)}, bf16[96,128]{1,0:T(8,128)(2,1)S(1)}, u32[]{:S(2)}, u32[]{:S(2)}) %collective-permute-start.8) | collective-permute-done | bytes 24608 | tf_op jit(solution)/shard_map/ppermute | solution.py:454
  34.9 2.9 %collective-permute-done.9 = bf16[96,128]{1,0:T(8,128)(2,1)S(1)} collective-permute-done((bf16[96,128]{1,0:T(8,128)(2,1)S(1)}, bf16[96,128]{1,0:T(8,128)(2,1)S(1)}, u32[]{:S(2)}, u32[]{:S(2)}) %collective-permute-start.9) | collective-permute-done | bytes 24608 | tf_op jit(solution)/shard_map/ppermute | solution.py:454
  37.8 0.7 %collective-permute-start.12 = (bf16[96,128]{1,0:T(8,128)(2,1)S(1)}, bf16[96,128]{1,0:T(8,128)(2,1)S(1)}, u32[]{:S(2)}, u32[]{:S(2)}) collective-permute-start(bf16[96,128]{1,0:T(8,128)(2,1)S(1)} %fusion), channel_id=1, source_target_pairs={{0,24},{1,25},{2,26},{3,27},{4,28},{5,29},{6,30},{7,31},{8,16},{9,... | collective-permute-start | bytes 73736 | tf_op jit(solution)/shard_map/ppermute | solution.py:454
  38.6 3.7 %collective-permute-start.10 = (bf16[96,128]{1,0:T(8,128)(2,1)S(1)}, bf16[96,128]{1,0:T(8,128)(2,1)S(1)}, u32[]{:S(2)}, u32[]{:S(2)}) collective-permute-start(bf16[96,128]{1,0:T(8,128)(2,1)S(1)} %fusion), channel_id=1, source_target_pairs={{0,8},{1,9},{2,10},{3,11},{4,12},{5,13},{6,14},{7,15},{8,0},{9,1},... | collective-permute-start | bytes 73736 | tf_op jit(solution)/shard_map/ppermute | solution.py:454
  42.8 0.8 %collective-permute-done.12 = bf16[96,128]{1,0:T(8,128)(2,1)S(1)} collective-permute-done((bf16[96,128]{1,0:T(8,128)(2,1)S(1)}, bf16[96,128]{1,0:T(8,128)(2,1)S(1)}, u32[]{:S(2)}, u32[]{:S(2)}) %collective-permute-start.12) | collective-permute-done | bytes 24608 | tf_op jit(solution)/shard_map/ppermute | solution.py:454
  43.6 0.5 %collective-permute-done.10 = bf16[96,128]{1,0:T(8,128)(2,1)S(1)} collective-permute-done((bf16[96,128]{1,0:T(8,128)(2,1)S(1)}, bf16[96,128]{1,0:T(8,128)(2,1)S(1)}, u32[]{:S(2)}, u32[]{:S(2)}) %collective-permute-start.10) | collective-permute-done | bytes 24608 | tf_op jit(solution)/shard_map/ppermute | solution.py:454
  44.8 2.9 %collective-permute-start.18 = (bf16[384,128]{1,0:T(8,128)(2,1)S(1)}, bf16[384,128]{1,0:T(8,128)(2,1)S(1)}, u32[]{:S(2)}, u32[]{:S(2)}) collective-permute-start(bf16[384,128]{1,0:T(8,128)(2,1)S(1)} %get-tuple-element.120), channel_id=1, source_target_pairs={{0,3},{1,2},{2,1},{3,0},{4,7},{5,6},{6,5},{7,4},{8,11},{9,10},{10,... | collective-permute-start | bytes 294920 | tf_op jit(solution)/shard_map/ppermute | solution.py:454
  47.7 0.8 %home.1 = (f32[288,128]{1,0:T(8,128)}, f32[288,128]{1,0:T(8,128)S(1)}, f32[288,128]{1,0:T(8,128)S(1)}) custom-call(f32[288,128]{1,0:T(8,128)S(1)} %get-tuple-element.99.own_ref, f32[288,128]{1,0:T(8,128)S(1)} %collective-permute-done.15.got_ref, f32[288,128]{1,0:T(8,128)S(1)} %bitcast.5), custom_call_target="tpu_custom_call" | custom-call | bytes 2214000 | tf_op jit(solution)/shard_map/home/pallas_call | solution.py:416
  49.2 1.2 %collective-permute-done.18.rest_2_ = bf16[384,128]{1,0:T(8,128)(2,1)S(1)} collective-permute-done((bf16[384,128]{1,0:T(8,128)(2,1)S(1)}, bf16[384,128]{1,0:T(8,128)(2,1)S(1)}, u32[]{:S(2)}, u32[]{:S(2)}) %collective-permute-start.18) | collective-permute-done | bytes 98336 | tf_op jit(solution)/shard_map/ppermute | solution.py:454
  50.4 0.8 %pair_grad.1 = f32[288,128]{1,0:T(8,128)} custom-call(f32[288,128]{1,0:T(8,128)S(1)} %get-tuple-element.126.own_ref, f32[288,128]{1,0:T(8,128)S(1)} %get-tuple-element.127.normed_ref, f32[288,128]{1,0:T(8,128)S(1)} %get-tuple-element.128.scaled_ref, bf16[384,128]{1,0:T(8,128)(2,1)S(1)} %collective-permute-done.16.rest_0_, ...), custom_call_target="tpu_custom_call" | custom-call | bytes 3690000 | tf_op jit(solution)/shard_map/pair_grad/pallas_call | solution.py:416
  51.7 0.8 %weights.1 = (f32[128,640]{1,0:T(8,128)}, f32[128,128]{1,0:T(8,128)}) custom-call(bf16[384,128]{1,0:T(8,128)(2,1)S(1)} %join.1.mine_ref, bf16[384,128]{1,0:T(8,128)(2,1)S(1)} %collective-permute-done.19.other_ref), custom_call_target="tpu_custom_call" | custom-call | bytes 2952000 | tf_op jit(solution)/shard_map/weights/pallas_call | solution.py:416
  (54 shorter events, 8.3 us)
Async XLA Ops:
  1.5 12.1 %copy-start.4 = (f32[12,24,128]{2,1,0:T(8,128)S(1)}, f32[12,24,128]{2,1,0:T(8,128)}, u32[]{:S(2)}) copy-start(f32[12,24,128]{2,1,0:T(8,128)} %param.9) | copy-start | bytes 442372
  1.5 12.1 %copy-start.5 = (bf16[128,128]{1,0:T(8,128)(2,1)S(1)}, bf16[128,128]{1,0:T(8,128)(2,1)}, u32[]{:S(2)}) copy-start(bf16[128,128]{1,0:T(8,128)(2,1)} %wout_ref.3) | copy-start | bytes 98308
  1.8 6.3 %collective-permute-start.2 = (bf16[288,128]{1,0:T(8,128)(2,1)S(1)}, bf16[288,128]{1,0:T(8,128)(2,1)S(1)}, u32[]{:S(2)}, u32[]{:S(2)}) collective-permute-start(bf16[288,128]{1,0:T(8,128)(2,1)S(1)} %norm.1), channel_id=1, source_target_pairs={{0,3},{1,2},{2,1},{3,0},{4,7},{5,6},{6,5},{7,4},{8,11},{9,10},{10,... | collective-permute-start | bytes 221192 | tf_op jit(solution)/shard_map/ppermute | solution.py:454
  5.7 4.4 %collective-permute-start.1 = (bf16[288,128]{1,0:T(8,128)(2,1)S(1)}, bf16[288,128]{1,0:T(8,128)(2,1)S(1)}, u32[]{:S(2)}, u32[]{:S(2)}) collective-permute-start(bf16[288,128]{1,0:T(8,128)(2,1)S(1)} %norm.1), channel_id=1, source_target_pairs={{0,2},{1,3},{2,0},{3,1},{4,6},{5,7},{6,4},{7,5},{8,10},{9,11},{10,... | collective-permute-start | bytes 221192 | tf_op jit(solution)/shard_map/ppermute | solution.py:454
  6.2 4.4 %collective-permute-start = (bf16[288,128]{1,0:T(8,128)(2,1)S(1)}, bf16[288,128]{1,0:T(8,128)(2,1)S(1)}, u32[]{:S(2)}, u32[]{:S(2)}) collective-permute-start(bf16[288,128]{1,0:T(8,128)(2,1)S(1)} %norm.1), channel_id=1, source_target_pairs={{0,1},{1,0},{2,3},{3,2},{4,5},{5,4},{6,7},{7,6},{8,9},{9,8},{10,11... | collective-permute-start | bytes 221192 | tf_op jit(solution)/shard_map/ppermute | solution.py:454
  10.6 3.4 %collective-permute-start.4 = (bf16[1152,128]{1,0:T(8,128)(2,1)S(1)}, bf16[1152,128]{1,0:T(8,128)(2,1)S(1)}, u32[]{:S(2)}, u32[]{:S(2)}) collective-permute-start(bf16[1152,128]{1,0:T(8,128)(2,1)S(1)} %pad_maximum_fusion.x_ref.home_ref), channel_id=1, source_target_pairs={{0,4},{1,17},{2,10},{3,27},{4,0},{5,21},{6,14},{7,31},{8,16},{9,1}... | collective-permute-start | bytes 884744 | tf_op jit(solution)/shard_map/ppermute | solution.py:454
  10.7 3.0 %collective-permute-start.3 = (f32[288,128]{1,0:T(8,128)}, f32[288,128]{1,0:T(8,128)S(1)}, u32[]{:S(2)}, u32[]{:S(2)}) collective-permute-start(f32[288,128]{1,0:T(8,128)} %bitcast.6), channel_id=1, source_target_pairs={{0,4},{1,5},{2,6},{3,7},{4,0},{5,1},{6,2},{7,3},{8,10},{9,11},{10,... | collective-permute-start | bytes 442376 | tf_op jit(solution)/shard_map/ppermute | solution.py:454
  14.0 1.6 %collective-permute-start.5 = (bf16[1152,128]{1,0:T(8,128)(2,1)S(1)}, bf16[1152,128]{1,0:T(8,128)(2,1)S(1)}, u32[]{:S(2)}, u32[]{:S(2)}) collective-permute-start(bf16[1152,128]{1,0:T(8,128)(2,1)S(1)} %collective-permute-done.4.x_ref.home_ref), channel_id=1, source_target_pairs={{0,4},{1,5},{2,6},{3,7},{4,0},{5,1},{6,2},{7,3},{8,12},{9,13},{10,... | collective-permute-start | bytes 884744 | tf_op jit(solution)/shard_map/ppermute | solution.py:454
  16.9 2.2 %copy-start.1 = (bf16[128,640]{1,0:T(8,128)(2,1)S(1)}, bf16[128,640]{1,0:T(8,128)(2,1)}, u32[]{:S(2)}) copy-start(bf16[128,640]{1,0:T(8,128)(2,1)} %w_ref.13) | copy-start | bytes 491524
  19.4 1.6 %collective-permute-start.13 = (bf16[1152,128]{1,0:T(8,128)(2,1)S(1)}, bf16[1152,128]{1,0:T(8,128)(2,1)S(1)}, u32[]{:S(2)}, u32[]{:S(2)}) collective-permute-start(bf16[1152,128]{1,0:T(8,128)(2,1)S(1)} %back_other.1), channel_id=1, source_target_pairs={{0,4},{1,5},{2,6},{3,7},{4,0},{5,1},{6,2},{7,3},{8,12},{9,13},{10,... | collective-permute-start | bytes 884744 | tf_op jit(solution)/shard_map/ppermute | solution.py:454
  20.2 1.4 %collective-permute-start.6 = (bf16[384,128]{1,0:T(8,128)(2,1)S(1)}, bf16[384,128]{1,0:T(8,128)(2,1)S(1)}, u32[]{:S(2)}, u32[]{:S(2)}) collective-permute-start(bf16[384,128]{1,0:T(8,128)(2,1)S(1)} %get-tuple-element.101), channel_id=1, source_target_pairs={{0,4},{1,5},{2,6},{3,7},{4,0},{5,1},{6,2},{7,3},{8,12},{9,13},{10,... | collective-permute-start | bytes 294920 | tf_op jit(solution)/shard_map/ppermute | solution.py:454
  21.1 21.5 %collective-permute-start.14 = (bf16[1152,128]{1,0:T(8,128)(2,1)S(1)}, bf16[1152,128]{1,0:T(8,128)(2,1)S(1)}, u32[]{:S(2)}, u32[]{:S(2)}) collective-permute-start(bf16[1152,128]{1,0:T(8,128)(2,1)S(1)} %core_sum.1.y_ref), channel_id=1, source_target_pairs={{0,4},{1,9},{2,18},{3,27},{4,0},{5,13},{6,22},{7,31},{8,16},{9,25}... | collective-permute-start | bytes 884744 | tf_op jit(solution)/shard_map/ppermute | solution.py:454
  21.6 11.5 %collective-permute-start.7 = (bf16[96,128]{1,0:T(8,128)(2,1)S(1)}, bf16[96,128]{1,0:T(8,128)(2,1)S(1)}, u32[]{:S(2)}, u32[]{:S(2)}) collective-permute-start(bf16[96,128]{1,0:T(8,128)(2,1)S(1)} %get-tuple-element.104), channel_id=1, source_target_pairs={{0,1},{1,0},{2,3},{3,2},{4,5},{5,4},{6,7},{7,6},{8,9},{9,8},{10,11... | collective-permute-start | bytes 73736 | tf_op jit(solution)/shard_map/ppermute | solution.py:454
  29.5 5.4 %collective-permute-start.8 = (bf16[96,128]{1,0:T(8,128)(2,1)S(1)}, bf16[96,128]{1,0:T(8,128)(2,1)S(1)}, u32[]{:S(2)}, u32[]{:S(2)}) collective-permute-start(bf16[96,128]{1,0:T(8,128)(2,1)S(1)} %get-tuple-element.105), channel_id=1, source_target_pairs={{0,2},{1,3},{2,0},{3,1},{4,6},{5,7},{6,4},{7,5},{8,10},{9,11},{10,... | collective-permute-start | bytes 73736 | tf_op jit(solution)/shard_map/ppermute | solution.py:454
  33.1 4.7 %collective-permute-start.9 = (bf16[96,128]{1,0:T(8,128)(2,1)S(1)}, bf16[96,128]{1,0:T(8,128)(2,1)S(1)}, u32[]{:S(2)}, u32[]{:S(2)}) collective-permute-start(bf16[96,128]{1,0:T(8,128)(2,1)S(1)} %get-tuple-element.106), channel_id=1, source_target_pairs={{0,3},{1,2},{2,1},{3,0},{4,7},{5,6},{6,5},{7,4},{8,11},{9,10},{10,... | collective-permute-start | bytes 73736 | tf_op jit(solution)/shard_map/ppermute | solution.py:454
  33.1 11.0 %collective-permute-start.15 = (f32[288,128]{1,0:T(8,128)S(1)}, f32[288,128]{1,0:T(8,128)S(1)}, u32[]{:S(2)}, u32[]{:S(2)}) collective-permute-start(f32[288,128]{1,0:T(8,128)S(1)} %get-tuple-element.99.own_ref), channel_id=1, source_target_pairs={{0,4},{1,5},{2,6},{3,7},{4,0},{5,1},{6,2},{7,3},{8,10},{9,11},{10,... | collective-permute-start | bytes 442376 | tf_op jit(solution)/shard_map/ppermute | solution.py:454
  37.8 5.7 %collective-permute-start.12 = (bf16[96,128]{1,0:T(8,128)(2,1)S(1)}, bf16[96,128]{1,0:T(8,128)(2,1)S(1)}, u32[]{:S(2)}, u32[]{:S(2)}) collective-permute-start(bf16[96,128]{1,0:T(8,128)(2,1)S(1)} %fusion), channel_id=1, source_target_pairs={{0,24},{1,25},{2,26},{3,27},{4,28},{5,29},{6,30},{7,31},{8,16},{9,... | collective-permute-start | bytes 73736 | tf_op jit(solution)/shard_map/ppermute | solution.py:454
  38.6 5.0 %collective-permute-start.11 = (bf16[96,128]{1,0:T(8,128)(2,1)S(1)}, bf16[96,128]{1,0:T(8,128)(2,1)S(1)}, u32[]{:S(2)}, u32[]{:S(2)}) collective-permute-start(bf16[96,128]{1,0:T(8,128)(2,1)S(1)} %fusion), channel_id=1, source_target_pairs={{0,16},{1,17},{2,18},{3,19},{4,20},{5,21},{6,22},{7,23},{8,24},{9,... | collective-permute-start | bytes 73736 | tf_op jit(solution)/shard_map/ppermute | solution.py:454
  38.6 5.5 %collective-permute-start.10 = (bf16[96,128]{1,0:T(8,128)(2,1)S(1)}, bf16[96,128]{1,0:T(8,128)(2,1)S(1)}, u32[]{:S(2)}, u32[]{:S(2)}) collective-permute-start(bf16[96,128]{1,0:T(8,128)(2,1)S(1)} %fusion), channel_id=1, source_target_pairs={{0,8},{1,9},{2,10},{3,11},{4,12},{5,13},{6,14},{7,15},{8,0},{9,1},... | collective-permute-start | bytes 73736 | tf_op jit(solution)/shard_map/ppermute | solution.py:454
  42.6 5.1 %copy-start.3 = (f32[12,24,128]{2,1,0:T(8,128)S(1)}, f32[12,24,128]{2,1,0:T(8,128)}, u32[]{:S(2)}) copy-start(f32[12,24,128]{2,1,0:T(8,128)} %param.5) | copy-start | bytes 442372
  44.2 4.7 %collective-permute-start.16 = (bf16[384,128]{1,0:T(8,128)(2,1)S(1)}, bf16[384,128]{1,0:T(8,128)(2,1)S(1)}, u32[]{:S(2)}, u32[]{:S(2)}) collective-permute-start(bf16[384,128]{1,0:T(8,128)(2,1)S(1)} %get-tuple-element.118), channel_id=1, source_target_pairs={{0,1},{1,0},{2,3},{3,2},{4,5},{5,4},{6,7},{7,6},{8,9},{9,8},{10,11... | collective-permute-start | bytes 294920 | tf_op jit(solution)/shard_map/ppermute | solution.py:454
  44.5 4.6 %collective-permute-start.17 = (bf16[384,128]{1,0:T(8,128)(2,1)S(1)}, bf16[384,128]{1,0:T(8,128)(2,1)S(1)}, u32[]{:S(2)}, u32[]{:S(2)}) collective-permute-start(bf16[384,128]{1,0:T(8,128)(2,1)S(1)} %get-tuple-element.119), channel_id=1, source_target_pairs={{0,2},{1,3},{2,0},{3,1},{4,6},{5,7},{6,4},{7,5},{8,10},{9,11},{10,... | collective-permute-start | bytes 294920 | tf_op jit(solution)/shard_map/ppermute | solution.py:454
  44.8 5.5 %collective-permute-start.18 = (bf16[384,128]{1,0:T(8,128)(2,1)S(1)}, bf16[384,128]{1,0:T(8,128)(2,1)S(1)}, u32[]{:S(2)}, u32[]{:S(2)}) collective-permute-start(bf16[384,128]{1,0:T(8,128)(2,1)S(1)} %get-tuple-element.120), channel_id=1, source_target_pairs={{0,3},{1,2},{2,1},{3,0},{4,7},{5,6},{6,5},{7,4},{8,11},{9,10},{10,... | collective-permute-start | bytes 294920 | tf_op jit(solution)/shard_map/ppermute | solution.py:454
  50.4 1.4 %collective-permute-start.19 = (bf16[384,128]{1,0:T(8,128)(2,1)S(1)}, bf16[384,128]{1,0:T(8,128)(2,1)S(1)}, u32[]{:S(2)}, u32[]{:S(2)}) collective-permute-start(bf16[384,128]{1,0:T(8,128)(2,1)S(1)} %join.1.mine_ref), channel_id=1, source_target_pairs={{0,4},{1,5},{2,6},{3,7},{4,0},{5,1},{6,2},{7,3},{8,12},{9,13},{10,... | collective-permute-start | bytes 294920 | tf_op jit(solution)/shard_map/ppermute | solution.py:454
  (3 other events, 2.5 us)
